TPU v7x, 32 devices: a whole 2x2x4 slice. The times are simulated.
32 devices in a mesh: grp: 4 (over y, x), seq: 8 (over z, core).
Axes of the slice: x: 2, y: 2, z: 4, core: 2. Of those that a mesh axis runs over, the one named last changes fastest.
Arguments:
- tokens: bfloat16 [2, 4, 512, 2048], P(None, 'grp', 'seq'), may hold values from -6 to 6
- cotangent: bfloat16 [2, 4, 512, 2048], P(None, 'grp', 'seq'), may hold values from -6 to 6
- lengths: int32 [2, 4], P(None, 'grp'), may hold values from 64 to 512, as said below
- decay_rate: float32 [16], replicated, may hold values from 0 to 1, as said below
- w_query: bfloat16 [2048, 2048], P('seq', 'grp'), may hold values from -0.125 to 0.125
- w_key: bfloat16 [2048, 2048], P('seq', 'grp'), may hold values from -0.125 to 0.125
- w_value: bfloat16 [2048, 2048], P('seq', 'grp'), may hold values from -0.125 to 0.125
- w_gate: bfloat16 [2048, 2048], P('seq', 'grp'), may hold values from -0.125 to 0.125
- w_out: bfloat16 [2048, 2048], P('seq', 'grp'), may hold values from -0.125 to 0.125
- w_first: bfloat16 [2048, 5632], P('seq', 'grp'), may hold values from -0.125 to 0.125
- w_second: bfloat16 [2048, 5632], P('seq', 'grp'), may hold values from -0.125 to 0.125
- w_third: bfloat16 [5632, 2048], P('seq', 'grp'), may hold values from -0.078125 to 0.078125
Outputs:
- layer_out: bfloat16 [2, 4, 512, 2048], P(None, 'grp', 'seq')
- grad_tokens: float32 [2, 4, 512, 2048], P(None, 'grp', 'seq')
- grad_query: float32 [2048, 2048], P('seq', 'grp')
- grad_key: float32 [2048, 2048], P('seq', 'grp')
- grad_value: float32 [2048, 2048], P('seq', 'grp')
- grad_gate: float32 [2048, 2048], P('seq', 'grp')
- grad_out: float32 [2048, 2048], P('seq', 'grp')
- grad_first: float32 [2048, 5632], P('seq', 'grp')
- grad_second: float32 [2048, 5632], P('seq', 'grp')
- grad_third: float32 [5632, 2048], P('seq', 'grp')
Inputs may be any that keep to these rules, and one draw needn't show every extreme that they name: `lengths`: every length lies between 64 and 512; some sequence fills all 512 slots and some has exactly 64. `decay_rate`: each rate is positive and under one.
All inputs are finite; a program needn't handle non-finite values.
Results may differ from a plain program's by a relative error of at most 0.012.
Values may be sent and summed in bfloat16 or wider, within the bound.
A program may use at most 640 MiB of HBM per device.

v0:
```python
import jax
import jax.numpy as jnp
from jax import lax
from jax.sharding import PartitionSpec as P

EPS = 1e-06
HIGH = lax.Precision.HIGHEST


def prefix(value, axis, join, neutral, backward):
    count, mine = (lax.axis_size(axis), lax.axis_index(axis))
    pieces = jax.tree.map(lambda part: lax.all_gather(part, axis), value)
    if backward:
        pieces = jax.tree.map(lambda part: part[::-1], pieces)
        mine = count - 1 - mine
    subtotal = jax.tree.map(
        lambda part, zero: jnp.full_like(part, 0) + jnp.asarray(zero, part.dtype), value, neutral
    )

    def step(position, subtotal):
        longer = join(subtotal, jax.tree.map(lambda part: part[position], pieces))
        return jax.tree.map(lambda new, old: jnp.where(position < mine, new, old), longer, subtotal)

    return lax.fori_loop(0, count - 1, step, subtotal)


def norm_rows(values):
    return values * lax.rsqrt(jnp.mean(values * values, axis=-1, keepdims=True) + EPS)


def norm_back(values, gradient):
    _, pull = jax.vjp(norm_rows, values)
    return pull(gradient)[0]


def silu_slope(values):
    sigma = jax.nn.sigmoid(values)
    return sigma * (1.0 + values * (1.0 - sigma))


def product(left, right):
    return jnp.dot(left, right, preferred_element_type=jnp.float32)


def product_left(left, right):
    return lax.dot_general(
        left, right, (((0,), (0,)), ((), ())), preferred_element_type=jnp.float32
    )


def product_right(left, right):
    return lax.dot_general(
        left, right, (((1,), (1,)), ((), ())), preferred_element_type=jnp.float32
    )


def combine_state(earlier, later):
    return (later[1][:, None, None] * earlier[0] + later[0], earlier[1] * later[1])


def shards(
    tokens,
    cotangent,
    lengths,
    decay_rate,
    w_query,
    w_key,
    w_value,
    w_gate,
    w_out,
    w_first,
    w_second,
    w_third,
):
    micro = tokens.shape[0]
    block_rows = tokens.shape[2]
    width = tokens.shape[3]
    heads = decay_rate.shape[0]
    head_dim = width // heads
    hidden_width = w_third.shape[0] * lax.axis_size("seq")
    places = jnp.arange(block_rows).astype(jnp.float32)
    slot_index = lax.axis_index("seq") * block_rows + jnp.arange(block_rows)
    offset = places[:, None] - places[None, :]
    weight = jnp.where(
        offset[None] >= 0, jnp.exp(-decay_rate[:, None, None] * jnp.maximum(offset, 0.0)[None]), 0.0
    )
    query_fac = jnp.exp(-decay_rate[None, :] * (places[:, None] + 1.0))[:, :, None]
    key_fac = jnp.exp(-decay_rate[None, :] * (block_rows - 1.0 - places[:, None]))[:, :, None]
    step_decay = jnp.exp(-decay_rate * block_rows)
    empty_state = jnp.zeros((heads, head_dim, head_dim), jnp.float32)
    unit_decay = jnp.ones((heads,), jnp.float32)
    partial_rows = (
        lax.all_gather(w_query, "grp", axis=1, tiled=True),
        lax.all_gather(w_key, "grp", axis=1, tiled=True),
        lax.all_gather(w_value, "grp", axis=1, tiled=True),
        lax.all_gather(w_gate, "grp", axis=1, tiled=True),
        lax.all_gather(w_out, "grp", axis=1, tiled=True),
        lax.all_gather(w_first, "grp", axis=1, tiled=True),
        lax.all_gather(w_second, "grp", axis=1, tiled=True),
        lax.all_gather(w_third, "grp", axis=1, tiled=True),
    )
    gathered = (
        lax.all_gather(partial_rows[0], "seq", axis=0, tiled=True),
        lax.all_gather(partial_rows[1], "seq", axis=0, tiled=True),
        lax.all_gather(partial_rows[2], "seq", axis=0, tiled=True),
        lax.all_gather(partial_rows[3], "seq", axis=0, tiled=True),
        lax.all_gather(partial_rows[4], "seq", axis=0, tiled=True),
        lax.all_gather(partial_rows[5], "seq", axis=0, tiled=True),
        lax.all_gather(partial_rows[6], "seq", axis=0, tiled=True),
        lax.all_gather(partial_rows[7], "seq", axis=0, tiled=True),
    )
    outputs = []
    input_grads = []
    first_norms = []
    attn_rows = []
    normed_rows = []
    branch_rows = []
    second_norms = []
    ffn_rows = []
    mixed_rows = []
    upstream_rows = []
    for batch_idx in range(micro):
        wq_full, wk_full, wv_full, wu_full, wo_full, first_full, second_full, third_full = gathered
        inputs = tokens[batch_idx, 0].astype(jnp.float32)
        live = (slot_index < lengths[batch_idx, 0]).astype(jnp.float32)[:, None]
        live_low = live.astype(jnp.bfloat16)
        first_norm = norm_rows(inputs).astype(jnp.bfloat16)
        query_pre = product(first_norm, wq_full)
        key_pre = product(first_norm, wk_full)
        value_pre = product(first_norm, wv_full)
        gate_pre = product(first_norm, wu_full)
        queries = jax.nn.silu(query_pre).astype(jnp.bfloat16).reshape(block_rows, heads, head_dim)
        key_heads = (jax.nn.silu(key_pre).astype(jnp.bfloat16) * live_low).reshape(
            block_rows, heads, head_dim
        )
        value_heads = (jax.nn.silu(value_pre).astype(jnp.bfloat16) * live_low).reshape(
            block_rows, heads, head_dim
        )
        query_wide = queries.astype(jnp.float32)
        key_wide = key_heads.astype(jnp.float32)
        value_wide = value_heads.astype(jnp.float32)
        local_state = jnp.einsum("jhd,jhe->hde", key_wide * key_fac, value_wide, precision=HIGH)
        prior_state, _ = prefix(
            (local_state, step_decay), "seq", combine_state, (empty_state, unit_decay), False
        )
        scores = (
            jnp.einsum("ihd,jhd->hij", queries, key_heads, preferred_element_type=jnp.float32)
            * weight
        )
        intra = jnp.einsum("hij,jhe->ihe", scores, value_wide, precision=HIGH)
        inter = jnp.einsum("ihd,hde->ihe", query_wide * query_fac, prior_state, precision=HIGH)
        attended = (intra + inter).reshape(block_rows, width)
        gate_act = jax.nn.silu(gate_pre)
        gated = gate_act * attended
        normed = norm_rows(gated).astype(jnp.bfloat16)
        hidden = inputs + product(normed, wo_full)
        second_norm = norm_rows(hidden).astype(jnp.bfloat16)
        first_proj = product(second_norm, first_full)
        second_proj = product(second_norm, second_full)
        mixed_in = (first_proj * second_proj).astype(jnp.bfloat16)
        result = hidden + product(mixed_in, third_full)
        outputs.append(result.astype(jnp.bfloat16))
        upstream = cotangent[batch_idx, 0].astype(jnp.float32) * live
        upstream_low = upstream.astype(jnp.bfloat16)
        grad_mixed = product_right(upstream_low, third_full)
        grad_first_proj = (grad_mixed * second_proj).astype(jnp.bfloat16)
        grad_second_proj = (grad_mixed * first_proj).astype(jnp.bfloat16)
        grad_norm_two = product_right(grad_first_proj, first_full) + product_right(
            grad_second_proj, second_full
        )
        grad_hidden = upstream + norm_back(hidden, grad_norm_two)
        grad_branch = grad_hidden.astype(jnp.bfloat16)
        grad_gated = norm_back(gated, product_right(grad_branch, wo_full))
        grad_attended = (grad_gated * gate_act).astype(jnp.bfloat16)
        grad_gate_pre = (grad_gated * attended * silu_slope(gate_pre)).astype(jnp.bfloat16)
        grad_heads = grad_attended.reshape(block_rows, heads, head_dim)
        grad_wide = grad_heads.astype(jnp.float32)
        local_grad = jnp.einsum("ihd,ihe->hde", query_wide * query_fac, grad_wide, precision=HIGH)
        later_grad, _ = prefix(
            (local_grad, step_decay), "seq", combine_state, (empty_state, unit_decay), True
        )
        grad_scores = (
            jnp.einsum("ihe,jhe->hij", grad_heads, value_heads, preferred_element_type=jnp.float32)
            * weight
        )
        grad_queries = jnp.einsum("hij,jhd->ihd", grad_scores, key_wide, precision=HIGH)
        grad_queries = (
            grad_queries
            + jnp.einsum("ihe,hde->ihd", grad_wide, prior_state, precision=HIGH) * query_fac
        )
        grad_keys = jnp.einsum("hij,ihd->jhd", grad_scores, query_wide, precision=HIGH)
        grad_keys = (
            grad_keys + jnp.einsum("hde,jhe->jhd", later_grad, value_wide, precision=HIGH) * key_fac
        )
        grad_values = jnp.einsum("hij,ihe->jhe", scores, grad_wide, precision=HIGH)
        grad_values = (
            grad_values + jnp.einsum("jhd,hde->jhe", key_wide, later_grad, precision=HIGH) * key_fac
        )
        grad_query_pre = (grad_queries.reshape(block_rows, width) * silu_slope(query_pre)).astype(
            jnp.bfloat16
        )
        grad_key_pre = (grad_keys.reshape(block_rows, width) * live * silu_slope(key_pre)).astype(
            jnp.bfloat16
        )
        grad_value_pre = (
            grad_values.reshape(block_rows, width) * live * silu_slope(value_pre)
        ).astype(jnp.bfloat16)
        grad_norm_one = product_right(grad_query_pre, wq_full) + product_right(
            grad_key_pre, wk_full
        )
        grad_norm_one = (
            grad_norm_one
            + product_right(grad_value_pre, wv_full)
            + product_right(grad_gate_pre, wu_full)
        )
        input_grads.append(grad_hidden + norm_back(inputs, grad_norm_one))
        first_norms.append(first_norm)
        attn_rows.append(
            jnp.concatenate([grad_query_pre, grad_key_pre, grad_value_pre, grad_gate_pre], axis=1)
        )
        normed_rows.append(normed)
        branch_rows.append(grad_branch)
        second_norms.append(second_norm)
        ffn_rows.append(jnp.concatenate([grad_first_proj, grad_second_proj], axis=1))
        mixed_rows.append(mixed_in)
        upstream_rows.append(upstream_low)
    first_all = jnp.concatenate(first_norms, axis=0)
    attn_all = jnp.concatenate(attn_rows, axis=0)
    normed_all = jnp.concatenate(normed_rows, axis=0)
    branch_all = jnp.concatenate(branch_rows, axis=0)
    second_all = jnp.concatenate(second_norms, axis=0)
    ffn_all = jnp.concatenate(ffn_rows, axis=0)
    mixed_all = jnp.concatenate(mixed_rows, axis=0)
    upstream_all = jnp.concatenate(upstream_rows, axis=0)
    proj_rows = lax.psum_scatter(
        product_left(first_all, attn_all), "seq", scatter_dimension=0, tiled=True
    )
    outproj_rows = lax.psum_scatter(
        product_left(normed_all, branch_all), "seq", scatter_dimension=0, tiled=True
    )
    ffn_part = lax.psum_scatter(
        product_left(second_all, ffn_all), "seq", scatter_dimension=0, tiled=True
    )
    down_rows = lax.psum_scatter(
        product_left(mixed_all, upstream_all), "seq", scatter_dimension=0, tiled=True
    )
    summed = (
        lax.psum_scatter(proj_rows[:, :width], "grp", scatter_dimension=1, tiled=True),
        lax.psum_scatter(proj_rows[:, width : 2 * width], "grp", scatter_dimension=1, tiled=True),
        lax.psum_scatter(
            proj_rows[:, 2 * width : 3 * width], "grp", scatter_dimension=1, tiled=True
        ),
        lax.psum_scatter(proj_rows[:, 3 * width :], "grp", scatter_dimension=1, tiled=True),
        lax.psum_scatter(outproj_rows, "grp", scatter_dimension=1, tiled=True),
        lax.psum_scatter(ffn_part[:, :hidden_width], "grp", scatter_dimension=1, tiled=True),
        lax.psum_scatter(ffn_part[:, hidden_width:], "grp", scatter_dimension=1, tiled=True),
        lax.psum_scatter(down_rows, "grp", scatter_dimension=1, tiled=True),
    )
    layer_out = jnp.stack(outputs)[:, None]
    grad_tokens = jnp.stack(input_grads)[:, None]
    return (
        layer_out,
        grad_tokens,
        summed[0],
        summed[1],
        summed[2],
        summed[3],
        summed[4],
        summed[5],
        summed[6],
        summed[7],
    )


def solution(mesh):
    in_specs = (
        P(None, "grp", "seq", None),
        P(None, "grp", "seq", None),
        P(None, "grp"),
        P(),
        P("seq", "grp"),
        P("seq", "grp"),
        P("seq", "grp"),
        P("seq", "grp"),
        P("seq", "grp"),
        P("seq", "grp"),
        P("seq", "grp"),
        P("seq", "grp"),
    )
    out_specs = (
        P(None, "grp", "seq", None),
        P(None, "grp", "seq", None),
        P("seq", "grp"),
        P("seq", "grp"),
        P("seq", "grp"),
        P("seq", "grp"),
        P("seq", "grp"),
        P("seq", "grp"),
        P("seq", "grp"),
        P("seq", "grp"),
    )
    return jax.shard_map(shards, mesh=mesh, in_specs=in_specs, out_specs=out_specs, check_vma=False)
```

profile of v0, /device:TPU:0, one launch (start us, length us, event | category | flops | bytes accessed | tf_op | source)
XLA Modules:
  0.0 5154.7 jit_solution(761911247679307517)
XLA Ops:
  9.4 29.6 all-gather.38.cloned.1.call-done
  39.1 28.3 all-gather.30.cloned.1.call-done
  70.9 24.9 all-gather.34.cloned.1.call-done
  103.7 75.6 %all-gather.40.cloned.1.call-done = bf16[2048,2048]{1,0:T(8,128)(2,1)} async-done(((bf16[256,2048]{1,0:T(8,128)(2,1)}), bf16[2048,2048]{1,0:T(8,128)(2,1)}) %all-gather.40.cloned.1.call-update) | async-done | bytes 8388624 | tf_op jit(solution)/shard_map/all_gather | solution.py:104
  184.3 77.1 %all-gather.32.cloned.1.call-done = bf16[2048,2048]{1,0:T(8,128)(2,1)} async-done(((bf16[256,2048]{1,0:T(8,128)(2,1)}), bf16[2048,2048]{1,0:T(8,128)(2,1)}) %all-gather.32.cloned.1.call-update) | async-done | bytes 8388624 | tf_op jit(solution)/shard_map/all_gather | solution.py:105
  269.8 5.5 fusion.208
  279.5 8.7 all-gather.26.cloned.1.call-done
  288.2 28.3 all-gather.42.cloned.1.call-done
  316.6 43.6 all-gather.50.cloned.1.call-done
  360.2 43.6 all-gather.46.cloned.1.call-done
  403.9 43.3 all-gather.54.cloned.1.call-done
  447.3 16.9 all-reduce
  466.5 64.5 %all-gather.36.cloned.1.call-done = bf16[2048,2048]{1,0:T(8,128)(2,1)} async-done(((bf16[256,2048]{1,0:T(8,128)(2,1)}), bf16[2048,2048]{1,0:T(8,128)(2,1)}) %all-gather.36.cloned.1.call-update) | async-done | bytes 8388624 | tf_op jit(solution)/shard_map/all_gather | solution.py:103
  530.9 5.1 fusion.207
  542.1 71.5 %all-gather.60.cloned.1.call-done = f32[128,128,128]{2,1,0:T(8,128)} async-done(((f32[16,128,128]{2,1,0:T(8,128)}), f32[128,128,128]{2,1,0:T(8,128)}) %all-gather.60.cloned.1.call-update) | async-done | bytes 8388624 | tf_op jit(solution)/shard_map/all_gather | solution.py:12
  613.6 10.7 while.57
  627.0 69.4 %all-gather.58.cloned.1.call-done = f32[128,128,128]{2,1,0:T(8,128)} async-done(((f32[16,128,128]{2,1,0:T(8,128)}), f32[128,128,128]{2,1,0:T(8,128)}) %all-gather.58.cloned.1.call-update) | async-done | bytes 8388624 | tf_op jit(solution)/shard_map/all_gather | solution.py:12
  696.4 11.2 while.56
  710.9 67.6 %all-gather.28.cloned.1.call-done = bf16[2048,2048]{1,0:T(8,128)(2,1)} async-done(((bf16[256,2048]{1,0:T(8,128)(2,1)}), bf16[2048,2048]{1,0:T(8,128)(2,1)}) %all-gather.28.cloned.1.call-update) | async-done | bytes 8388624 | tf_op jit(solution)/shard_map/all_gather | solution.py:106
  778.5 5.9 multiply_reduce_fusion.7
  784.6 76.0 %all-gather.44.cloned.1.call-done = bf16[2048,2048]{1,0:T(8,128)(2,1)} async-done(((bf16[256,2048]{1,0:T(8,128)(2,1)}), bf16[2048,2048]{1,0:T(8,128)(2,1)}) %all-gather.44.cloned.1.call-update) | async-done | bytes 8388624 | tf_op jit(solution)/shard_map/all_gather | solution.py:107
  860.6 5.2 multiply_reduce_fusion.6
  865.9 7.3 multiply_reduce_fusion.5
  876.1 187.2 %all-gather.52.cloned.1.call-done = bf16[2048,5632]{1,0:T(8,128)(2,1)} async-done(((bf16[256,5632]{1,0:T(8,128)(2,1)}), bf16[2048,5632]{1,0:T(8,128)(2,1)}) %all-gather.52.cloned.1.call-update) | async-done | bytes 23068688 | tf_op jit(solution)/shard_map/all_gather | solution.py:109
  1063.3 11.5 fusion.215
  1074.8 190.9 %all-gather.48.cloned.1.call-done = bf16[2048,5632]{1,0:T(8,128)(2,1)} async-done(((bf16[256,5632]{1,0:T(8,128)(2,1)}), bf16[2048,5632]{1,0:T(8,128)(2,1)}) %all-gather.48.cloned.1.call-update) | async-done | bytes 23068688 | tf_op jit(solution)/shard_map/all_gather | solution.py:108
  1265.7 11.5 fusion.214
  1277.2 190.9 %all-gather.56.cloned.1.call-done = bf16[5632,2048]{1,0:T(8,128)(2,1)} async-done(((bf16[704,2048]{1,0:T(8,128)(2,1)}), bf16[5632,2048]{1,0:T(8,128)(2,1)}) %all-gather.56.cloned.1.call-update) | async-done | bytes 23068688 | tf_op jit(solution)/shard_map/all_gather | solution.py:110
  1468.1 13.4 multiply_convert_fusion
  1481.5 11.6 fusion.218
  1493.1 12.4 multiply_reduce_fusion.1
  1505.5 10.8 fusion.210
  1516.3 10.8 fusion.209
  1527.1 13.4 multiply_convert_fusion.2
  1540.5 11.7 fusion.216
  1552.3 11.9 multiply_reduce_fusion.3
  1565.7 6.3 multiply_reduce_fusion
  1576.0 6.3 multiply_reduce_fusion.2
  1586.3 9.3 fusion.85
  1596.8 33.6 fusion.4
  1631.9 18.0 fusion.32
  1667.3 7.8 rev.12
  1675.1 63.8 %all-gather.62.cloned.1.call-done = f32[128,128,128]{2,1,0:T(8,128)} async-done(((f32[16,128,128]{2,1,0:T(8,128)}), f32[128,128,128]{2,1,0:T(8,128)}) %all-gather.62.cloned.1.call-update) | async-done | bytes 8388624 | tf_op jit(solution)/shard_map/all_gather | solution.py:12
  1738.9 8.1 rev.11
  1747.0 10.7 while.59
  1762.2 10.7 while.58
  1780.3 26.6 fusion.16
  1807.0 101.1 %reduce-scatter.22.cloned.1.call-done = f32[256,2048]{1,0:T(8,128)} async-done(((f32[2048,2048]{1,0:T(8,128)}), f32[256,2048]{1,0:T(8,128)}) %reduce-scatter.22.cloned.1.call-update) | async-done | bytes 2097168 | tf_op jit(solution)/shard_map/reduce_scatter | solution.py:238
  1908.8 1750.9 %all-reduce.4.cloned.1.call-done = f32[2048,11264]{1,0:T(8,128)} async-done(((f32[2048,11264]{1,0:T(8,128)}), f32[2048,11264]{1,0:T(8,128)}) %all-reduce.4.cloned.1.call-update) | async-done | bytes 92274704
  3659.7 10.7 fusion.202
  3671.1 434.5 %reduce-scatter.30.cloned.1.call-done = f32[704,2048]{1,0:T(8,128)} async-done(((f32[5632,2048]{1,0:T(8,128)}), f32[704,2048]{1,0:T(8,128)}) %reduce-scatter.30.cloned.1.call-update) | async-done | bytes 5767184 | tf_op jit(solution)/shard_map/reduce_scatter | solution.py:244
  4105.7 640.8 %reduce-scatter.12.cloned.1.call-done = f32[256,8192]{1,0:T(8,128)} async-done(((f32[2048,8192]{1,0:T(8,128)}), f32[256,8192]{1,0:T(8,128)}) %reduce-scatter.12.cloned.1.call-update) | async-done | bytes 8388624 | tf_op jit(solution)/shard_map/reduce_scatter | solution.py:235
  4746.5 7.3 fusion.203
  4755.2 10.4 fusion.14
  4765.6 10.3 fusion.15
  4783.0 6.2 convolution_add_fusion.2
  4789.3 6.2 convolution_add_fusion.1
  4808.2 45.0 reduce-scatter.28.cloned.1.call-done
  4853.1 69.5 %reduce-scatter.26.cloned.1.call-done = f32[256,1408]{1,0:T(8,128)} async-done(((f32[256,5632]{1,0:T(8,128)}), f32[256,1408]{1,0:T(8,128)}) %reduce-scatter.26.cloned.1.call-update) | async-done | bytes 1441808 | tf_op jit(solution)/shard_map/reduce_scatter | solution.py:255
  4922.7 69.7 %reduce-scatter.32.cloned.1.call-done = f32[704,512]{1,0:T(8,128)} async-done(((f32[704,2048]{1,0:T(8,128)}), f32[704,512]{1,0:T(8,128)}) %reduce-scatter.32.cloned.1.call-update) | async-done | bytes 1441808 | tf_op jit(solution)/shard_map/reduce_scatter | solution.py:257
  4992.3 39.0 reduce-scatter.20.cloned.1.call-done
  5031.3 38.6 reduce-scatter.18.cloned.1.call-done
  5069.9 39.0 reduce-scatter.16.cloned.1.call-done
  5109.0 38.8 reduce-scatter.14.cloned.1.call-done
  (449 shorter events, 152.1 us)
Async XLA Ops:
  7.2 31.9 all-gather.38.cloned.1.call-start
  7.9 59.5 %all-gather.30.cloned.1.call-start = ((), (), s32[]{:S(2)}) async-start(), calls=%async_computation.13 | async-start | bytes 1310720 | tf_op jit(solution)/shard_map/all_gather | solution.py:95
  8.7 87.1 %all-gather.34.cloned.1.call-start = ((), (), s32[]{:S(2)}) async-start(), calls=%async_computation.15 | async-start | bytes 1310720 | tf_op jit(solution)/shard_map/all_gather | solution.py:93
  9.4 169.9 %all-gather.40.cloned.1.call-start = ((), (), s32[]{:S(2)}) async-start(), calls=%async_computation.18 | async-start | bytes 9437184 | tf_op jit(solution)/shard_map/all_gather | solution.py:104
  39.1 222.3 %all-gather.32.cloned.1.call-start = ((), (), s32[]{:S(2)}) async-start(), calls=%async_computation.14 | async-start | bytes 9437184 | tf_op jit(solution)/shard_map/all_gather | solution.py:105
  67.4 220.7 %all-gather.26.cloned.1.call-start = ((), (), s32[]{:S(2)}) async-start(), calls=%async_computation.11 | async-start | bytes 1310720 | tf_op jit(solution)/shard_map/all_gather | solution.py:96
  68.0 248.5 %all-gather.42.cloned.1.call-start = ((), (), s32[]{:S(2)}) async-start(), calls=%async_computation.19 | async-start | bytes 1310720 | tf_op jit(solution)/shard_map/all_gather | solution.py:97
  68.8 291.4 %all-gather.50.cloned.1.call-start = ((), (), s32[]{:S(2)}) async-start(), calls=%async_computation.23 | async-start | bytes 3604480 | tf_op jit(solution)/shard_map/all_gather | solution.py:99
  69.5 334.4 %all-gather.46.cloned.1.call-start = ((), (), s32[]{:S(2)}) async-start(), calls=%async_computation.21 | async-start | bytes 3604480 | tf_op jit(solution)/shard_map/all_gather | solution.py:98
  70.2 377.0 %all-gather.54.cloned.1.call-start = ((), (), s32[]{:S(2)}) async-start(), calls=%async_computation.25 | async-start | bytes 3604480 | tf_op jit(solution)/shard_map/all_gather | solution.py:100
  70.8 460.1 %all-gather.36.cloned.1.call-start = ((), (), s32[]{:S(2)}) async-start(), calls=%async_computation.16 | async-start | bytes 9437184 | tf_op jit(solution)/shard_map/all_gather | solution.py:103
  95.8 517.8 %all-gather.60.cloned.1.call-start = ((), (), s32[]{:S(2)}) async-start(), calls=%async_computation.39 | async-start | bytes 9437184 | tf_op jit(solution)/shard_map/all_gather | solution.py:12
  101.1 83.2 %copy-start.104 = (f32[64]{0:T(128)}, f32[64]{0:T(128)S(1)}, u32[]{:S(2)}) copy-start(f32[64]{0:T(128)S(1)} %get-tuple-element.485) | copy-start | bytes 772
  101.7 82.6 %copy-start.96 = (f32[64]{0:T(128)}, f32[64]{0:T(128)S(1)}, u32[]{:S(2)}) copy-start(f32[64]{0:T(128)S(1)} %fusion.186) | copy-start | bytes 772
  101.7 82.6 %copy-start.98 = (f32[64]{0:T(128)}, f32[64]{0:T(128)S(1)}, u32[]{:S(2)}) copy-start(f32[64]{0:T(128)S(1)} %fusion.189) | copy-start | bytes 772
  102.4 437.0 %copy-start.100 = (f32[16]{0:T(128)}, f32[16]{0:T(128)S(1)}, u32[]{:S(2)}) copy-start(f32[16]{0:T(128)S(1)} %get-tuple-element.575) | copy-start | bytes 196
  102.5 174.7 %copy-start.88 = (f32[64,16]{0,1:T(8,128)}, f32[64,16]{0,1:T(8,128)S(1)}, u32[]{:S(2)}) copy-start(f32[64,16]{0,1:T(8,128)S(1)} %get-tuple-element.573) | copy-start | bytes 12292
  103.7 674.8 %copy-start.4 = (bf16[64,2048]{1,0:T(8,128)(2,1)}, bf16[64,2048]{1,0:T(8,128)(2,1)S(1)}, u32[]{:S(2)}) copy-start(bf16[64,2048]{1,0:T(8,128)(2,1)S(1)} %get-tuple-element.560) | copy-start | bytes 786436
  103.7 762.1 %copy-start.6 = (bf16[64,2048]{1,0:T(8,128)(2,1)}, bf16[64,2048]{1,0:T(8,128)(2,1)S(1)}, u32[]{:S(2)}) copy-start(bf16[64,2048]{1,0:T(8,128)(2,1)S(1)} %get-tuple-element.561) | copy-start | bytes 786436
  184.3 82.4 %copy-start.33 = (f32[64,2048]{1,0:T(8,128)}, f32[64,2048]{1,0:T(8,128)S(1)}, u32[]{:S(2)}) copy-start(f32[64,2048]{1,0:T(8,128)S(1)} %fusion.213) | copy-start | bytes 1572868
  268.9 427.6 %all-gather.58.cloned.1.call-start = ((), (), s32[]{:S(2)}) async-start(), calls=%async_computation.38 | async-start | bytes 9437184 | tf_op jit(solution)/shard_map/all_gather | solution.py:12
  276.9 170.4 %copy-start.39 = (f32[64,2048]{1,0:T(8,128)}, f32[64,2048]{1,0:T(8,128)S(1)}, u32[]{:S(2)}) copy-start(f32[64,2048]{1,0:T(8,128)S(1)} %fusion.206) | copy-start | bytes 1572868
  277.2 258.8 %copy-start.52 = (bf16[8,16,8,128]{3,2,1,0:T(8,128)(2,1)}, bf16[8,16,8,128]{3,2,1,0:T(8,128)(2,1)S(1)}, u32[]{:S(2)}) copy-start(bf16[8,16,8,128]{3,2,1,0:T(8,128)(2,1)S(1)} %get-tuple-element.568) | copy-start | bytes 786436
  277.2 261.3 %copy-start.50 = (bf16[8,16,8,128]{3,2,1,0:T(8,128)(2,1)}, bf16[8,16,8,128]{3,2,1,0:T(8,128)(2,1)S(1)}, u32[]{:S(2)}) copy-start(bf16[8,16,8,128]{3,2,1,0:T(8,128)(2,1)S(1)} %get-tuple-element.569) | copy-start | bytes 786436
  279.4 499.1 %all-gather.28.cloned.1.call-start = ((), (), s32[]{:S(2)}) async-start(), calls=%async_computation.12 | async-start | bytes 9437184 | tf_op jit(solution)/shard_map/all_gather | solution.py:106
  288.2 572.4 %all-gather.44.cloned.1.call-start = ((), (), s32[]{:S(2)}) async-start(), calls=%async_computation.20 | async-start | bytes 9437184 | tf_op jit(solution)/shard_map/all_gather | solution.py:107
  316.5 746.8 %all-gather.52.cloned.1.call-start = ((), (), s32[]{:S(2)}) async-start(), calls=%async_computation.24 | async-start | bytes 25952256 | tf_op jit(solution)/shard_map/all_gather | solution.py:109
  360.2 905.5 %all-gather.48.cloned.1.call-start = ((), (), s32[]{:S(2)}) async-start(), calls=%async_computation.22 | async-start | bytes 25952256 | tf_op jit(solution)/shard_map/all_gather | solution.py:108
  403.9 1064.2 %all-gather.56.cloned.1.call-start = ((), (), s32[]{:S(2)}) async-start(), calls=%async_computation.26 | async-start | bytes 25952256 | tf_op jit(solution)/shard_map/all_gather | solution.py:110
  447.3 1220.1 %all-gather.64.cloned.1.call-start = ((), (), s32[]{:S(2)}) async-start(), calls=%async_computation.41 | async-start | bytes 9437184 | tf_op jit(solution)/shard_map/all_gather | solution.py:12
  464.4 75.0 %copy-start.94 = (pred[64,64]{1,0:T(8,128)(4,1)}, pred[64,64]{1,0:T(8,128)(4,1)S(1)}, u32[]{:S(2)}) copy-start(pred[64,64]{1,0:T(8,128)(4,1)S(1)} %subtract_compare_fusion) | copy-start | bytes 12292
  464.5 75.0 %copy-start.90 = (f32[64,64]{1,0:T(8,128)}, f32[64,64]{1,0:T(8,128)S(1)}, u32[]{:S(2)}) copy-start(f32[64,64]{1,0:T(8,128)S(1)} %subtract_maximum_fusion) | copy-start | bytes 49156
  536.7 170.9 %copy-start.40 = (bf16[8,16,8,128]{3,2,1,0:T(8,128)(2,1)}, bf16[8,16,8,128]{3,2,1,0:T(8,128)(2,1)S(1)}, u32[]{:S(2)}) copy-start(bf16[8,16,8,128]{3,2,1,0:T(8,128)(2,1)S(1)} %fusion.152) | copy-start | bytes 786436
  539.1 74.5 %copy-start.43 = (bf16[8,16,8,128]{3,2,1,0:T(8,128)(2,1)}, bf16[8,16,8,128]{3,2,1,0:T(8,128)(2,1)S(1)}, u32[]{:S(2)}) copy-start(bf16[8,16,8,128]{3,2,1,0:T(8,128)(2,1)S(1)} %fusion.153) | copy-start | bytes 786436
  624.4 72.0 %copy-start.3 = (f32[16,128,128]{2,1,0:T(8,128)}, f32[16,128,128]{2,1,0:T(8,128)S(1)}, u32[]{:S(2)}) copy-start(f32[16,128,128]{2,1,0:T(8,128)S(1)} %get-tuple-element.387) | copy-start | bytes 3145732
  627.0 238.9 %copy-start.30 = (f32[16,8,8,128]{3,2,1,0:T(8,128)}, f32[16,8,8,128]{3,2,1,0:T(8,128)S(1)}, u32[]{:S(2)}) copy-start(f32[16,8,8,128]{3,2,1,0:T(8,128)S(1)} %fusion.36) | copy-start | bytes 1572868
  707.6 76.8 %copy-start.1 = (f32[16,128,128]{2,1,0:T(8,128)}, f32[16,128,128]{2,1,0:T(8,128)S(1)}, u32[]{:S(2)}) copy-start(f32[16,128,128]{2,1,0:T(8,128)S(1)} %get-tuple-element.386) | copy-start | bytes 3145732
  707.6 76.8 %copy-start.92 = (f32[8,16]{1,0:T(8,128)}, f32[8,16]{1,0:T(8,128)S(1)}, u32[]{:S(2)}) copy-start(f32[8,16]{1,0:T(8,128)S(1)} %get-tuple-element.919) | copy-start | bytes 1540
  710.9 149.6 %copy-start.12 = (bf16[2,1,64,2048]{3,2,1,0:T(8,128)(2,1)S(1)}, bf16[2,1,64,2048]{3,2,1,0:T(8,128)(2,1)}, u32[]{:S(2)}) copy-start(bf16[2,1,64,2048]{3,2,1,0:T(8,128)(2,1)} %param.20) | copy-start | bytes 1572868
  784.5 88.7 %copy-start.16 = (f32[64,2048]{1,0:T(8,128)}, f32[64,2048]{1,0:T(8,128)S(1)}, u32[]{:S(2)}) copy-start(f32[64,2048]{1,0:T(8,128)S(1)} %get-tuple-element.531) | copy-start | bytes 1572868
  784.6 88.6 %copy-start.60 = (bf16[64,2048]{1,0:T(8,128)(2,1)}, bf16[64,2048]{1,0:T(8,128)(2,1)S(1)}, u32[]{:S(2)}) copy-start(bf16[64,2048]{1,0:T(8,128)(2,1)S(1)} %multiply_convert_fusion.14) | copy-start | bytes 786436
  865.8 698.4 %copy-start.8 = (f32[64,2048]{1,0:T(8,128)}, f32[64,2048]{1,0:T(8,128)S(1)}, u32[]{:S(2)}) copy-start(f32[64,2048]{1,0:T(8,128)S(1)} %get-tuple-element.583) | copy-start | bytes 1572868
  875.9 688.4 %copy-start.10 = (f32[64,2048]{1,0:T(8,128)}, f32[64,2048]{1,0:T(8,128)S(1)}, u32[]{:S(2)}) copy-start(f32[64,2048]{1,0:T(8,128)S(1)} %get-tuple-element.580) | copy-start | bytes 1572868
  876.1 389.6 %copy-start.24 = (bf16[64,2048]{1,0:T(8,128)(2,1)}, bf16[64,2048]{1,0:T(8,128)(2,1)S(1)}, u32[]{:S(2)}) copy-start(bf16[64,2048]{1,0:T(8,128)(2,1)S(1)} %multiply_convert_fusion.8) | copy-start | bytes 786436
  1074.8 393.3 %copy-start.64 = (bf16[64,2048]{1,0:T(8,128)(2,1)S(1)}, bf16[64,2048]{1,0:T(8,128)(2,1)}, u32[]{:S(2)}) copy-start(bf16[64,2048]{1,0:T(8,128)(2,1)} %get-tuple-element.559) | copy-start | bytes 786436
  1575.9 163.0 %all-gather.62.cloned.1.call-start = ((), (), s32[]{:S(2)}) async-start(), calls=%async_computation.40 | async-start | bytes 9437184 | tf_op jit(solution)/shard_map/all_gather | solution.py:12
  1586.2 321.9 %reduce-scatter.22.cloned.1.call-start = ((), (), s32[]{:S(2)}) async-start(), calls=%async_computation.32 | async-start | bytes 18874368 | tf_op jit(solution)/shard_map/reduce_scatter | solution.py:238
  1595.7 2064.1 %all-reduce.4.cloned.1.call-start = ((), (), s32[]{:S(2)}) async-start(), calls=%async_computation.42 | async-start | bytes 184549376
  1630.5 2475.1 %reduce-scatter.30.cloned.1.call-start = ((), (), s32[]{:S(2)}) async-start(), calls=%async_computation.36 | async-start | bytes 51904512 | tf_op jit(solution)/shard_map/reduce_scatter | solution.py:244
  1649.9 3096.6 %reduce-scatter.12.cloned.1.call-start = ((), (), s32[]{:S(2)}) async-start(), calls=%async_computation.27 | async-start | bytes 75497472 | tf_op jit(solution)/shard_map/reduce_scatter | solution.py:235
  1778.6 28.3 copy-start.71
  1778.6 28.3 copy-start.75
  1780.3 26.6 copy-start.73
  1806.9 3001.2 %reduce-scatter.24.cloned.1.call-start = ((), (), s32[]{:S(2)}) async-start(), calls=%async_computation.33 | async-start | bytes 2621440 | tf_op jit(solution)/shard_map/reduce_scatter | solution.py:254
  1908.2 2945.0 %reduce-scatter.28.cloned.1.call-start = ((), (), s32[]{:S(2)}) async-start(), calls=%async_computation.35 | async-start | bytes 7208960 | tf_op jit(solution)/shard_map/reduce_scatter | solution.py:256
  3670.5 1252.2 %reduce-scatter.26.cloned.1.call-start = ((), (), s32[]{:S(2)}) async-start(), calls=%async_computation.34 | async-start | bytes 7208960 | tf_op jit(solution)/shard_map/reduce_scatter | solution.py:255
  3671.1 1321.2 %reduce-scatter.32.cloned.1.call-start = ((), (), s32[]{:S(2)}) async-start(), calls=%async_computation.37 | async-start | bytes 7208960 | tf_op jit(solution)/shard_map/reduce_scatter | solution.py:257
  4105.6 649.6 %copy-start.11 = (f32[64,2048]{1,0:T(8,128)S(1)}, f32[64,2048]{1,0:T(8,128)}, u32[]{:S(2)}) copy-start(f32[64,2048]{1,0:T(8,128)} %copy-done.10) | copy-start | bytes 1572868
  4105.6 649.6 %copy-start.21 = (bf16[64,5632]{1,0:T(8,128)(2,1)S(1)}, bf16[64,5632]{1,0:T(8,128)(2,1)}, u32[]{:S(2)}) copy-start(bf16[64,5632]{1,0:T(8,128)(2,1)} %get-tuple-element.552) | copy-start | bytes 2162692
  4105.6 925.7 %reduce-scatter.20.cloned.1.call-start = ((), (), s32[]{:S(2)}) async-start(), calls=%async_computation.31 | async-start | bytes 2621440 | tf_op jit(solution)/shard_map/reduce_scatter | solution.py:253
  4753.8 316.1 %reduce-scatter.18.cloned.1.call-start = ((), (), s32[]{:S(2)}) async-start(), calls=%async_computation.30 | async-start | bytes 2621440 | tf_op jit(solution)/shard_map/reduce_scatter | solution.py:250
  4754.4 354.6 %reduce-scatter.16.cloned.1.call-start = ((), (), s32[]{:S(2)}) async-start(), calls=%async_computation.29 | async-start | bytes 2621440 | tf_op jit(solution)/shard_map/reduce_scatter | solution.py:249
  4755.2 392.6 %reduce-scatter.14.cloned.1.call-start = ((), (), s32[]{:S(2)}) async-start(), calls=%async_computation.28 | async-start | bytes 2621440 | tf_op jit(solution)/shard_map/reduce_scatter | solution.py:248
  4755.2 21.6 slice-start.8
  (86 other events, 607.8 us)
Sparse Core Ops, SparseCore 0:
  9.8 29.1 all-gather.37
  40.9 26.4 all-gather.29
  69.2 26.4 all-gather.33
  97.2 82.0 all-gather.39
  180.8 80.5 all-gather.31
  263.1 25.0 all-gather.25
  290.0 26.4 all-gather.41
  318.3 41.8 all-gather.49
  362.0 41.7 all-gather.45
  405.5 41.6 all-gather.53
  448.8 82.0 all-gather.35
  533.0 80.6 all-gather.59
  615.8 80.5 all-gather.57
  697.9 80.5 all-gather.27
  780.0 80.5 all-gather.43
  862.1 201.1 all-gather.51
  1064.8 200.8 all-gather.47
  1267.2 200.8 all-gather.55
  1576.0 80.2 all-gather.63
  1658.3 80.5 all-gather.61
  1741.3 166.7 reduce-scatter.21
  1910.7 1749.0 all-reduce.3
  3662.1 443.4 reduce-scatter.29
  4107.9 638.4 reduce-scatter.11
  4750.0 33.5 reduce-scatter.23
  4787.3 65.8 reduce-scatter.27
  4856.8 65.7 reduce-scatter.25
  4926.5 65.7 reduce-scatter.31
  4996.1 35.1 reduce-scatter.19
  5034.7 35.1 reduce-scatter.17
  5073.7 35.1 reduce-scatter.15
  5112.5 35.1 reduce-scatter.13
where the time goes:
time: 5160 us; the launch traced here: 5150 us
  waiting for transfers between devices  4660 us (90%)
  matrix products  354 us (7%)
  other arithmetic  60.7 us (1%)
    unnamed x33, waiting for transfers between devices  1760 us
    reduce_scatter x1, waiting for transfers between devices, shards(): lax.psum_scatter(product_left(first_all, attn_all), 'seq', scatter_dimens...  641 us
    reduce_scatter x1, waiting for transfers between devices, shards(): lax.psum_scatter(product_left(mixed_all, upstream_all), 'seq', scatter_di...  434 us
    all_gather x4, waiting for transfers between devices, prefix(): pieces = jax.tree.map(lambda part: lax.all_gather(part, axis), value)  205 us
    all_gather x1, waiting for transfers between devices, shards(): lax.all_gather(partial_rows[7], 'seq', axis=0, tiled=True)  191 us
    all_gather x1, waiting for transfers between devices, shards(): lax.all_gather(partial_rows[5], 'seq', axis=0, tiled=True)  191 us
    all_gather x1, waiting for transfers between devices, shards(): lax.all_gather(partial_rows[6], 'seq', axis=0, tiled=True)  187 us
    dot_general x16, matrix products, product_right(): lax.dot_general(left, right, (((1,), (1,)), ((), ())), preferred_element_...  117 us
  transfers between devices with their start and end apart: 32, of which 30 were waited for; matrix products, arithmetic and copies ran while one was open for 7% of the time, Pallas kernels for 0%

commit v1 on v0

--- a/solution.py
+++ b/solution.py
@@ -1,10 +1,15 @@
 import jax
 import jax.numpy as jnp
 from jax import lax
+from jax.experimental import pallas as pl
+from jax.experimental.pallas import tpu as pltpu
 from jax.sharding import PartitionSpec as P
 
 EPS = 1e-06
 HIGH = lax.Precision.HIGHEST
+MESH = pl.DeviceIdType.MESH
+ANY = pl.BlockSpec(memory_space=pl.ANY)
+VMEM = pl.BlockSpec(memory_space=pltpu.VMEM)
 
 
 def prefix(value, axis, join, neutral, backward):
@@ -272,6 +277,735 @@
     )
 
 
+class Copies:
+    def __init__(self, sems):
+        self.sems = sems
+        self.used = 0
+        self.pending = []
+
+    def remote(self, src, dst, recv_sem, group, place, when=None):
+        copy = pltpu.make_async_remote_copy(
+            src_ref=src,
+            dst_ref=dst,
+            send_sem=self.sems.at[self.used],
+            recv_sem=recv_sem,
+            device_id=(group, place),
+            device_id_type=MESH,
+        )
+        self.used += 1
+        self.pending.append((copy, when))
+        if when is None:
+            copy.start()
+        else:
+            pl.when(when)(copy.start)
+
+    def finish(self):
+        for copy, when in self.pending:
+            if when is None:
+                copy.wait_send()
+            else:
+                pl.when(when)(copy.wait_send)
+        self.pending = []
+
+
+def local(src, dst, sem, when=None):
+    copy = pltpu.make_async_copy(src, dst, sem)
+    if when is None:
+        copy.start()
+    else:
+        pl.when(when)(copy.start)
+
+
+def arrived(ref, sem, when=None):
+    copy = pltpu.make_async_copy(ref, ref, sem)
+    if when is None:
+        copy.wait()
+    else:
+        pl.when(when)(copy.wait)
+
+
+def where_am_i():
+    g, s = lax.axis_index("grp"), lax.axis_index("seq")
+    return g, s, g // 2, g % 2, s // 2, s % 2
+
+
+def across(y, x):
+    return (y * 2 + 1 - x, (1 - y) * 2 + x, (1 - y) * 2 + 1 - x)
+
+
+def greet(partners):
+    barrier = pltpu.get_barrier_semaphore()
+    for partner in partners:
+        pl.semaphore_signal(barrier, inc=1, device_id=partner, device_id_type=MESH)
+    pl.semaphore_wait(barrier, len(partners))
+
+
+def aligned(index, unit, step):
+    return pl.ds(pl.multiple_of(index * unit, step), unit)
+
+
+class Gather:
+    def __init__(self, copies, out, rows, hop_sem, side_sem):
+        self.copies, self.out, self.rows = copies, out, rows
+        self.hop_sem, self.side_sem = hop_sem, side_sem
+        self.g, self.s, _, _, self.z, self.c = where_am_i()
+
+    def block(self, b, z, core):
+        return self.out.at[b, aligned(2 * z + core, self.rows, 16)]
+
+    def spread(self, src, b, z_of, k, right, left):
+        g, s, z, c = self.g, self.s, self.z, self.c
+        dst = self.block(b, z_of, c)
+        if right is not None:
+            self.copies.remote(src, dst, self.hop_sem.at[b, 0, k], g, (s + 2) % 8, right)
+        if left is not None:
+            self.copies.remote(src, dst, self.hop_sem.at[b, 1, k], g, (s + 6) % 8, left)
+
+    def begin(self, src, own_sem, b):
+        g, s, z, c = self.g, self.s, self.z, self.c
+        self.spread(src, b, z, 0, z < 3, z > 0)
+        self.copies.remote(src, self.block(b, z, c), self.side_sem.at[b, 0], g, s + 1 - 2 * c)
+        local(src, self.block(b, z, c), own_sem)
+
+    def step(self, b, k):
+        g, s, z, c = self.g, self.s, self.z, self.c
+        side = s + 1 - 2 * c
+        has = z >= k
+        at = jnp.maximum(z - k, 0)
+        ref = self.block(b, at, c)
+        arrived(ref, self.hop_sem.at[b, 0, k - 1], has)
+        if k < 3:
+            self.spread(ref, b, at, k, jnp.logical_and(has, z < 3), None)
+        self.copies.remote(ref, ref, self.side_sem.at[b, k], g, side, has)
+        has = z + k <= 3
+        at = jnp.minimum(z + k, 3)
+        ref = self.block(b, at, c)
+        arrived(ref, self.hop_sem.at[b, 1, k - 1], has)
+        if k < 3:
+            self.spread(ref, b, at, k, None, jnp.logical_and(has, z > 0))
+        self.copies.remote(ref, ref, self.side_sem.at[b, 3 + k], g, side, has)
+
+    def finish(self, own_sem, b):
+        z, c = self.z, self.c
+        arrived(self.block(b, z, c), own_sem)
+        arrived(self.block(b, z, 1 - c), self.side_sem.at[b, 0])
+        for k in (1, 2, 3):
+            arrived(self.block(b, jnp.maximum(z - k, 0), 1 - c), self.side_sem.at[b, k], z >= k)
+            arrived(self.block(b, jnp.minimum(z + k, 3), 1 - c), self.side_sem.at[b, 3 + k], z + k <= 3)
+
+
+def line_partners(g, s):
+    return [(g, (s + d) % 8) for d in range(1, 8)]
+
+
+def distribute(
+    n1, dm, wq, wk, wv, wu, wo, w1, w2, w3,
+    n1_all, dm_all, q_all, k_all, v_all, u_all, o_all, f_all, s_all, t_all,
+    send, own, hop_n, side_n, hop_d, side_d, z_head, z_out, z_ff, xy_head, xy_out, xy_ff,
+):
+    g, s, y, x, z, c = where_am_i()
+    others = across(y, x)
+    greet(line_partners(g, s) + [(o, s) for o in others])
+    copies = Copies(send)
+    rows = n1.shape[1]
+    gather_n = Gather(copies, n1_all, rows, hop_n, side_n)
+    gather_d = Gather(copies, dm_all, rows, hop_d, side_d)
+    heads = list(zip((wq, wk, wv, wu), (q_all, k_all, v_all, u_all)))
+    depth = wq.shape[0]
+    head = q_all.shape[1] // 2
+    wide = wq.shape[1]
+    ff = f_all.shape[0] // 4
+    for b in range(2):
+        gather_n.begin(n1.at[b], own.at[0, b], b)
+    target = g // 2
+    mine = aligned(g % 2, head, head)
+    for d in (1, 2, 3, 0):
+        to = (z + d) % 4
+        for n, (src, dst) in enumerate(heads):
+            a, b = src.at[:, aligned(to, head, head)], dst.at[aligned(s, depth, 16), mine]
+            if d:
+                copies.remote(a, b, z_head.at[n, z], g, 2 * to + target)
+            else:
+                copies.remote(a, b, z_head.at[n, z], g, 2 * to + target, c != target)
+                local(a, b, z_head.at[n, z], c == target)
+    for i in range(2):
+        to = 2 * c + i
+        a = wo.at[pl.ds(i * head, head)]
+        b = o_all.at[aligned(z % 2, head, head), aligned(g, wide, 128)]
+        self_ = jnp.logical_and(to == z, c == z // 2)
+        copies.remote(a, b, z_out.at[z % 2], g, 2 * to + z // 2, jnp.logical_not(self_))
+        local(a, b, z_out.at[z % 2], self_)
+    for n, (src, dst) in enumerate(((w1, f_all), (w2, s_all))):
+        for d in (1, 2, 3, 4, 5, 6, 7, 0):
+            to = (s + d) % 8
+            a = src.at[aligned(to, ff, 16)]
+            b = dst.at[aligned(g, ff, 16), aligned(s, depth, 128)]
+            if d:
+                copies.remote(a, b, z_ff.at[n, z], g, to)
+            else:
+                local(a, b, z_ff.at[n, z])
+    for d in (1, 2, 3, 0):
+        to = 4 * c + (s + d) % 4
+        a = w3.at[aligned(to % 4, ff, 16)]
+        b = t_all.at[aligned(z, ff, 16), aligned(g, wide, 128)]
+        if d:
+            copies.remote(a, b, z_ff.at[2, z], g, to)
+        else:
+            self_ = s // 4 == c
+            copies.remote(a, b, z_ff.at[2, z], g, to, jnp.logical_not(self_))
+            local(a, b, z_ff.at[2, z], self_)
+    for b in range(2):
+        gather_d.begin(dm.at[b], own.at[1, b], b)
+
+    order = [(z + d) % 4 for d in (0, 1, 3, 2)]
+    for k in (1, 2, 3):
+        for b in range(2):
+            gather_n.step(b, k)
+    here = c == target
+    for d, zs in enumerate(order):
+        for n, (_, dst) in enumerate(heads):
+            block = dst.at[aligned(zs, 2 * depth, 16), mine]
+            arrived(block, z_head.at[n, zs], here)
+            for r, o in enumerate(others):
+                copies.remote(block, block, xy_head.at[n, r, zs], o, s, here)
+    block = o_all.at[:, aligned(g, wide, 128)]
+    for j in range(2):
+        arrived(o_all.at[pl.ds(j * head, head), aligned(g, wide, 128)], z_out.at[j])
+    for r, o in enumerate(others):
+        copies.remote(block, block, xy_out.at[r], o, s)
+    for n, dst in enumerate((f_all, s_all)):
+        for zs in order:
+            block = dst.at[aligned(g, ff, 16), aligned(zs, 2 * depth, 128)]
+            arrived(block, z_ff.at[n, zs])
+            for r, o in enumerate(others):
+                copies.remote(block, block, xy_ff.at[n, r, zs], o, s)
+    for zs in order:
+        block = t_all.at[aligned(zs, ff, 16), aligned(g, wide, 128)]
+        arrived(block, z_ff.at[2, zs])
+        for r, o in enumerate(others):
+            copies.remote(block, block, xy_ff.at[2, r, zs], o, s)
+    for k in (1, 2, 3):
+        for b in range(2):
+            gather_d.step(b, k)
+
+    for b in range(2):
+        gather_n.finish(own.at[0, b], b)
+        gather_d.finish(own.at[1, b], b)
+    for r, o in enumerate(others):
+        from_here = (o // 2) == c
+        for zs in range(4):
+            for n, (_, dst) in enumerate(heads):
+                block = dst.at[pl.ds(zs * 2 * depth, 2 * depth), aligned(o % 2, head, head)]
+                arrived(block, xy_head.at[n, r, zs], from_here)
+        arrived(o_all.at[:, aligned(o, wide, 128)], xy_out.at[r])
+        for n, dst in enumerate((f_all, s_all)):
+            for zs in range(4):
+                arrived(dst.at[aligned(o, ff, 16), pl.ds(zs * 2 * depth, 2 * depth)], xy_ff.at[n, r, zs])
+        for zs in range(4):
+            arrived(t_all.at[pl.ds(zs * ff, ff), aligned(o, wide, 128)], xy_ff.at[2, r, zs])
+    copies.finish()
+
+
+class Scatter:
+    def __init__(self, copies, part, rows, side, own, inbox, side_sem, own_sem, line_sem):
+        self.copies, self.part, self.rows = copies, part, rows
+        self.side, self.own, self.inbox = side, own, inbox
+        self.side_sem, self.own_sem, self.line_sem = side_sem, own_sem, line_sem
+        self.g, self.s, _, _, self.z, self.c = where_am_i()
+
+    def begin(self):
+        g, s, z, c = self.g, self.s, self.z, self.c
+        for k in (2, 1, 3, 0):
+            to = (z + k) % 4
+            theirs = aligned(2 * to + 1 - c, self.rows, 16)
+            mine = aligned(2 * to + c, self.rows, 16)
+            self.copies.remote(
+                self.part.at[:, theirs], self.side.at[k], self.side_sem.at[k], g, s + 1 - 2 * c
+            )
+            local(self.part.at[:, mine], self.own.at[k], self.own_sem.at[k])
+
+    def send(self, k):
+        arrived(self.side.at[k], self.side_sem.at[k])
+        arrived(self.own.at[k], self.own_sem.at[k])
+        if k == 0:
+            return
+        own, side = self.own.at[k], self.side.at[k]
+
+        def add(i, carry):
+            piece = aligned(i, 16, 16)
+            for b in range(2):
+                both = own[b, piece].astype(jnp.float32) + side[b, piece].astype(jnp.float32)
+                own[b, piece] = both.astype(jnp.bfloat16)
+            return carry
+
+        lax.fori_loop(0, self.rows // 16, add, 0)
+        to = (self.z + k) % 4
+        self.copies.remote(own, self.inbox.at[k - 1], self.line_sem.at[k - 1], self.g, 2 * to + self.c)
+
+    def receive(self):
+        for k in range(3):
+            arrived(self.inbox.at[k], self.line_sem.at[k])
+
+    def total(self, b, piece):
+        value = self.own[0, b, piece].astype(jnp.float32) + self.side[0, b, piece].astype(jnp.float32)
+        for k in range(3):
+            value = value + self.inbox[k, b, piece].astype(jnp.float32)
+        return value
+
+
+def everyone_on_line(copies, src, dst, sem, g, s, to_rows):
+    for d in range(1, 8):
+        to = (s + d) % 8
+        copies.remote(to_rows(to), dst.at[s], sem.at[d - 1], g, to)
+
+
+def mean_square(values):
+    return jnp.mean(values * values, axis=-1, keepdims=True)
+
+
+def attention_out(
+    part, squares, x,
+    n2_all, h, branch, scale_all,
+    send, side, own, inbox, side_sem, own_sem, line_sem, n2, inbox_sq, scale, sq_sem, sc_sem, hop, hside, keep, x_v, x_sem,
+    column,
+):
+    g, s, _, _, z, c = where_am_i()
+    greet(line_partners(g, s))
+    copies = Copies(send)
+    rows = x.shape[1]
+    width = x.shape[2]
+    scatter = Scatter(copies, part, rows, side, own, inbox, side_sem, own_sem, line_sem)
+    gather = Gather(copies, n2_all, rows, hop, hside)
+    scatter.begin()
+    everyone_on_line(copies, squares, inbox_sq, sq_sem, g, s, lambda to: squares.at[to])
+    local(squares.at[s], inbox_sq.at[s], sq_sem.at[7])
+    local(x, x_v, x_sem)
+    for k in (2, 1, 3, 0):
+        scatter.send(k)
+    for d in range(8):
+        arrived(inbox_sq.at[0], sq_sem.at[d])
+    total = inbox_sq[0]
+    for d in range(1, 8):
+        total = total + inbox_sq[d]
+    row = lax.rsqrt(total / width + EPS)
+    scale[...] = row
+    for d in range(1, 8):
+        to = (s + d) % 8
+        copies.remote(scale, scale_all.at[s], sc_sem.at[d - 1], g, to)
+    local(scale, scale_all.at[s], sc_sem.at[7])
+    column[...] = jnp.broadcast_to(row[:1], (2 * rows, 2 * rows)).T
+    arrived(x_v, x_sem)
+    scatter.receive()
+    for b in range(2):
+
+        def finish(i, carry):
+            piece = aligned(i, 16, 16)
+            at = aligned(b * (rows // 16) + i, 16, 16)
+            a = scatter.total(b, piece) * column[at, :1]
+            hidden = x_v[b, piece].astype(jnp.float32) + a
+            branch[at] = a
+            h[at] = hidden
+            n2[b, piece] = (hidden * lax.rsqrt(mean_square(hidden) + EPS)).astype(jnp.bfloat16)
+            return carry
+
+        lax.fori_loop(0, rows // 16, finish, 0)
+        gather.begin(n2.at[b], keep.at[b], b)
+    for k in (1, 2, 3):
+        for b in range(2):
+            gather.step(b, k)
+    for b in range(2):
+        gather.finish(keep.at[b], b)
+    for d in range(8):
+        arrived(scale, sc_sem.at[d])
+    copies.finish()
+
+
+def ffn_back(
+    part, part_m, dy, h, branch,
+    da_all, dh, out, mix_all,
+    send, side, own, inbox, side_sem, own_sem, line_sem,
+    side_m, own_m, inbox_m, side_sem_m, own_sem_m, line_sem_m,
+    da, mix, mix_sem, hop, hside, keep, column,
+):
+    g, s, _, _, z, c = where_am_i()
+    greet(line_partners(g, s))
+    copies = Copies(send)
+    rows = part.shape[1] // 8
+    width = part.shape[2]
+    scatter = Scatter(copies, part, rows, side, own, inbox, side_sem, own_sem, line_sem)
+    scatter_m = Scatter(copies, part_m, rows, side_m, own_m, inbox_m, side_sem_m, own_sem_m, line_sem_m)
+    gather = Gather(copies, da_all, rows, hop, hside)
+    scatter.begin()
+    for k in (2, 1, 3, 0):
+        scatter.send(k)
+    scatter_m.begin()
+    scatter.receive()
+    for b in range(2):
+
+        def finish(i, carry):
+            piece = aligned(i, 16, 16)
+            at = aligned(b * (rows // 16) + i, 16, 16)
+            hidden = h[at]
+            inverse = lax.rsqrt(mean_square(hidden) + EPS)
+            normed = hidden * inverse
+            grad = scatter.total(b, piece)
+            along = jnp.mean(normed * grad, axis=-1, keepdims=True)
+            grad_hidden = dy[at] + inverse * (grad - normed * along)
+            dh[at] = grad_hidden
+            low = grad_hidden.astype(jnp.bfloat16)
+            da[b, piece] = low
+            dot = jnp.mean(low.astype(jnp.float32) * branch[at], axis=-1, keepdims=True)
+            column[at] = jnp.broadcast_to(dot, (16, 2 * rows))
+            return carry
+
+        lax.fori_loop(0, rows // 16, finish, 0)
+        gather.begin(da.at[b], keep.at[b], b)
+    mix[...] = column[...].T[:8]
+    for d in range(1, 8):
+        copies.remote(mix, mix_all.at[s], mix_sem.at[d - 1], g, (s + d) % 8)
+    local(mix, mix_all.at[s], mix_sem.at[7])
+    for k in (2, 1, 3, 0):
+        scatter_m.send(k)
+    for k in (1, 2, 3):
+        for b in range(2):
+            gather.step(b, k)
+    scatter_m.receive()
+    for b in range(2):
+
+        def write(i, carry):
+            piece = aligned(i, 16, 16)
+            at = aligned(b * (rows // 16) + i, 16, 16)
+            out[at] = (h[at] + scatter_m.total(b, piece)).astype(jnp.bfloat16)
+            return carry
+
+        lax.fori_loop(0, rows // 16, write, 0)
+    for b in range(2):
+        gather.finish(keep.at[b], b)
+    for d in range(8):
+        arrived(mix, mix_sem.at[d])
+    copies.finish()
+
+
+def gradients(
+    part, gq, gk, gv, gu, go, gf, gs, gt,
+    dn1, fq, fk, fv, fu, fo, ff_, fs, ft,
+    send, side, own, inbox, side_sem, own_sem, line_sem,
+    in_h, in_o, in_f, in_t, xy_h, xy_o, xy_f, xy_t, sum_h, sum_o, sum_f, sum_t, z_h, z_o, z_f, z_t,
+):
+    g, s, y, x, z, c = where_am_i()
+    others = across(y, x)
+    plane = [(o, 2 * z + e) for o in others for e in range(2)]
+    greet(line_partners(g, s) + plane)
+    copies = Copies(send)
+    rows = part.shape[1] // 8
+    scatter = Scatter(copies, part, rows, side, own, inbox, side_sem, own_sem, line_sem)
+    head = 128
+    wide = fo.shape[1]
+    ff = gf.shape[0] // 4
+    depth = fq.shape[0]
+    scatter.begin()
+    for k in (2, 1, 3, 0):
+        scatter.send(k)
+    grads_h = (gq, gk, gv, gu)
+    for n, (src, dst) in enumerate(((gf, in_f), (gs, in_f))):
+        for r, o in enumerate(others):
+            copies.remote(src.at[aligned(o, ff, 16)], dst.at[n, r], xy_f.at[n, r], o, s)
+        local(src.at[aligned(g, ff, 16)], dst.at[n, 3], xy_f.at[n, 3])
+    for r, o in enumerate(others):
+        copies.remote(gt.at[:, aligned(o, wide, 128)], in_t.at[r], xy_t.at[r], o, s)
+    local(gt.at[:, aligned(g, wide, 128)], in_t.at[3], xy_t.at[3])
+    for r, o in enumerate(others):
+        copies.remote(go.at[:, aligned(o, wide, 128)], in_o.at[r], xy_o.at[r], o, s)
+    local(go.at[:, aligned(g, wide, 128)], in_o.at[3], xy_o.at[3])
+    for r, o in enumerate(others + (g,)):
+        holds = o // 2 == c
+        for n, src in enumerate(grads_h):
+            for e in range(2):
+                a = src.at[:, e, :, aligned(o % 2, head, head)]
+                b = in_h.at[n, r]
+                to_self = jnp.logical_and(holds, c == e)
+                if r < 3:
+                    copies.remote(a, b, xy_h.at[n, r], o, 2 * z + e, holds)
+                else:
+                    copies.remote(a, b, xy_h.at[n, r], g, 2 * z + e, jnp.logical_and(holds, c != e))
+                    local(a, b, xy_h.at[n, r], to_self)
+
+    def add_up(read, write, count):
+        def add(i, carry):
+            piece = aligned(i, 16, 16)
+            value = read(0, piece)
+            for r in range(1, 4):
+                value = value + read(r, piece)
+            write(piece, value.astype(jnp.bfloat16))
+            return carry
+
+        lax.fori_loop(0, count, add, 0)
+
+    for n, out in enumerate((ff_, fs)):
+        for r in range(4):
+            arrived(in_f.at[n, r], xy_f.at[n, r])
+        total = sum_f.at[n]
+
+        def write(piece, value):
+            total[piece] = value
+
+        add_up(lambda r, piece: in_f[n, r, piece].astype(jnp.float32), write, ff // 16)
+        for d in (4, 3, 5, 2, 6, 1, 7, 0):
+            to = (s + d) % 8
+            a = total.at[:, aligned(to, depth, 128)]
+            b = out.at[aligned(s, ff, 16)]
+            if d:
+                copies.remote(a, b, z_f.at[n, d], g, to)
+            else:
+                local(a, b, z_f.at[n, d])
+    for r in range(4):
+        arrived(in_t.at[r], xy_t.at[r])
+
+    def write(piece, value):
+        sum_t[piece] = value
+
+    add_up(lambda r, piece: in_t[r, piece].astype(jnp.float32), write, 4 * ff // 16)
+    for d in (2, 1, 3, 0):
+        to = 2 * ((z + d) % 4) + s // 4
+        a = sum_t.at[aligned((z + d) % 4, ff, 16)]
+        b = ft.at[aligned(s % 4, ff, 16)]
+        self_ = to == s
+        if d:
+            copies.remote(a, b, z_t.at[s % 4], g, to)
+        else:
+            copies.remote(a, b, z_t.at[s % 4], g, to, jnp.logical_not(self_))
+            local(a, b, z_t.at[s % 4], self_)
+    for r in range(4):
+        arrived(in_o.at[r], xy_o.at[r])
+
+    def write(piece, value):
+        sum_o[piece] = value
+
+    add_up(lambda r, piece: in_o[r, piece].astype(jnp.float32), write, 2 * head // 16)
+    for j in range(2):
+        to = 2 * (2 * c + j) + z // 2
+        a = sum_o.at[pl.ds(j * head, head)]
+        b = fo.at[aligned(z % 2, head, head)]
+        self_ = to == s
+        copies.remote(a, b, z_o.at[z % 2], g, to, jnp.logical_not(self_))
+        local(a, b, z_o.at[z % 2], self_)
+    for n, out in enumerate((fq, fk, fv, fu)):
+        for r in range(4):
+            arrived(in_h.at[n, r], xy_h.at[n, r])
+        total = sum_h.at[n]
+        for q in range(4):
+
+            def write(piece, value):
+                total[q, piece] = value
+
+            add_up(lambda r, piece: in_h[n, r, q, piece].astype(jnp.float32), write, depth // 16)
+        for d in (2, 1, 3, 0):
+            to = (z + d) % 4
+            a = total.at[to]
+            b = out.at[:, aligned(z, head, head)]
+            if d:
+                copies.remote(a, b, z_h.at[n, d], g, 2 * to + c)
+            else:
+                local(a, b, z_h.at[n, d])
+    scatter.receive()
+    for b in range(2):
+
+        def finish(i, carry):
+            piece = aligned(i, 16, 16)
+            at = aligned(b * (rows // 16) + i, 16, 16)
+            dn1[at] = scatter.total(b, piece)
+            return carry
+
+        lax.fori_loop(0, rows // 16, finish, 0)
+    for n, out in enumerate((ff_, fs)):
+        for d in range(8):
+            arrived(out.at[pl.ds(0, ff)], z_f.at[n, d])
+    for d in range(4):
+        arrived(ft.at[pl.ds(0, ff)], z_t.at[d])
+    for j in range(2):
+        arrived(fo.at[pl.ds(0, head)], z_o.at[j])
+    for n, out in enumerate((fq, fk, fv, fu)):
+        for d in range(4):
+            arrived(out.at[:, pl.ds(0, head)], z_h.at[n, d])
+    copies.finish()
+
+
+def call(kernel, number, ins, outs, scratch, name):
+    return pl.pallas_call(
+        kernel,
+        out_shape=[shape for shape, _ in outs],
+        in_specs=[spec for _, spec in ins],
+        out_specs=[spec for _, spec in outs],
+        scratch_shapes=scratch,
+        compiler_params=pltpu.CompilerParams(
+            collective_id=number, has_side_effects=True, vmem_limit_bytes=48 * 2**20
+        ),
+        name=name,
+    )(*[value for value, _ in ins])
+
+
+def low_array(*shape):
+    return jax.ShapeDtypeStruct(shape, jnp.bfloat16)
+
+
+def wide_array(*shape):
+    return jax.ShapeDtypeStruct(shape, jnp.float32)
+
+
+def dma(*shape):
+    return pltpu.SemaphoreType.DMA(shape)
+
+
+def scatter_scratch(rows, width):
+    return [
+        pltpu.VMEM((4, 2, rows, width), jnp.bfloat16),
+        pltpu.VMEM((4, 2, rows, width), jnp.bfloat16),
+        pltpu.VMEM((3, 2, rows, width), jnp.bfloat16),
+        dma(4),
+        dma(4),
+        dma(3),
+    ]
+
+
+def line_shards(
+    tokens, cotangent, lengths, decay_rate,
+    w_query, w_key, w_value, w_gate, w_out, w_first, w_second, w_third,
+):
+    bf16, f32 = jnp.bfloat16, jnp.float32
+    rows, width = tokens.shape[2], tokens.shape[3]
+    depth, wide = w_query.shape
+    head = width // decay_rate.shape[0]
+    hidden = w_third.shape[0]
+    length = 8 * rows
+    s = lax.axis_index("seq")
+    z, c = s // 2, s % 2
+    x_low = tokens[:, 0]
+    x = x_low.astype(f32).reshape(2 * rows, width)
+    slots = s * rows + jnp.arange(rows)
+    mine = (slots[None] < lengths[:, :1]).astype(f32).reshape(2 * rows, 1)
+    live = (jnp.arange(length)[None] < lengths[:, :1]).astype(f32).reshape(2 * length, 1)
+    dy = cotangent[:, 0].astype(f32).reshape(2 * rows, width) * mine
+    n1 = norm_rows(x).astype(bf16).reshape(2, rows, width)
+    dm = dy.astype(bf16).reshape(2, rows, width)
+
+    n1_all, dm_all, q_w, k_w, v_w, u_w, o_w, f_w, s_w, t_w = call(
+        distribute,
+        0,
+        [(v, ANY) for v in (n1, dm, w_query, w_key, w_value, w_gate, w_out, w_first.T, w_second.T, w_third)],
+        [(low_array(2, length, width), ANY)] * 2
+        + [(low_array(width, 2 * head), ANY)] * 4
+        + [(low_array(2 * head, width), ANY)]
+        + [(low_array(hidden, width), ANY)] * 3,
+        [dma(200), dma(2, 2), dma(2, 2, 3), dma(2, 7), dma(2, 2, 3), dma(2, 7),
+         dma(4, 4), dma(2), dma(3, 4), dma(4, 3, 4), dma(3), dma(3, 3, 4)],
+        "distribute",
+    )
+    n1_all = n1_all.reshape(2 * length, width)
+    dm_all = dm_all.reshape(2 * length, width)
+    q_pre, k_pre, v_pre, u_pre = [product(n1_all, w) for w in (q_w, k_w, v_w, u_w)]
+
+    def split(values):
+        return values.reshape(2, length, 2, head)
+
+    q = split(jax.nn.silu(q_pre).astype(bf16))
+    live_low = live.astype(bf16)
+    k = split(jax.nn.silu(k_pre).astype(bf16) * live_low)
+    v = split(jax.nn.silu(v_pre).astype(bf16) * live_low)
+    rates = jnp.take(decay_rate, 4 * (2 * c + jnp.arange(2)) + z)
+    places = jnp.arange(length).astype(f32)
+    offset = places[:, None] - places[None, :]
+    weight = jnp.where(offset >= 0, jnp.exp(-rates[:, None, None] * jnp.maximum(offset, 0.0)), 0.0)
+    scores = (jnp.einsum("bihd,bjhd->bhij", q, k, preferred_element_type=f32) * weight).astype(bf16)
+    o = jnp.einsum("bhij,bjhe->bihe", scores, v, preferred_element_type=f32).reshape(2 * length, 2 * head)
+    u = jax.nn.silu(u_pre)
+    g = u * o
+    squares = jnp.sum(g * g, axis=-1).reshape(2, 8, rows).transpose(1, 0, 2).reshape(8, 1, 2 * rows)
+    squares = jnp.broadcast_to(squares, (8, 8, 2 * rows))
+    part = product(g.astype(bf16), o_w).astype(bf16).reshape(2, length, width)
+
+    n2_all, h, branch, scale_all = call(
+        attention_out,
+        1,
+        [(part, ANY), (squares, ANY), (x_low, ANY)],
+        [(low_array(2, length, width), ANY), (wide_array(2 * rows, width), VMEM), (wide_array(2 * rows, width), VMEM),
+         (wide_array(8, 8, 2 * rows), ANY)],
+        [dma(80)] + scatter_scratch(rows, width)
+        + [pltpu.VMEM((2, rows, width), bf16), pltpu.VMEM((8, 8, 2 * rows), f32), pltpu.VMEM((8, 2 * rows), f32), dma(8), dma(8),
+           dma(2, 2, 3), dma(2, 7), dma(2), pltpu.VMEM((2, rows, width), bf16), dma(),
+           pltpu.VMEM((2 * rows, 2 * rows), f32)],
+        "attention_out",
+    )
+
+    def per_token(values):
+        return values[:, 0].reshape(8, 2, rows).transpose(1, 0, 2).reshape(2 * length, 1)
+
+    n2_all = n2_all.reshape(2 * length, width)
+    h1 = product_right(n2_all, f_w)
+    h2 = product_right(n2_all, s_w)
+    p = (h1 * h2).astype(bf16)
+    part_m = product(p, t_w).astype(bf16).reshape(2, length, width)
+    dp = product_right(dm_all, t_w)
+    dh1 = (dp * h2).astype(bf16)
+    dh2 = (dp * h1).astype(bf16)
+    part = (product(dh1, f_w) + product(dh2, s_w)).astype(bf16).reshape(2, length, width)
+    gf = product_left(dh1, n2_all).astype(bf16)
+    gs = product_left(dh2, n2_all).astype(bf16)
+    gt = product_left(p, dm_all).astype(bf16)
+
+    da_all, dh, out, mix_all = call(
+        ffn_back,
+        2,
+        [(part, ANY), (part_m, ANY), (dy, VMEM), (h, VMEM), (branch, VMEM)],
+        [(low_array(2, length, width), ANY), (wide_array(2 * rows, width), VMEM), (low_array(2 * rows, width), VMEM),
+         (wide_array(8, 8, 2 * rows), ANY)],
+        [dma(80)] + scatter_scratch(rows, width) + scatter_scratch(rows, width)
+        + [pltpu.VMEM((2, rows, width), bf16), pltpu.VMEM((8, 2 * rows), f32), dma(8),
+           dma(2, 2, 3), dma(2, 7), dma(2), pltpu.VMEM((2 * rows, 2 * rows), f32)],
+        "ffn_back",
+    )
+    da_all = da_all.reshape(2 * length, width)
+    inverse = per_token(scale_all)
+    mix = per_token(mix_all)
+    nat = g * inverse
+    go = product_left(nat.astype(bf16), da_all).astype(bf16)
+    dg = inverse * (product_right(da_all, o_w) - nat * mix)
+    do = split((dg * u).astype(bf16))
+    du_pre = (dg * o * silu_slope(u_pre)).astype(bf16)
+    d_scores = (jnp.einsum("bihe,bjhe->bhij", do, v, preferred_element_type=f32) * weight).astype(bf16)
+    dq = jnp.einsum("bhij,bjhd->bihd", d_scores, k, preferred_element_type=f32).reshape(2 * length, 2 * head)
+    dk = jnp.einsum("bhij,bihd->bjhd", d_scores, q, preferred_element_type=f32).reshape(2 * length, 2 * head)
+    dv = jnp.einsum("bhij,bihe->bjhe", scores, do, preferred_element_type=f32).reshape(2 * length, 2 * head)
+    dq_pre = (dq * silu_slope(q_pre)).astype(bf16)
+    dk_pre = (dk * live * silu_slope(k_pre)).astype(bf16)
+    dv_pre = (dv * live * silu_slope(v_pre)).astype(bf16)
+    part = product_right(dq_pre, q_w) + product_right(dk_pre, k_w)
+    part = (part + product_right(dv_pre, v_w) + product_right(du_pre, u_w)).astype(bf16).reshape(2, length, width)
+    heads = [product_left(n1_all, d).astype(bf16).reshape(4, 2, depth, 2 * head) for d in (dq_pre, dk_pre, dv_pre, du_pre)]
+
+    dn1, fq, fk, fv, fu, fo, ff, fs, ft = call(
+        gradients,
+        3,
+        [(v, ANY) for v in [part] + heads + [go, gf, gs, gt]],
+        [(wide_array(2 * rows, width), VMEM)] + [(low_array(depth, wide), ANY)] * 4 + [(low_array(depth, wide), ANY)]
+        + [(low_array(2 * hidden, depth), ANY)] * 2 + [(low_array(hidden, wide), ANY)],
+        [dma(140)] + scatter_scratch(rows, width)
+        + [pltpu.VMEM((4, 4, 4, depth, head), bf16), pltpu.VMEM((4, 2 * head, wide), bf16),
+           pltpu.VMEM((2, 4, hidden // 4, width), bf16), pltpu.VMEM((4, hidden, wide), bf16),
+           dma(4, 4), dma(4), dma(2, 4), dma(4),
+           pltpu.VMEM((4, 4, depth, head), bf16), pltpu.VMEM((2 * head, wide), bf16),
+           pltpu.VMEM((2, hidden // 4, width), bf16), pltpu.VMEM((hidden, wide), bf16),
+           dma(4, 4), dma(2), dma(2, 8), dma(4)],
+        "gradients",
+    )
+    grad_x = dh + norm_back(x, dn1)
+    return (
+        out.reshape(2, 1, rows, width),
+        grad_x.reshape(2, 1, rows, width),
+        fq.astype(f32), fk.astype(f32), fv.astype(f32), fu.astype(f32), fo.astype(f32),
+        ff.T.astype(f32), fs.T.astype(f32), ft.astype(f32),
+    )
+
+
 def solution(mesh):
     in_specs = (
         P(None, "grp", "seq", None),
@@ -299,4 +1033,5 @@
         P("seq", "grp"),
         P("seq", "grp"),
     )
-    return jax.shard_map(shards, mesh=mesh, in_specs=in_specs, out_specs=out_specs, check_vma=False)
+    fast = mesh.shape["grp"] == 4 and mesh.shape["seq"] == 8
+    return jax.shard_map(line_shards if fast else shards, mesh=mesh, in_specs=in_specs, out_specs=out_specs, check_vma=False)

time: 5160 us -> 822 us (0.16)
  waiting for transfers between devices: 4660 us -> 0 us
  Pallas kernels: 0 us -> 649 us
  matrix products: 354 us -> 109 us
    unnamed x33 -> x0, waiting for transfers between devices: 1760 us -> none
    reduce_scatter x11 -> x0, waiting for transfers between devices: 1520 us -> none  [the longest x1 641 us: shards(): lax.psum_scatter(product_left(first_all, attn_all), 'seq', scatter_dimens...]
    all_gather x20 -> x0, waiting for transfers between devices: 1380 us -> none  [the longest x4 205 us: prefix(): pieces = jax.tree.map(lambda part: lax.all_gather(part, axis), value)]
    pallas_call x0 -> x4, Pallas kernels: none -> 649 us  [call(): pl.pallas_call(kernel, out_shape=[shape for shape, _ in outs], in_specs=[...]
    dot_general x16 -> x8, matrix products: 109 us -> 32.5 us  [product(): return jnp.dot(left, right, preferred_element_type=jnp.float32)]
    dot_general x16 -> x8, matrix products: 117 us -> 44.7 us  [product_right(): lax.dot_general(left, right, (((1,), (1,)), ((), ())), preferred_element_...]
    dot_general x4 -> x8, matrix products: 87.5 us -> 24.6 us  [product_left(): lax.dot_general(left, right, (((0,), (0,)), ((), ())), preferred_element_...]
  transfers between devices with their start and end apart: 32 -> 0, of which waited for: 30 -> 0; matrix products, arithmetic and copies ran while one was open for 7% -> 0% of each run, Pallas kernels for 0% -> 0%
where the time goes in v1:
time: 822 us; the launch traced here: 810 us
  Pallas kernels  649 us (79%)
  matrix products  109 us (13%)
  local copies, waits for them, and re-layouts  30.6 us (4%)
  other arithmetic  18.8 us (2%)
    pallas_call x4, Pallas kernels, call(): pl.pallas_call(kernel, out_shape=[shape for shape, _ in outs], in_specs=[...  649 us
    dot_general x8, matrix products, product_right(): lax.dot_general(left, right, (((1,), (1,)), ((), ())), preferred_element_...  44.7 us
    dot_general x8, matrix products, product(): return jnp.dot(left, right, preferred_element_type=jnp.float32)  32.5 us
    dot_general x8, matrix products, product_left(): lax.dot_general(left, right, (((0,), (0,)), ((), ())), preferred_element_...  24.6 us
    unnamed x110, local copies, waits for them, and re-layouts  16.7 us

profile of v1, /device:TPU:0, one launch (start us, length us, event | category | flops | bytes accessed | tf_op | source)
XLA Modules:
  0.0 809.6 jit_solution(9375470304344577005)
XLA Ops:
  0.7 0.8 compare_convert_fusion.1
  2.1 1.2 fusion.2
  6.4 0.9 subtract_compare_fusion
  7.4 1.4 copy.83
  9.2 2.7 exponential_select_fusion
  13.4 262.6 %distribute.1 = (bf16[2,512,2048]{2,1,0:T(8,128)(2,1)}, bf16[2,512,2048]{2,1,0:T(8,128)(2,1)}, bf16[2048,256]{1,0:T(8,128)(2,1)S(1)}, bf16[2048,256]{1,0:T(8,128...) custom-call(bf16[2,64,2048]{2,1,0:T(8,128)(2,1)S(1)} %get-tuple-elem, ...), custom_call_target="tpu_custom_call" | custom-call | tf_op jit(solution)/shard_map/distribute/pallas_call | solution.py:834
  276.1 5.2 fusion.24
  281.3 2.5 multiply_convert_fusion.11
  283.8 1.4 reshape.282
  285.3 5.2 fusion.9
  290.4 1.4 reshape.283
  291.9 2.4 reshape.281
  294.3 1.5 copy.100
  295.8 2.5 multiply_convert_fusion.1
  298.4 0.8 convolution_bitcast_fusion.3
  299.3 0.8 copy.94
  300.3 1.3 copy-done.41
  302.1 2.4 multiply_reduce_fusion
  304.6 8.1 %fusion.23 = f32[1024,704]{0,1:T(8,128)} fusion(bf16[1024,2048]{1,0:T(8,128)(2,1)} %bitcast.181, bf16[704,2048]{1,0:T(8,128)(2,1)} %get-tuple-element.38), kind=kOutput, calls=%fused_computation.86 | convolution fusion | flops 2952790016 | bytes 9961472 | tf_op jit(solution)/shard_map/dot_general | solution.py:57
  312.8 3.3 convolution_convert_fusion.1
  316.0 94.7 %attention_out.1 = (bf16[2,512,2048]{2,1,0:T(8,128)(2,1)}, f32[128,2048]{1,0:T(8,128)S(1)}, f32[128,2048]{1,0:T(8,128)S(1)}, f32[8,8,128]{2,1,0:T(8,128)S(1)}) custom-call(bf16[2,512,2048]{2,1,0:T(8,128)(2,1)} %bitcast.149, f32[8,8,128]{2,1,0:T(8,128)S(1)} %broadcast_in_dim.19.squares, bf16[2,64,2048]{2,1,0:T(8,128)(2,1)S(1)} %bitcast.144), custom_call_target="tpu_custom_call" | custom-call | tf_op jit(solution)/shard_map/attention_out/pallas_call | solution.py:834
  410.8 1.0 copy-done.5
  411.8 1.0 copy-done.7
  413.0 6.4 fusion.25
  419.4 3.5 multiply_convert_fusion.2
  423.0 4.6 convolution_convert_fusion.2.gt
  427.5 5.1 convolution_convert_fusion
  432.7 4.5 convolution_convert_fusion.4.gf
  437.2 4.6 convolution_convert_fusion.3.gs
  441.8 3.6 fusion.26
  445.4 5.2 add_convert_fusion.1
  450.6 132.0 %ffn_back.1 = (bf16[2,512,2048]{2,1,0:T(8,128)(2,1)}, f32[128,2048]{1,0:T(8,128)S(1)}, bf16[128,2048]{1,0:T(8,128)(2,1)S(1)}, f32[8,8,128]{2,1,0:T(8,128)S(1)}) custom-call(bf16[2,512,2048]{2,1,0:T(8,128)(2,1)} %bitcast.159, bf16[2,512,2048]{2,1,0:T(8,128)(2,1)} %bitcast.158, f32[128,2048]{1,0:T(8,128)S(1)} %bitcast_multiply_fusion.2.dy, ...), custom_call_target="tpu_custom_call" | custom-call | tf_op jit(solution)/shard_map/ffn_back/pallas_call | solution.py:834
  582.6 0.8 copy-done.10
  583.6 6.2 multiply_convert_fusion.5
  589.7 2.3 convolution_convert_fusion.5.go
  592.0 1.5 reshape.292
  593.5 2.2 convolution_bitcast_fusion
  596.5 0.8 copy.108
  598.4 0.8 convolution_bitcast_fusion.2
  599.2 0.8 copy.102
  600.8 0.8 copy.105
  602.0 0.8 multiply_convert_fusion.7
  602.8 1.3 copy-done.42
  604.0 2.4 convolution_convert_fusion.8
  606.4 2.6 convolution_convert_fusion.7
  609.0 1.4 convolution_convert_fusion.9
  610.4 2.4 convolution_convert_fusion.6
  612.8 1.3 fusion.27
  614.1 4.7 fusion.29
  618.8 4.6 fusion.28
  623.3 10.0 %add_convert_fusion = bf16[1024,2048]{1,0:T(8,128)(2,1)} fusion(f32[1024,2048]{1,0:T(8,128)} %fusion.29, f32[1024,2048]{1,0:T(8,128)S(1)} %fusion.27, f32[1024,2048]{1,0:T(8,128)} %fusion.28, bf16[1024,256]{0,1:T(8,128)(2,1)S(1)} %copy-done.36, bf16[2048,256]{1,0:T(8,128)(2,1)} %get-tuple-element.40), kind=kOutput, calls=%fused_computation.1 | convolution fusion | flops 1082130432 | bytes 30932992 | tf_op jit(solution)/shard_map/dot_general | solution.py:57
  633.3 159.9 %gradients.1 = (f32[128,2048]{1,0:T(8,128)S(1)}, bf16[256,512]{1,0:T(8,128)(2,1)S(1)}, bf16[256,512]{1,0:T(8,128)(2,1)S(1)}, bf16[256,512]{1,0:T(8,128)(2,1)S(1)...) custom-call(bf16[2,512,2048]{2,1,0:T(8,128)(2,1)} %bitcast.150, ...), custom_call_target="tpu_custom_call" | custom-call | tf_op jit(solution)/shard_map/gradients/pallas_call | solution.py:834
  793.4 1.3 fusion.1
  794.7 0.9 convert_element_type.237
  795.5 0.9 convert_element_type.238
  796.4 0.9 convert_element_type.239
  797.2 0.9 convert_element_type.240
  798.1 0.9 convert_element_type.241
  798.9 1.2 convert_bitcast_fusion.1
  800.1 2.9 copy.112
  803.0 1.2 convert_bitcast_fusion
  804.2 3.0 copy.113
  807.2 1.3 convert_element_type.246
  808.5 0.8 copy.140
  (133 shorter events, 10.0 us)
Async XLA Ops:
  0.6 3.3 copy-start
  0.7 8.1 copy-start.35
  8.8 3.2 copy-start.2
  8.8 3.2 copy-start.25
  9.2 3.1 copy-start.38
  12.0 1.1 copy-start.9
  12.0 1.2 copy-start.12
  12.0 1.2 copy-start.13
  12.0 1.3 copy-start.14
  12.0 1.4 copy-start.15
  12.0 1.4 copy-start.16
  276.1 5.2 copy-start.3
  276.1 5.2 copy-start.40
  281.3 4.0 copy-start.26
  281.3 4.0 copy-start.37
  291.9 6.5 copy-start.19
  295.8 2.6 copy-start.21
  298.4 1.7 copy-start.18
  298.4 3.2 copy-start.41
  299.3 2.8 copy-start.34
  300.3 4.2 copy-start.31
  304.5 8.3 %copy-start.23 = (f32[1024,256]{0,1:T(8,128)}, f32[1024,256]{0,1:T(8,128)S(1)}, u32[]{:S(2)}) copy-start(f32[1024,256]{0,1:T(8,128)S(1)} %get-tuple-element.95) | copy-start | bytes 3145732
  304.6 8.1 %copy-start.29 = (bf16[256,2048]{1,0:T(8,128)(2,1)S(1)}, bf16[256,2048]{1,0:T(8,128)(2,1)}, u32[]{:S(2)}) copy-start(bf16[256,2048]{1,0:T(8,128)(2,1)} %get-tuple-element.44) | copy-start | bytes 3145732
  410.8 1.0 copy-start.5
  411.8 1.0 copy-start.7
  413.0 6.4 copy-start.44
  413.0 6.4 copy-start.47
  413.0 6.4 copy-start.49
  419.4 3.5 copy-start.43
  422.9 4.6 copy-start.48
  441.8 3.6 copy-start.46
  445.4 5.2 copy-start.6
  445.4 5.2 copy-start.8
  582.6 0.8 copy-start.10
  583.6 6.2 copy-start.24
  583.6 6.2 copy-start.45
  592.0 3.7 copy-start.22
  593.5 2.2 copy-start.17
  597.3 1.0 copy-start.20
  599.2 1.2 copy-start.30
  600.4 1.4 copy-start.32
  600.4 1.6 copy-start.33
  601.8 2.2 copy-start.42
  609.0 1.4 copy-start.36
  610.4 2.4 copy-start.4
  612.8 1.3 copy-start.28
  614.1 4.7 copy-start.27
  633.3 160.1 %copy-start.39 = (f32[128]{0:T(128)S(1)}, f32[128]{0:T(128)}, u32[]{:S(2)}) copy-start(f32[128]{0:T(128)} %add.165) | copy-start | bytes 1540
  803.0 6.3 copy-start.1
  804.2 4.3 copy-start.11

commit v2 on v1

--- a/solution.py
+++ b/solution.py
@@ -398,114 +398,6 @@
     return [(g, (s + d) % 8) for d in range(1, 8)]
 
 
-def distribute(
-    n1, dm, wq, wk, wv, wu, wo, w1, w2, w3,
-    n1_all, dm_all, q_all, k_all, v_all, u_all, o_all, f_all, s_all, t_all,
-    send, own, hop_n, side_n, hop_d, side_d, z_head, z_out, z_ff, xy_head, xy_out, xy_ff,
-):
-    g, s, y, x, z, c = where_am_i()
-    others = across(y, x)
-    greet(line_partners(g, s) + [(o, s) for o in others])
-    copies = Copies(send)
-    rows = n1.shape[1]
-    gather_n = Gather(copies, n1_all, rows, hop_n, side_n)
-    gather_d = Gather(copies, dm_all, rows, hop_d, side_d)
-    heads = list(zip((wq, wk, wv, wu), (q_all, k_all, v_all, u_all)))
-    depth = wq.shape[0]
-    head = q_all.shape[1] // 2
-    wide = wq.shape[1]
-    ff = f_all.shape[0] // 4
-    for b in range(2):
-        gather_n.begin(n1.at[b], own.at[0, b], b)
-    target = g // 2
-    mine = aligned(g % 2, head, head)
-    for d in (1, 2, 3, 0):
-        to = (z + d) % 4
-        for n, (src, dst) in enumerate(heads):
-            a, b = src.at[:, aligned(to, head, head)], dst.at[aligned(s, depth, 16), mine]
-            if d:
-                copies.remote(a, b, z_head.at[n, z], g, 2 * to + target)
-            else:
-                copies.remote(a, b, z_head.at[n, z], g, 2 * to + target, c != target)
-                local(a, b, z_head.at[n, z], c == target)
-    for i in range(2):
-        to = 2 * c + i
-        a = wo.at[pl.ds(i * head, head)]
-        b = o_all.at[aligned(z % 2, head, head), aligned(g, wide, 128)]
-        self_ = jnp.logical_and(to == z, c == z // 2)
-        copies.remote(a, b, z_out.at[z % 2], g, 2 * to + z // 2, jnp.logical_not(self_))
-        local(a, b, z_out.at[z % 2], self_)
-    for n, (src, dst) in enumerate(((w1, f_all), (w2, s_all))):
-        for d in (1, 2, 3, 4, 5, 6, 7, 0):
-            to = (s + d) % 8
-            a = src.at[aligned(to, ff, 16)]
-            b = dst.at[aligned(g, ff, 16), aligned(s, depth, 128)]
-            if d:
-                copies.remote(a, b, z_ff.at[n, z], g, to)
-            else:
-                local(a, b, z_ff.at[n, z])
-    for d in (1, 2, 3, 0):
-        to = 4 * c + (s + d) % 4
-        a = w3.at[aligned(to % 4, ff, 16)]
-        b = t_all.at[aligned(z, ff, 16), aligned(g, wide, 128)]
-        if d:
-            copies.remote(a, b, z_ff.at[2, z], g, to)
-        else:
-            self_ = s // 4 == c
-            copies.remote(a, b, z_ff.at[2, z], g, to, jnp.logical_not(self_))
-            local(a, b, z_ff.at[2, z], self_)
-    for b in range(2):
-        gather_d.begin(dm.at[b], own.at[1, b], b)
-
-    order = [(z + d) % 4 for d in (0, 1, 3, 2)]
-    for k in (1, 2, 3):
-        for b in range(2):
-            gather_n.step(b, k)
-    here = c == target
-    for d, zs in enumerate(order):
-        for n, (_, dst) in enumerate(heads):
-            block = dst.at[aligned(zs, 2 * depth, 16), mine]
-            arrived(block, z_head.at[n, zs], here)
-            for r, o in enumerate(others):
-                copies.remote(block, block, xy_head.at[n, r, zs], o, s, here)
-    block = o_all.at[:, aligned(g, wide, 128)]
-    for j in range(2):
-        arrived(o_all.at[pl.ds(j * head, head), aligned(g, wide, 128)], z_out.at[j])
-    for r, o in enumerate(others):
-        copies.remote(block, block, xy_out.at[r], o, s)
-    for n, dst in enumerate((f_all, s_all)):
-        for zs in order:
-            block = dst.at[aligned(g, ff, 16), aligned(zs, 2 * depth, 128)]
-            arrived(block, z_ff.at[n, zs])
-            for r, o in enumerate(others):
-                copies.remote(block, block, xy_ff.at[n, r, zs], o, s)
-    for zs in order:
-        block = t_all.at[aligned(zs, ff, 16), aligned(g, wide, 128)]
-        arrived(block, z_ff.at[2, zs])
-        for r, o in enumerate(others):
-            copies.remote(block, block, xy_ff.at[2, r, zs], o, s)
-    for k in (1, 2, 3):
-        for b in range(2):
-            gather_d.step(b, k)
-
-    for b in range(2):
-        gather_n.finish(own.at[0, b], b)
-        gather_d.finish(own.at[1, b], b)
-    for r, o in enumerate(others):
-        from_here = (o // 2) == c
-        for zs in range(4):
-            for n, (_, dst) in enumerate(heads):
-                block = dst.at[pl.ds(zs * 2 * depth, 2 * depth), aligned(o % 2, head, head)]
-                arrived(block, xy_head.at[n, r, zs], from_here)
-        arrived(o_all.at[:, aligned(o, wide, 128)], xy_out.at[r])
-        for n, dst in enumerate((f_all, s_all)):
-            for zs in range(4):
-                arrived(dst.at[aligned(o, ff, 16), pl.ds(zs * 2 * depth, 2 * depth)], xy_ff.at[n, r, zs])
-        for zs in range(4):
-            arrived(t_all.at[pl.ds(zs * ff, ff), aligned(o, wide, 128)], xy_ff.at[2, r, zs])
-    copies.finish()
-
-
 class Scatter:
     def __init__(self, copies, part, rows, side, own, inbox, side_sem, own_sem, line_sem):
         self.copies, self.part, self.rows = copies, part, rows
@@ -563,60 +455,326 @@
     return jnp.mean(values * values, axis=-1, keepdims=True)
 
 
-def attention_out(
-    part, squares, x,
-    n2_all, h, branch, scale_all,
-    send, side, own, inbox, side_sem, own_sem, line_sem, n2, inbox_sq, scale, sq_sem, sc_sem, hop, hside, keep, x_v, x_sem,
-    column,
+def pour(read, write, count):
+    def piece(i, carry):
+        at = aligned(i, 16, 16)
+        write(at, read(at))
+        return carry
+
+    lax.fori_loop(0, count, piece, 0)
+
+
+class HalfScatter:
+    def __init__(self, copies, part, rows, side, inbox, side_sem, line_sem):
+        self.copies, self.part, self.rows = copies, part, rows
+        self.side, self.inbox, self.side_sem, self.line_sem = side, inbox, side_sem, line_sem
+        self.g, self.s, _, _, self.z, self.c = where_am_i()
+
+    def mine(self, k):
+        return self.part.at[aligned(2 * ((self.z + k) % 4) + self.c, self.rows, 16)]
+
+    def begin(self):
+        for k in (2, 1, 3, 0):
+            theirs = aligned(2 * ((self.z + k) % 4) + 1 - self.c, self.rows, 16)
+            self.copies.remote(
+                self.part.at[theirs], self.side.at[k], self.side_sem.at[k], self.g, self.s + 1 - 2 * self.c
+            )
+
+    def send(self):
+        for k in (2, 1, 3, 0):
+            arrived(self.side.at[k], self.side_sem.at[k])
+            if k == 0:
+                continue
+            own, side = self.mine(k), self.side.at[k]
+
+            def write(at, value):
+                own[at] = value.astype(jnp.bfloat16)
+
+            pour(lambda at: own[at].astype(jnp.float32) + side[at].astype(jnp.float32), write, self.rows // 16)
+            to = (self.z + k) % 4
+            self.copies.remote(own, self.inbox.at[k - 1], self.line_sem.at[k - 1], self.g, 2 * to + self.c)
+
+    def receive(self):
+        for k in range(3):
+            arrived(self.inbox.at[k], self.line_sem.at[k])
+
+    def total(self, at):
+        value = self.mine(0)[at].astype(jnp.float32) + self.side[0, at].astype(jnp.float32)
+        for k in range(3):
+            value = value + self.inbox[k, at].astype(jnp.float32)
+        return value
+
+
+def silu(values):
+    return values / (1.0 + jnp.exp(-values))
+
+
+def decay_table(rate, length):
+    offset = lax.broadcasted_iota(jnp.int32, (length, length), 0) - lax.broadcasted_iota(jnp.int32, (length, length), 1)
+    steps = jnp.maximum(offset, 0).astype(jnp.float32)
+    return jnp.where(offset >= 0, jnp.exp(-rate * steps), 0.0)
+
+
+def live_rows(first, count, length):
+    return ((first + lax.broadcasted_iota(jnp.int32, (count, 1), 0)) < length).astype(jnp.float32)
+
+
+def forward_part(
+    lengths, decay, x, cot, wq, wk, wv, wu, wo, w1, w2, w3,
+    n1_all, dm_all, n2_all, q_all, k_all, v_all, u_all, o_all, f_all, s_all, t_all, pre_all, h, branch, scale_all,
+    send, own, hop_n, side_n, hop_d, side_d, hop_m, side_m, z_head, z_out, z_ff, xy_head, xy_out, xy_ff,
+    n1, dm, n2, n1_v, w_v, wo_v, load, pre_v, pre_sem, part, side, inbox, side_sem, line_sem,
+    table, squares, inbox_sq, scale, sq_sem, sc_sem, column,
 ):
-    g, s, _, _, z, c = where_am_i()
-    greet(line_partners(g, s))
+    g, s, y, x_, z, c = where_am_i()
+    others = across(y, x_)
+    greet(line_partners(g, s) + [(o, s) for o in others])
     copies = Copies(send)
-    rows = x.shape[1]
-    width = x.shape[2]
-    scatter = Scatter(copies, part, rows, side, own, inbox, side_sem, own_sem, line_sem)
-    gather = Gather(copies, n2_all, rows, hop, hside)
-    scatter.begin()
-    everyone_on_line(copies, squares, inbox_sq, sq_sem, g, s, lambda to: squares.at[to])
-    local(squares.at[s], inbox_sq.at[s], sq_sem.at[7])
-    local(x, x_v, x_sem)
-    for k in (2, 1, 3, 0):
-        scatter.send(k)
-    for d in range(8):
-        arrived(inbox_sq.at[0], sq_sem.at[d])
-    total = inbox_sq[0]
-    for d in range(1, 8):
-        total = total + inbox_sq[d]
-    row = lax.rsqrt(total / width + EPS)
-    scale[...] = row
-    for d in range(1, 8):
-        to = (s + d) % 8
-        copies.remote(scale, scale_all.at[s], sc_sem.at[d - 1], g, to)
-    local(scale, scale_all.at[s], sc_sem.at[7])
-    column[...] = jnp.broadcast_to(row[:1], (2 * rows, 2 * rows)).T
-    arrived(x_v, x_sem)
-    scatter.receive()
-    for b in range(2):
+    rows, width = x.shape[1], x.shape[2]
+    length = 8 * rows
+    gather_n = Gather(copies, n1_all, rows, hop_n, side_n)
+    gather_d = Gather(copies, dm_all, rows, hop_d, side_d)
+    gather_m = Gather(copies, n2_all, rows, hop_m, side_m)
+    heads = list(zip((wq, wk, wv, wu), (q_all, k_all, v_all, u_all)))
+    depth, wide = wq.shape
+    head = q_all.shape[1] // 2
+    ff = f_all.shape[0] // 4
+    target = g // 2
+    mine = aligned(g % 2, head, head)
+    here = c == target
+    order = [(z + d) % 4 for d in (0, 1, 3, 2)]
+
+    def send_heads(n):
+        src, dst = heads[n]
+        for d in (2, 1, 3, 0):
+            to = (z + d) % 4
+            a, b = src.at[:, aligned(to, head, head)], dst.at[aligned(s, depth, 16), mine]
+            if d:
+                copies.remote(a, b, z_head.at[n, z], g, 2 * to + target)
+            else:
+                copies.remote(a, b, z_head.at[n, z], g, 2 * to + target, c != target)
+                local(a, b, z_head.at[n, z], here)
+
+    def pass_heads(n):
+        dst = heads[n][1]
+        for zs in order:
+            block = dst.at[aligned(zs, 2 * depth, 16), mine]
+            arrived(block, z_head.at[n, zs], here)
+            for r, o in enumerate(others):
+                copies.remote(block, block, xy_head.at[n, r, zs], o, s, here)
+
+    def send_out():
+        for i in range(2):
+            to = 2 * c + i
+            a = wo.at[pl.ds(i * head, head)]
+            b = o_all.at[aligned(z % 2, head, head), aligned(g, wide, 128)]
+            self_ = jnp.logical_and(to == z, c == z // 2)
+            copies.remote(a, b, z_out.at[z % 2], g, 2 * to + z // 2, jnp.logical_not(self_))
+            local(a, b, z_out.at[z % 2], self_)
+
+    def pass_out():
+        for j in range(2):
+            arrived(o_all.at[pl.ds(j * head, head), aligned(g, wide, 128)], z_out.at[j])
+        block = o_all.at[:, aligned(g, wide, 128)]
+        for r, o in enumerate(others):
+            copies.remote(block, block, xy_out.at[r], o, s)
+
+    def send_ff(n):
+        src, dst = ((w1, f_all), (w2, s_all))[n]
+        for d in (4, 3, 5, 2, 6, 1, 7, 0):
+            to = (s + d) % 8
+            a = src.at[aligned(to, ff, 16)]
+            b = dst.at[aligned(g, ff, 16), aligned(s, depth, 128)]
+            if d:
+                copies.remote(a, b, z_ff.at[n, z], g, to)
+            else:
+                local(a, b, z_ff.at[n, z])
+
+    def pass_ff(n):
+        dst = (f_all, s_all)[n]
+        for zs in order:
+            block = dst.at[aligned(g, ff, 16), aligned(zs, 2 * depth, 128)]
+            arrived(block, z_ff.at[n, zs])
+            for r, o in enumerate(others):
+                copies.remote(block, block, xy_ff.at[n, r, zs], o, s)
+
+    def send_third():
+        for d in (2, 1, 3, 0):
+            to = 4 * c + (s + d) % 4
+            a = w3.at[aligned(to % 4, ff, 16)]
+            b = t_all.at[aligned(z, ff, 16), aligned(g, wide, 128)]
+            if d:
+                copies.remote(a, b, z_ff.at[2, z], g, to)
+            else:
+                self_ = s // 4 == c
+                copies.remote(a, b, z_ff.at[2, z], g, to, jnp.logical_not(self_))
+                local(a, b, z_ff.at[2, z], self_)
+
+    def pass_third():
+        for zs in order:
+            block = t_all.at[aligned(zs, ff, 16), aligned(g, wide, 128)]
+            arrived(block, z_ff.at[2, zs])
+            for r, o in enumerate(others):
+                copies.remote(block, block, xy_ff.at[2, r, zs], o, s)
+
+    send_heads(0)
+    send_heads(1)
+    for b in range(2):
+
+        def norm(at):
+            v = x[b, at].astype(jnp.float32)
+            return v * lax.rsqrt(mean_square(v) + EPS)
+
+        def keep(at, value):
+            n1[b, at] = value.astype(jnp.bfloat16)
+
+        pour(norm, keep, rows // 16)
+        first = s * rows
+
+        def masked(i, carry):
+            at = aligned(i, 16, 16)
+            live = live_rows(first + i * 16, 16, lengths[b, 0])
+            dm[b, at] = (cot[b, at].astype(jnp.float32) * live).astype(jnp.bfloat16)
+            return carry
+
+        lax.fori_loop(0, rows // 16, masked, 0)
+    pass_heads(0)
+    send_heads(2)
+    pass_heads(1)
+    send_heads(3)
+    for b in range(2):
+        gather_n.begin(n1.at[b], own.at[0, b], b)
+    send_out()
+    pass_heads(2)
+    pass_heads(3)
+    gather_n.step(0, 1)
+    gather_n.step(1, 1)
+    pass_out()
+    gather_n.step(0, 2)
+    gather_n.step(1, 2)
+    send_ff(0)
+    gather_n.step(0, 3)
+    gather_n.step(1, 3)
+    for r, o in enumerate(others):
+        from_here = (o // 2) == c
+        for n, (_, dst) in enumerate(heads):
+            for zs in range(4):
+                block = dst.at[pl.ds(zs * 2 * depth, 2 * depth), aligned(o % 2, head, head)]
+                arrived(block, xy_head.at[n, r, zs], from_here)
+        arrived(o_all.at[:, aligned(o, wide, 128)], xy_out.at[r])
+    for n, (_, dst) in enumerate(heads):
+        local(dst, w_v.at[n], load.at[n])
+    local(o_all, wo_v, load.at[4])
+    for b in range(2):
+        gather_n.finish(own.at[0, b], b)
+        local(n1_all.at[b], n1_v.at[b], load.at[5 + b])
+    for j in range(2):
+        table[j] = decay_table(decay[4 * (2 * c + j) + z], length)
+    for n in range(4):
+        arrived(w_v.at[n], load.at[n])
+    arrived(wo_v, load.at[4])
+    scatters = []
+    for b in range(2):
+        arrived(n1_v.at[b], load.at[5 + b])
+        half = length // 2
+
+        def project(i, carry):
+            at = aligned(i, half, 16)
+            for n in range(4):
+                pre_v[n, b, at] = product(n1_v[b, at], w_v[n])
+            return carry
+
+        lax.fori_loop(0, 2, project, 0)
+        live = live_rows(0, length, lengths[b, 0])
+        for j in range(2):
+            lanes = pl.ds(j * head, head)
+            q = silu(pre_v[0, b, :, lanes]).astype(jnp.bfloat16)
+            k = (silu(pre_v[1, b, :, lanes]) * live).astype(jnp.bfloat16)
+            v = (silu(pre_v[2, b, :, lanes]) * live).astype(jnp.bfloat16)
+            scores = (product_right(q, k) * table[j]).astype(jnp.bfloat16)
+            pre_v[4, b, :, lanes] = product(scores, v)
+        gated = silu(pre_v[3, b]) * pre_v[4, b]
+        square = jnp.sum(gated * gated, axis=-1, keepdims=True)
+        row = jnp.broadcast_to(square, (length, 128)).T[:8]
+        for to in range(8):
+            squares[b, to, :, :rows] = row[:, to * rows : (to + 1) * rows]
+        low = gated.astype(jnp.bfloat16)
+
+        def out_part(i, carry):
+            at = aligned(i, 256, 256)
+            part[b, :, at] = product(low, wo_v[:, at]).astype(jnp.bfloat16)
+            return carry
+
+        lax.fori_loop(0, width // 256, out_part, 0)
+        scatter = HalfScatter(copies, part.at[b], rows, side.at[b], inbox.at[b], side_sem.at[b], line_sem.at[b])
+        scatter.begin()
+        everyone_on_line(copies, squares, inbox_sq.at[b], sq_sem.at[b], g, s, lambda to: squares.at[b, to])
+        local(squares.at[b, s], inbox_sq.at[b, s], sq_sem.at[b, 7])
+        scatter.send()
+        scatters.append(scatter)
+    local(pre_v, pre_all, pre_sem)
+    pass_ff(0)
+    for b in range(2):
+        for d in range(8):
+            arrived(inbox_sq.at[b, 0], sq_sem.at[b, d])
+        total = inbox_sq[b, 0]
+        for d in range(1, 8):
+            total = total + inbox_sq[b, d]
+        row = lax.rsqrt(total / width + EPS)
+        scale[b] = row
+        for d in range(1, 8):
+            copies.remote(scale.at[b], scale_all.at[b, s], sc_sem.at[b, d - 1], g, (s + d) % 8)
+        local(scale.at[b], scale_all.at[b, s], sc_sem.at[b, 7])
+        column[b] = jnp.broadcast_to(row[:1], (128, 128)).T
+    for b in range(2):
+        scatter = scatters[b]
+        scatter.receive()
+        if b == 0:
+            send_ff(1)
+        else:
+            send_third()
 
         def finish(i, carry):
             piece = aligned(i, 16, 16)
             at = aligned(b * (rows // 16) + i, 16, 16)
-            a = scatter.total(b, piece) * column[at, :1]
-            hidden = x_v[b, piece].astype(jnp.float32) + a
+            a = scatter.total(piece) * column[b, piece, :1]
+            hidden = x[b, piece].astype(jnp.float32) + a
             branch[at] = a
             h[at] = hidden
             n2[b, piece] = (hidden * lax.rsqrt(mean_square(hidden) + EPS)).astype(jnp.bfloat16)
             return carry
 
         lax.fori_loop(0, rows // 16, finish, 0)
-        gather.begin(n2.at[b], keep.at[b], b)
-    for k in (1, 2, 3):
+        gather_m.begin(n2.at[b], own.at[2, b], b)
+    for b in range(2):
+        gather_d.begin(dm.at[b], own.at[1, b], b)
+    gather_m.step(0, 1)
+    gather_m.step(1, 1)
+    pass_ff(1)
+    gather_m.step(0, 2)
+    gather_m.step(1, 2)
+    gather_d.step(0, 1)
+    gather_d.step(1, 1)
+    pass_third()
+    gather_m.step(0, 3)
+    gather_m.step(1, 3)
+    for k in (2, 3):
         for b in range(2):
-            gather.step(b, k)
-    for b in range(2):
-        gather.finish(keep.at[b], b)
-    for d in range(8):
-        arrived(scale, sc_sem.at[d])
+            gather_d.step(b, k)
+
+    for b in range(2):
+        gather_d.finish(own.at[1, b], b)
+        gather_m.finish(own.at[2, b], b)
+    for r, o in enumerate(others):
+        for n, dst in enumerate((f_all, s_all)):
+            for zs in range(4):
+                arrived(dst.at[aligned(o, ff, 16), pl.ds(zs * 2 * depth, 2 * depth)], xy_ff.at[n, r, zs])
+        for zs in range(4):
+            arrived(t_all.at[pl.ds(zs * ff, ff), aligned(o, wide, 128)], xy_ff.at[2, r, zs])
+    for b in range(2):
+        for d in range(8):
+            arrived(scale.at[b], sc_sem.at[b, d])
+    arrived(pre_v, pre_sem)
     copies.finish()
 
 
@@ -885,24 +1043,33 @@
     mine = (slots[None] < lengths[:, :1]).astype(f32).reshape(2 * rows, 1)
     live = (jnp.arange(length)[None] < lengths[:, :1]).astype(f32).reshape(2 * length, 1)
     dy = cotangent[:, 0].astype(f32).reshape(2 * rows, width) * mine
-    n1 = norm_rows(x).astype(bf16).reshape(2, rows, width)
-    dm = dy.astype(bf16).reshape(2, rows, width)
-
-    n1_all, dm_all, q_w, k_w, v_w, u_w, o_w, f_w, s_w, t_w = call(
-        distribute,
+    in_smem = pl.BlockSpec(memory_space=pltpu.SMEM)
+
+    (n1_all, dm_all, n2_all, q_w, k_w, v_w, u_w, o_w, f_w, s_w, t_w, pre_all, h, branch, scale_all) = call(
+        forward_part,
         0,
-        [(v, ANY) for v in (n1, dm, w_query, w_key, w_value, w_gate, w_out, w_first.T, w_second.T, w_third)],
-        [(low_array(2, length, width), ANY)] * 2
+        [(lengths, in_smem), (decay_rate, in_smem), (x_low, VMEM), (cotangent[:, 0], VMEM)]
+        + [(v, ANY) for v in (w_query, w_key, w_value, w_gate, w_out, w_first.T, w_second.T, w_third)],
+        [(low_array(2, length, width), ANY)] * 3
         + [(low_array(width, 2 * head), ANY)] * 4
         + [(low_array(2 * head, width), ANY)]
-        + [(low_array(hidden, width), ANY)] * 3,
-        [dma(200), dma(2, 2), dma(2, 2, 3), dma(2, 7), dma(2, 2, 3), dma(2, 7),
-         dma(4, 4), dma(2), dma(3, 4), dma(4, 3, 4), dma(3), dma(3, 3, 4)],
-        "distribute",
+        + [(low_array(hidden, width), ANY)] * 3
+        + [(wide_array(5, 2, length, 2 * head), ANY), (wide_array(2 * rows, width), VMEM), (wide_array(2 * rows, width), VMEM),
+           (wide_array(2, 8, 8, 128), ANY)],
+        [dma(260), dma(3, 2), dma(2, 2, 3), dma(2, 7), dma(2, 2, 3), dma(2, 7), dma(2, 2, 3), dma(2, 7),
+         dma(4, 4), dma(2), dma(3, 4), dma(4, 3, 4), dma(3), dma(3, 3, 4),
+         pltpu.VMEM((2, rows, width), bf16), pltpu.VMEM((2, rows, width), bf16), pltpu.VMEM((2, rows, width), bf16),
+         pltpu.VMEM((2, length, width), bf16), pltpu.VMEM((4, width, 2 * head), bf16), pltpu.VMEM((2 * head, width), bf16), dma(7),
+         pltpu.VMEM((5, 2, length, 2 * head), f32), dma(),
+         pltpu.VMEM((2, length, width), bf16), pltpu.VMEM((2, 4, rows, width), bf16), pltpu.VMEM((2, 3, rows, width), bf16),
+         dma(2, 4), dma(2, 3),
+         pltpu.VMEM((2, length, length), f32), pltpu.VMEM((2, 8, 8, 128), f32), pltpu.VMEM((2, 8, 8, 128), f32),
+         pltpu.VMEM((2, 8, 128), f32), dma(2, 8), dma(2, 8), pltpu.VMEM((2, 128, 128), f32)],
+        "forward_part",
     )
     n1_all = n1_all.reshape(2 * length, width)
     dm_all = dm_all.reshape(2 * length, width)
-    q_pre, k_pre, v_pre, u_pre = [product(n1_all, w) for w in (q_w, k_w, v_w, u_w)]
+    q_pre, k_pre, v_pre, u_pre, o = [pre_all[n].reshape(2 * length, 2 * head) for n in range(5)]
 
     def split(values):
         return values.reshape(2, length, 2, head)
@@ -916,25 +1083,8 @@
     offset = places[:, None] - places[None, :]
     weight = jnp.where(offset >= 0, jnp.exp(-rates[:, None, None] * jnp.maximum(offset, 0.0)), 0.0)
     scores = (jnp.einsum("bihd,bjhd->bhij", q, k, preferred_element_type=f32) * weight).astype(bf16)
-    o = jnp.einsum("bhij,bjhe->bihe", scores, v, preferred_element_type=f32).reshape(2 * length, 2 * head)
     u = jax.nn.silu(u_pre)
     g = u * o
-    squares = jnp.sum(g * g, axis=-1).reshape(2, 8, rows).transpose(1, 0, 2).reshape(8, 1, 2 * rows)
-    squares = jnp.broadcast_to(squares, (8, 8, 2 * rows))
-    part = product(g.astype(bf16), o_w).astype(bf16).reshape(2, length, width)
-
-    n2_all, h, branch, scale_all = call(
-        attention_out,
-        1,
-        [(part, ANY), (squares, ANY), (x_low, ANY)],
-        [(low_array(2, length, width), ANY), (wide_array(2 * rows, width), VMEM), (wide_array(2 * rows, width), VMEM),
-         (wide_array(8, 8, 2 * rows), ANY)],
-        [dma(80)] + scatter_scratch(rows, width)
-        + [pltpu.VMEM((2, rows, width), bf16), pltpu.VMEM((8, 8, 2 * rows), f32), pltpu.VMEM((8, 2 * rows), f32), dma(8), dma(8),
-           dma(2, 2, 3), dma(2, 7), dma(2), pltpu.VMEM((2, rows, width), bf16), dma(),
-           pltpu.VMEM((2 * rows, 2 * rows), f32)],
-        "attention_out",
-    )
 
     def per_token(values):
         return values[:, 0].reshape(8, 2, rows).transpose(1, 0, 2).reshape(2 * length, 1)
@@ -964,7 +1114,7 @@
         "ffn_back",
     )
     da_all = da_all.reshape(2 * length, width)
-    inverse = per_token(scale_all)
+    inverse = scale_all[:, :, 0, :rows].reshape(2 * length, 1)
     mix = per_token(mix_all)
     nat = g * inverse
     go = product_left(nat.astype(bf16), da_all).astype(bf16)

time: 822 us -> 684 us (0.83)
  Pallas kernels: 649 us -> 531 us
  matrix products: 109 us -> 94.4 us
    pallas_call x4 -> x3, Pallas kernels: 649 us -> 531 us  [call(): pl.pallas_call(kernel, out_shape=[shape for shape, _ in outs], in_specs=[...]
    dot_general x8 -> x3, matrix products: 32.5 us -> 13.7 us  [product(): return jnp.dot(left, right, preferred_element_type=jnp.float32)]
    dot_general x8, matrix products: 44.7 us -> 35 us  [product_right(): lax.dot_general(left, right, (((1,), (1,)), ((), ())), preferred_element_...]
    dot_general x8, matrix products: 24.6 us -> 33.7 us  [product_left(): lax.dot_general(left, right, (((0,), (0,)), ((), ())), preferred_element_...]
    unnamed x110 -> x97, local copies, waits for them, and re-layouts: 16.7 us -> 10.4 us
where the time goes in v2:
time: 684 us; the launch traced here: 678 us
  Pallas kernels  531 us (78%)
  matrix products  94.4 us (14%)
  local copies, waits for them, and re-layouts  29.4 us (4%)
  other arithmetic  21.5 us (3%)
    pallas_call x3, Pallas kernels, call(): pl.pallas_call(kernel, out_shape=[shape for shape, _ in outs], in_specs=[...  531 us
    dot_general x8, matrix products, product_right(): lax.dot_general(left, right, (((1,), (1,)), ((), ())), preferred_element_...  35 us
    dot_general x8, matrix products, product_left(): lax.dot_general(left, right, (((0,), (0,)), ((), ())), preferred_element_...  33.7 us
    dot_general x3, matrix products, product(): return jnp.dot(left, right, preferred_element_type=jnp.float32)  13.7 us

profile of v2, /device:TPU:0, one launch (start us, length us, event | category | flops | bytes accessed | tf_op | source)
XLA Modules:
  0.0 677.5 jit_solution(9298659627636293952)
XLA Ops:
  0.7 0.8 compare_convert_fusion.1
  1.5 0.6 reshape.298
  2.1 0.7 copy.46.lengths
  2.8 1.2 fusion.9
  4.1 0.7 add.198
  4.7 1.3 gather_fusion
  6.0 0.7 compare_convert_fusion
  6.8 0.2 subtract_compare_fusion
  7.0 1.4 copy.44
  8.4 0.3 copy.45
  9.0 1.7 exponential_select_fusion
  10.9 227.6 %forward_part.1 = (bf16[2,512,2048]{2,1,0:T(8,128)(2,1)}, bf16[2,512,2048]{2,1,0:T(8,128)(2,1)}, bf16[2,512,2048]{2,1,0:T(8,128)(2,1)}, bf16[2048,256]{1,0:T(8,1...) custom-call(s32[2,1]{1,0:T(2,128)S(1)} %copy.46.lengths, ...), custom_call_target="tpu_custom_call" | custom-call | tf_op jit(solution)/shard_map/forward_part/pallas_call | solution.py:992
  238.5 1.0 copy-done.3
  239.7 4.8 multiply_convert_fusion.5
  244.5 1.3 copy.73
  245.8 2.5 copy.72
  248.3 2.6 copy.71
  251.0 6.5 fusion.56
  257.5 3.2 fusion.57
  260.7 3.3 multiply_convert_fusion.2
  264.1 4.5 convolution_convert_fusion.1.gt
  268.7 5.1 convolution_convert_fusion
  273.8 4.5 convolution_convert_fusion.3.gf
  278.3 4.6 convolution_convert_fusion.2.gs
  282.9 3.5 fusion.58
  286.5 5.1 add_convert_fusion.1
  291.5 143.5 %ffn_back.1 = (bf16[2,512,2048]{2,1,0:T(8,128)(2,1)}, f32[128,2048]{1,0:T(8,128)S(1)}, bf16[128,2048]{1,0:T(8,128)(2,1)S(1)}, f32[8,8,128]{2,1,0:T(8,128)S(1)}) custom-call(bf16[2,512,2048]{2,1,0:T(8,128)(2,1)} %bitcast.230, bf16[2,512,2048]{2,1,0:T(8,128)(2,1)} %bitcast.229, f32[128,2048]{1,0:T(8,128)S(1)} %convert_multiply_fusion.dy, ...), custom_call_target="tpu_custom_call" | custom-call | tf_op jit(solution)/shard_map/ffn_back/pallas_call | solution.py:992
  435.0 0.8 copy-done.10
  436.0 4.6 convolution_convert_fusion.4.go
  440.6 0.3 fusion.27
  441.0 0.9 copy-done.42
  441.8 2.4 fusion.29
  444.4 0.6 copy.58
  445.0 4.8 convolution_convert_fusion.5
  449.8 0.8 multiply_convert_fusion.1
  450.6 1.3 copy-done.22
  451.9 1.5 convolution_bitcast_fusion
  453.4 5.4 multiply_convert_fusion.6
  458.8 4.3 multiply_convert_fusion.8
  463.1 2.1 copy.61
  465.2 1.3 copy.57
  466.5 0.4 copy.65
  466.9 4.6 convolution_convert_fusion.6
  471.4 0.4 copy.63
  471.9 4.7 convolution_convert_fusion.7
  476.5 1.4 convolution_convert_fusion.8
  477.9 2.2 copy.59
  480.2 2.5 copy.54
  482.7 4.1 fusion.7
  486.8 1.3 fusion.60
  488.1 4.6 fusion.61
  492.8 4.5 fusion.59
  497.3 9.1 %add_convert_fusion = bf16[1024,2048]{1,0:T(8,128)(2,1)} fusion(f32[1024,2048]{1,0:T(8,128)} %fusion.61, f32[1024,2048]{1,0:T(8,128)} %fusion.59, f32[1024,2048]{1,0:T(8,128)S(1)} %fusion.60, bf16[1024,256]{1,0:T(8,128)(2,1)S(1)} %copy-done.29, bf16[2048,256]{1,0:T(8,128)(2,1)S(1)} %copy-done.27), kind=kOutput, calls=%fused_computation.1 | convolution fusion | flops 1082130432 | bytes 30932992 | tf_op jit(solution)/shard_map/dot_general | solution.py:57
  506.5 159.7 %gradients.1 = (f32[128,2048]{1,0:T(8,128)S(1)}, bf16[256,512]{1,0:T(8,128)(2,1)S(1)}, bf16[256,512]{1,0:T(8,128)(2,1)S(1)}, bf16[256,512]{1,0:T(8,128)(2,1)S(1)...) custom-call(bf16[2,512,2048]{2,1,0:T(8,128)(2,1)} %bitcast.223, ...), custom_call_target="tpu_custom_call" | custom-call | tf_op jit(solution)/shard_map/gradients/pallas_call | solution.py:992
  666.3 1.2 fusion.3
  667.6 0.9 convert_element_type.235
  668.4 0.9 convert_element_type.236
  669.3 0.9 convert_element_type.237
  670.1 0.9 convert_element_type.238
  671.0 0.9 convert_element_type.239
  672.0 1.5 copy.68
  673.6 1.5 copy.69
  675.2 1.3 convert_element_type.244
  676.5 0.8 copy.99
  (107 shorter events, 1.4 us)
Async XLA Ops:
  0.6 7.8 %copy-start.28 = (bf16[256,1408]{1,0:T(8,128)(2,1)S(1)}, bf16[256,1408]{1,0:T(8,128)(2,1)}, u32[]{:S(2)}) copy-start(bf16[256,1408]{1,0:T(8,128)(2,1)} %param.22) | copy-start | bytes 2162692
  8.4 2.3 copy-start.2
  8.7 2.0 copy-start.33
  8.7 2.1 copy-start
  8.7 2.1 copy-start.1
  8.7 2.1 copy-start.9
  8.7 2.1 copy-start.12
  8.8 2.1 copy-start.13
  8.8 2.1 copy-start.14
  8.8 2.1 copy-start.15
  8.8 2.1 copy-start.16
  238.5 1.0 copy-start.3
  244.5 13.0 %copy-start.18 = (f32[1,2,512,256]{3,2,1,0:T(8,128)}, f32[1,2,512,256]{3,2,1,0:T(8,128)S(1)}, u32[]{:S(2)}) copy-start(f32[1,2,512,256]{3,2,1,0:T(8,128)S(1)} %get-tuple-element.87) | copy-start | bytes 3145732
  251.0 6.5 copy-start.36
  251.0 6.6 copy-start.39
  257.5 3.2 copy-start.40
  260.7 3.4 copy-start.37
  264.1 9.7 %copy-start.43 = (bf16[1024,704]{0,1:T(8,128)(2,1)}, bf16[1024,704]{0,1:T(8,128)(2,1)S(1)}, u32[]{:S(2)}) copy-start(bf16[1024,704]{0,1:T(8,128)(2,1)S(1)} %get-tuple-element.93) | copy-start | bytes 4325380
  264.1 4.6 copy-start.41
  278.3 4.6 copy-start.44
  286.4 5.1 copy-start.5
  286.4 5.1 copy-start.6
  435.0 0.8 copy-start.10
  436.0 4.6 copy-start.19
  436.0 4.6 copy-start.20
  436.0 5.0 copy-start.38
  440.6 1.2 copy-start.42
  445.0 4.8 copy-start.17
  445.0 4.8 copy-start.21
  449.8 2.1 copy-start.25
  450.6 1.3 copy-start.22
  458.8 6.3 copy-start.26
  463.1 3.4 copy-start.31
  466.9 4.6 copy-start.30
  471.9 4.7 copy-start.32
  471.9 4.7 copy-start.35
  482.7 4.2 copy-start.24
  486.8 1.3 copy-start.23
  488.1 4.6 copy-start.4
  492.8 4.5 copy-start.27
  492.8 4.5 copy-start.29
  506.4 159.9 %copy-start.34 = (f32[128]{0:T(128)S(1)}, f32[128]{0:T(128)}, u32[]{:S(2)}) copy-start(f32[128]{0:T(128)} %add.198) | copy-start | bytes 1540
  666.1 2.3 copy-start.7
  671.0 2.5 copy-start.8
  673.6 2.9 copy-start.11

commit v3 on v2

--- a/solution.py
+++ b/solution.py
@@ -284,6 +284,7 @@
         self.pending = []
 
     def remote(self, src, dst, recv_sem, group, place, when=None):
+        assert self.used < self.sems.shape[0]
         copy = pltpu.make_async_remote_copy(
             src_ref=src,
             dst_ref=dst,
@@ -398,53 +399,6 @@
     return [(g, (s + d) % 8) for d in range(1, 8)]
 
 
-class Scatter:
-    def __init__(self, copies, part, rows, side, own, inbox, side_sem, own_sem, line_sem):
-        self.copies, self.part, self.rows = copies, part, rows
-        self.side, self.own, self.inbox = side, own, inbox
-        self.side_sem, self.own_sem, self.line_sem = side_sem, own_sem, line_sem
-        self.g, self.s, _, _, self.z, self.c = where_am_i()
-
-    def begin(self):
-        g, s, z, c = self.g, self.s, self.z, self.c
-        for k in (2, 1, 3, 0):
-            to = (z + k) % 4
-            theirs = aligned(2 * to + 1 - c, self.rows, 16)
-            mine = aligned(2 * to + c, self.rows, 16)
-            self.copies.remote(
-                self.part.at[:, theirs], self.side.at[k], self.side_sem.at[k], g, s + 1 - 2 * c
-            )
-            local(self.part.at[:, mine], self.own.at[k], self.own_sem.at[k])
-
-    def send(self, k):
-        arrived(self.side.at[k], self.side_sem.at[k])
-        arrived(self.own.at[k], self.own_sem.at[k])
-        if k == 0:
-            return
-        own, side = self.own.at[k], self.side.at[k]
-
-        def add(i, carry):
-            piece = aligned(i, 16, 16)
-            for b in range(2):
-                both = own[b, piece].astype(jnp.float32) + side[b, piece].astype(jnp.float32)
-                own[b, piece] = both.astype(jnp.bfloat16)
-            return carry
-
-        lax.fori_loop(0, self.rows // 16, add, 0)
-        to = (self.z + k) % 4
-        self.copies.remote(own, self.inbox.at[k - 1], self.line_sem.at[k - 1], self.g, 2 * to + self.c)
-
-    def receive(self):
-        for k in range(3):
-            arrived(self.inbox.at[k], self.line_sem.at[k])
-
-    def total(self, b, piece):
-        value = self.own[0, b, piece].astype(jnp.float32) + self.side[0, b, piece].astype(jnp.float32)
-        for k in range(3):
-            value = value + self.inbox[k, b, piece].astype(jnp.float32)
-        return value
-
-
 def everyone_on_line(copies, src, dst, sem, g, s, to_rows):
     for d in range(1, 8):
         to = (s + d) % 8
@@ -464,45 +418,70 @@
     lax.fori_loop(0, count, piece, 0)
 
 
-class HalfScatter:
+class LineScatter:
     def __init__(self, copies, part, rows, side, inbox, side_sem, line_sem):
         self.copies, self.part, self.rows = copies, part, rows
         self.side, self.inbox, self.side_sem, self.line_sem = side, inbox, side_sem, line_sem
         self.g, self.s, _, _, self.z, self.c = where_am_i()
 
-    def mine(self, k):
-        return self.part.at[aligned(2 * ((self.z + k) % 4) + self.c, self.rows, 16)]
+    def mine(self, chip):
+        return self.part.at[aligned(2 * chip + self.c, self.rows, 16)]
 
     def begin(self):
-        for k in (2, 1, 3, 0):
-            theirs = aligned(2 * ((self.z + k) % 4) + 1 - self.c, self.rows, 16)
+        for chip in (3, 0, 2, 1):
+            theirs = aligned(2 * chip + 1 - self.c, self.rows, 16)
             self.copies.remote(
-                self.part.at[theirs], self.side.at[k], self.side_sem.at[k], self.g, self.s + 1 - 2 * self.c
+                self.part.at[theirs], self.side.at[chip], self.side_sem.at[chip], self.g, self.s + 1 - 2 * self.c
             )
 
-    def send(self):
-        for k in (2, 1, 3, 0):
-            arrived(self.side.at[k], self.side_sem.at[k])
-            if k == 0:
-                continue
-            own, side = self.mine(k), self.side.at[k]
-
-            def write(at, value):
-                own[at] = value.astype(jnp.bfloat16)
-
-            pour(lambda at: own[at].astype(jnp.float32) + side[at].astype(jnp.float32), write, self.rows // 16)
-            to = (self.z + k) % 4
-            self.copies.remote(own, self.inbox.at[k - 1], self.line_sem.at[k - 1], self.g, 2 * to + self.c)
+    def pass_on(self, chip, way, edge):
+        z = self.z
+        slot = chip - 1 if way == 0 else chip
+        own, side, come = self.mine(chip), self.side.at[chip], self.inbox.at[way, slot]
+        before = (z < chip) if way == 0 else (z > chip)
+        first = (z == 0) if way == 0 else (z == 3)
+        go = jnp.logical_and(before, first if edge else jnp.logical_not(first))
+
+        def write(at, value):
+            own[at] = value.astype(jnp.bfloat16)
+
+        def two(at):
+            return own[at].astype(jnp.float32) + side[at].astype(jnp.float32)
+
+        @pl.when(go)
+        def _():
+            arrived(side, self.side_sem.at[chip])
+            if edge:
+                pour(two, write, self.rows // 16)
+            else:
+                arrived(come, self.line_sem.at[way, slot])
+                pour(lambda at: two(at) + come[at].astype(jnp.float32), write, self.rows // 16)
+
+        to = (self.s + 2) % 8 if way == 0 else (self.s + 6) % 8
+        self.copies.remote(own, come, self.line_sem.at[way, slot], self.g, to, go)
+
+    def ends(self):
+        for i in range(3):
+            self.pass_on(3 - i, 0, True)
+            self.pass_on(i, 1, True)
+
+    def hop(self, i):
+        self.pass_on(3 - i, 0, False)
+        self.pass_on(i, 1, False)
 
     def receive(self):
-        for k in range(3):
-            arrived(self.inbox.at[k], self.line_sem.at[k])
+        z = self.z
+        arrived(self.side.at[z], self.side_sem.at[z])
+        left, right = jnp.maximum(z - 1, 0), jnp.minimum(z, 2)
+        arrived(self.inbox.at[0, left], self.line_sem.at[0, left], z > 0)
+        arrived(self.inbox.at[1, right], self.line_sem.at[1, right], z < 3)
 
     def total(self, at):
-        value = self.mine(0)[at].astype(jnp.float32) + self.side[0, at].astype(jnp.float32)
-        for k in range(3):
-            value = value + self.inbox[k, at].astype(jnp.float32)
-        return value
+        z = self.z
+        value = self.mine(z)[at].astype(jnp.float32) + self.side[z, at].astype(jnp.float32)
+        from_left = self.inbox[0, jnp.maximum(z - 1, 0), at].astype(jnp.float32)
+        from_right = self.inbox[1, jnp.minimum(z, 2), at].astype(jnp.float32)
+        return value + jnp.where(z > 0, from_left, 0.0) + jnp.where(z < 3, from_right, 0.0)
 
 
 def silu(values):
@@ -521,7 +500,7 @@
 
 def forward_part(
     lengths, decay, x, cot, wq, wk, wv, wu, wo, w1, w2, w3,
-    n1_all, dm_all, n2_all, q_all, k_all, v_all, u_all, o_all, f_all, s_all, t_all, pre_all, h, branch, scale_all,
+    n1_all, dm_all, n2_all, q_all, k_all, v_all, u_all, o_all, f_all, s_all, t_all, pre_all, h, scale_all,
     send, own, hop_n, side_n, hop_d, side_d, hop_m, side_m, z_head, z_out, z_ff, xy_head, xy_out, xy_ff,
     n1, dm, n2, n1_v, w_v, wo_v, load, pre_v, pre_sem, part, side, inbox, side_sem, line_sem,
     table, squares, inbox_sq, scale, sq_sem, sc_sem, column,
@@ -706,13 +685,19 @@
             return carry
 
         lax.fori_loop(0, width // 256, out_part, 0)
-        scatter = HalfScatter(copies, part.at[b], rows, side.at[b], inbox.at[b], side_sem.at[b], line_sem.at[b])
+        scatter = LineScatter(copies, part.at[b], rows, side.at[b], inbox.at[b], side_sem.at[b], line_sem.at[b])
         scatter.begin()
+        scatter.ends()
         everyone_on_line(copies, squares, inbox_sq.at[b], sq_sem.at[b], g, s, lambda to: squares.at[b, to])
         local(squares.at[b, s], inbox_sq.at[b, s], sq_sem.at[b, 7])
-        scatter.send()
         scatters.append(scatter)
     local(pre_v, pre_all, pre_sem)
+    scatters[0].hop(0)
+    scatters[0].hop(1)
+    scatters[1].hop(0)
+    scatters[0].hop(2)
+    scatters[1].hop(1)
+    scatters[1].hop(2)
     pass_ff(0)
     for b in range(2):
         for d in range(8):
@@ -739,7 +724,6 @@
             at = aligned(b * (rows // 16) + i, 16, 16)
             a = scatter.total(piece) * column[b, piece, :1]
             hidden = x[b, piece].astype(jnp.float32) + a
-            branch[at] = a
             h[at] = hidden
             n2[b, piece] = (hidden * lax.rsqrt(mean_square(hidden) + EPS)).astype(jnp.bfloat16)
             return carry
@@ -778,214 +762,449 @@
     copies.finish()
 
 
-def ffn_back(
-    part, part_m, dy, h, branch,
-    da_all, dh, out, mix_all,
-    send, side, own, inbox, side_sem, own_sem, line_sem,
-    side_m, own_m, inbox_m, side_sem_m, own_sem_m, line_sem_m,
-    da, mix, mix_sem, hop, hside, keep, column,
+def slope(values):
+    sigma = 1.0 / (1.0 + jnp.exp(-values))
+    return sigma * (1.0 + values * (1.0 - sigma))
+
+
+def turned_table(rate, length):
+    offset = lax.broadcasted_iota(jnp.int32, (length, length), 1) - lax.broadcasted_iota(jnp.int32, (length, length), 0)
+    steps = jnp.maximum(offset, 0).astype(jnp.float32)
+    return jnp.where(offset >= 0, jnp.exp(-rate * steps), 0.0)
+
+
+def columns_of(out, tiles, b, rows):
+    for owner in range(8):
+        out[pl.ds(owner * rows, rows)] = jnp.broadcast_to(tiles[b, owner, :1], (128, 128)).T[:rows]
+
+
+def turn(dst, read, count, columns):
+    def block(i, carry):
+        dst[pl.ds(0, columns), aligned(i, 128, 128)] = read(aligned(i, 128, 128)).T
+        return carry
+
+    lax.fori_loop(0, count, block, 0)
+
+
+def tiles_of(width, body):
+    def tile(i, carry):
+        body(aligned(i, 256, 256), i)
+        return carry
+
+    lax.fori_loop(0, width // 256, tile, 0)
+
+
+def backward_part(
+    lengths, decay, x, cot, h, n1_all, dm_all, n2_all, q_all, k_all, v_all, u_all, o_all, f_all, s_all, t_all, pre_all, scale_all,
+    da_all, mix_all, out, grad_x, fq, fk, fv, fu, fo, ff_, fs, ft, in_f, in_t, in_o, in_h,
+    send_a, send_b, send_c, send_d, load, own, hop, hside,
+    a_v, b_v, w_v, wa_v, wo_v, p_v, turned, part, side, inbox, side_sem, line_sem, side_m, inbox_m, side_sem_m, line_sem_m,
+    scale, mix, mix_in, mix_sem, column, inverse, mixed, da, table, pre, dz, nat_v, go_v, grads_h,
+    xy_f, xy_t, xy_o, xy_h, z_f, z_t, z_o, z_h,
 ):
-    g, s, _, _, z, c = where_am_i()
-    greet(line_partners(g, s))
-    copies = Copies(send)
-    rows = part.shape[1] // 8
-    width = part.shape[2]
-    scatter = Scatter(copies, part, rows, side, own, inbox, side_sem, own_sem, line_sem)
-    scatter_m = Scatter(copies, part_m, rows, side_m, own_m, inbox_m, side_sem_m, own_sem_m, line_sem_m)
-    gather = Gather(copies, da_all, rows, hop, hside)
-    scatter.begin()
-    for k in (2, 1, 3, 0):
-        scatter.send(k)
-    scatter_m.begin()
-    scatter.receive()
-    for b in range(2):
+    g, s, y, x_, z, c = where_am_i()
+    others = across(y, x_)
+    plane = [(o, 2 * z + e) for o in others for e in range(2)]
+    rows, width = x.shape[1], x.shape[2]
+    length = 8 * rows
+    tokens = 2 * length
+    ff = in_f.shape[2]
+    hidden = 4 * ff
+    head = dz.shape[2] // 2
+    wide, depth = fo.shape[1], fo.shape[0]
+
+    def at_b(b):
+        return pl.ds(b * length, length)
+
+    for b in range(2):
+        local(n2_all.at[b], a_v.at[at_b(b)], load.at[b])
+        local(dm_all.at[b], b_v.at[at_b(b)], load.at[2 + b])
+    for n, src in enumerate((f_all, s_all, t_all)):
+        local(src, w_v.at[pl.ds(n * hidden, hidden)], load.at[4 + n])
+    for n, src in enumerate((q_all, k_all, v_all, u_all)):
+        local(src, wa_v.at[n], load.at[7 + n])
+    local(o_all, wo_v, load.at[11])
+    local(scale_all, scale, load.at[12])
+    greet(line_partners(g, s) + plane)
+    sums = Copies(send_a)
+    bulk = Copies(send_b)
+    last = Copies(send_c)
+    early = Copies(send_d)
+    gather = Gather(last, da_all, rows, hop, hside)
+    w1 = w_v.at[pl.ds(0, hidden)]
+    w2 = w_v.at[pl.ds(hidden, hidden)]
+    w3 = w_v.at[pl.ds(2 * hidden, hidden)]
+
+    def feed_forward(b):
+        def tile(i, carry):
+            at = aligned(b * 2 + i, length // 2, 16)
+            first = product_right(a_v[at], w1[...])
+            second = product_right(a_v[at], w2[...])
+            back = product_right(b_v[at], w3[...])
+            p_v[0, at] = (back * second).astype(jnp.bfloat16)
+            p_v[1, at] = (back * first).astype(jnp.bfloat16)
+            p_v[2, at] = (first * second).astype(jnp.bfloat16)
+            return carry
+
+        lax.fori_loop(0, 2, tile, 0)
+
+    def norm_part(b):
+        def body(at, i):
+            value = product(p_v[0, at_b(b)], w1[:, at]) + product(p_v[1, at_b(b)], w2[:, at])
+            part[b, :, at] = value.astype(jnp.bfloat16)
+
+        tiles_of(width, body)
+
+    def scatter_of(b, copies):
+        return LineScatter(copies, part.at[b], rows, side.at[b], inbox.at[b], side_sem.at[b], line_sem.at[b])
+
+    def scatter_m_of(b, copies):
+        return LineScatter(copies, part.at[b], rows, side_m.at[b], inbox_m.at[b], side_sem_m.at[b], line_sem_m.at[b])
+
+    second = [scatter_of(b, early) for b in range(2)]
+    for n in (0, 4, 5, 2, 6):
+        ref = {0: a_v.at[at_b(0)], 2: b_v.at[at_b(0)], 4: w1, 5: w2, 6: w3}[n]
+        arrived(ref, load.at[n])
+    feed_forward(0)
+    norm_part(0)
+    second[0].begin()
+    second[0].ends()
+    arrived(a_v.at[at_b(1)], load.at[1])
+    arrived(b_v.at[at_b(1)], load.at[3])
+    feed_forward(1)
+    second[0].hop(0)
+    norm_part(1)
+    second[1].begin()
+    second[1].ends()
+    second[0].hop(1)
+    second[0].hop(2)
+
+    def weight_part(n, operand):
+        turn(turned, lambda t: p_v[n, t], tokens // 128, hidden)
+
+        def body(at, i):
+            w_v[pl.ds(n * hidden, hidden), at] = product(turned[...], operand[:, at]).astype(jnp.bfloat16)
+
+        tiles_of(width, body)
+        for r, o in enumerate(others):
+            if n < 2:
+                bulk.remote(w_v.at[aligned(4 * n + o, ff, 16)], in_f.at[n, r], xy_f.at[n, r], o, s)
+            else:
+                bulk.remote(w_v.at[pl.ds(n * hidden, hidden), aligned(o, wide, 128)], in_t.at[r], xy_t.at[r], o, s)
+
+    weight_part(0, a_v)
+    second[1].hop(0)
+    second[1].hop(1)
+    weight_part(1, a_v)
+    second[1].hop(2)
+
+    for b in range(2):
+        second[b].receive()
+        scatter = second[b]
 
         def finish(i, carry):
             piece = aligned(i, 16, 16)
             at = aligned(b * (rows // 16) + i, 16, 16)
-            hidden = h[at]
-            inverse = lax.rsqrt(mean_square(hidden) + EPS)
-            normed = hidden * inverse
-            grad = scatter.total(b, piece)
+            hidden_state = h[at]
+            scale_h = lax.rsqrt(mean_square(hidden_state) + EPS)
+            normed = hidden_state * scale_h
+            grad = scatter.total(piece)
             along = jnp.mean(normed * grad, axis=-1, keepdims=True)
-            grad_hidden = dy[at] + inverse * (grad - normed * along)
-            dh[at] = grad_hidden
+            live = live_rows(s * rows + i * 16, 16, lengths[b, 0])
+            upstream = cot[b, piece].astype(jnp.float32) * live
+            grad_hidden = upstream + scale_h * (grad - normed * along)
+            grad_x[at] = grad_hidden
             low = grad_hidden.astype(jnp.bfloat16)
             da[b, piece] = low
-            dot = jnp.mean(low.astype(jnp.float32) * branch[at], axis=-1, keepdims=True)
-            column[at] = jnp.broadcast_to(dot, (16, 2 * rows))
+            dot = jnp.mean(low.astype(jnp.float32) * (hidden_state - x[b, piece].astype(jnp.float32)), axis=-1, keepdims=True)
+            column[b, piece] = jnp.broadcast_to(dot, (16, 128))
             return carry
 
         lax.fori_loop(0, rows // 16, finish, 0)
-        gather.begin(da.at[b], keep.at[b], b)
-    mix[...] = column[...].T[:8]
-    for d in range(1, 8):
-        copies.remote(mix, mix_all.at[s], mix_sem.at[d - 1], g, (s + d) % 8)
-    local(mix, mix_all.at[s], mix_sem.at[7])
-    for k in (2, 1, 3, 0):
-        scatter_m.send(k)
-    for k in (1, 2, 3):
-        for b in range(2):
-            gather.step(b, k)
-    scatter_m.receive()
-    for b in range(2):
-
-        def write(i, carry):
+        gather.begin(da.at[b], own.at[b], b)
+        mix[b, :, :rows] = column[b].T[:8, :rows]
+        for d in range(1, 8):
+            last.remote(mix.at[b], mix_in.at[b, s], mix_sem.at[b, d - 1], g, (s + d) % 8)
+        local(mix.at[b], mix_in.at[b, s], mix_sem.at[b, 7])
+    early.finish()
+
+    third = [scatter_m_of(b, sums) for b in range(2)]
+    for b in range(2):
+
+        def body(at, i):
+            part[b, :, at] = product(p_v[2, at_b(b)], w3[:, at]).astype(jnp.bfloat16)
+
+        tiles_of(width, body)
+        third[b].begin()
+    gather.step(0, 1)
+    gather.step(1, 1)
+    for b in range(2):
+        third[b].ends()
+    weight_part(2, b_v)
+    gather.step(0, 2)
+    gather.step(1, 2)
+    third[0].hop(0)
+    third[1].hop(0)
+    gather.step(0, 3)
+    gather.step(1, 3)
+    for i in (1, 2):
+        third[0].hop(i)
+        third[1].hop(i)
+    for b in range(2):
+        third[b].receive()
+        scatter = third[b]
+
+        def result(i, carry):
             piece = aligned(i, 16, 16)
             at = aligned(b * (rows // 16) + i, 16, 16)
-            out[at] = (h[at] + scatter_m.total(b, piece)).astype(jnp.bfloat16)
+            out[at] = (h[at] + scatter.total(piece)).astype(jnp.bfloat16)
             return carry
 
-        lax.fori_loop(0, rows // 16, write, 0)
-    for b in range(2):
-        gather.finish(keep.at[b], b)
-    for d in range(8):
-        arrived(mix, mix_sem.at[d])
-    copies.finish()
-
-
-def gradients(
-    part, gq, gk, gv, gu, go, gf, gs, gt,
-    dn1, fq, fk, fv, fu, fo, ff_, fs, ft,
-    send, side, own, inbox, side_sem, own_sem, line_sem,
-    in_h, in_o, in_f, in_t, xy_h, xy_o, xy_f, xy_t, sum_h, sum_o, sum_f, sum_t, z_h, z_o, z_f, z_t,
-):
-    g, s, y, x, z, c = where_am_i()
-    others = across(y, x)
-    plane = [(o, 2 * z + e) for o in others for e in range(2)]
-    greet(line_partners(g, s) + plane)
-    copies = Copies(send)
-    rows = part.shape[1] // 8
-    scatter = Scatter(copies, part, rows, side, own, inbox, side_sem, own_sem, line_sem)
-    head = 128
-    wide = fo.shape[1]
-    ff = gf.shape[0] // 4
-    depth = fq.shape[0]
-    scatter.begin()
-    for k in (2, 1, 3, 0):
-        scatter.send(k)
-    grads_h = (gq, gk, gv, gu)
-    for n, (src, dst) in enumerate(((gf, in_f), (gs, in_f))):
-        for r, o in enumerate(others):
-            copies.remote(src.at[aligned(o, ff, 16)], dst.at[n, r], xy_f.at[n, r], o, s)
-        local(src.at[aligned(g, ff, 16)], dst.at[n, 3], xy_f.at[n, 3])
-    for r, o in enumerate(others):
-        copies.remote(gt.at[:, aligned(o, wide, 128)], in_t.at[r], xy_t.at[r], o, s)
-    local(gt.at[:, aligned(g, wide, 128)], in_t.at[3], xy_t.at[3])
-    for r, o in enumerate(others):
-        copies.remote(go.at[:, aligned(o, wide, 128)], in_o.at[r], xy_o.at[r], o, s)
-    local(go.at[:, aligned(g, wide, 128)], in_o.at[3], xy_o.at[3])
-    for r, o in enumerate(others + (g,)):
-        holds = o // 2 == c
-        for n, src in enumerate(grads_h):
-            for e in range(2):
-                a = src.at[:, e, :, aligned(o % 2, head, head)]
-                b = in_h.at[n, r]
-                to_self = jnp.logical_and(holds, c == e)
-                if r < 3:
-                    copies.remote(a, b, xy_h.at[n, r], o, 2 * z + e, holds)
-                else:
-                    copies.remote(a, b, xy_h.at[n, r], g, 2 * z + e, jnp.logical_and(holds, c != e))
-                    local(a, b, xy_h.at[n, r], to_self)
-
-    def add_up(read, write, count):
-        def add(i, carry):
-            piece = aligned(i, 16, 16)
-            value = read(0, piece)
-            for r in range(1, 4):
-                value = value + read(r, piece)
-            write(piece, value.astype(jnp.bfloat16))
-            return carry
-
-        lax.fori_loop(0, count, add, 0)
-
-    for n, out in enumerate((ff_, fs)):
-        for r in range(4):
+        lax.fori_loop(0, rows // 16, result, 0)
+    for j in range(2):
+        table[j] = turned_table(decay[4 * (2 * c + j) + z], length)
+    arrived(scale, load.at[12])
+    for b in range(2):
+        columns_of(inverse.at[at_b(b)], scale, b, rows)
+    for n in range(4):
+        arrived(wa_v.at[n], load.at[7 + n])
+    arrived(wo_v, load.at[11])
+
+    def sum_ff(n, result):
+        for r in range(3):
             arrived(in_f.at[n, r], xy_f.at[n, r])
-        total = sum_f.at[n]
-
-        def write(piece, value):
-            total[piece] = value
-
-        add_up(lambda r, piece: in_f[n, r, piece].astype(jnp.float32), write, ff // 16)
+            local(in_f.at[n, r], b_v.at[pl.ds(r * ff, ff)], load.at[13 + r])
+        for r in range(3):
+            arrived(b_v.at[pl.ds(r * ff, ff)], load.at[13 + r])
+        mine = w_v.at[aligned(4 * n + g, ff, 16)]
+
+        def read(at):
+            value = mine[at].astype(jnp.float32)
+            for r in range(3):
+                value = value + b_v.at[pl.ds(r * ff, ff)][at].astype(jnp.float32)
+            return value
+
+        def write(at, value):
+            mine[at] = value.astype(jnp.bfloat16)
+
+        pour(read, write, ff // 16)
         for d in (4, 3, 5, 2, 6, 1, 7, 0):
             to = (s + d) % 8
-            a = total.at[:, aligned(to, depth, 128)]
-            b = out.at[aligned(s, ff, 16)]
+            src = mine.at[:, aligned(to, depth, 128)]
+            dst = result.at[aligned(s, ff, 16)]
             if d:
-                copies.remote(a, b, z_f.at[n, d], g, to)
+                last.remote(src, dst, z_f.at[n, d], g, to)
             else:
-                local(a, b, z_f.at[n, d])
-    for r in range(4):
-        arrived(in_t.at[r], xy_t.at[r])
-
-    def write(piece, value):
-        sum_t[piece] = value
-
-    add_up(lambda r, piece: in_t[r, piece].astype(jnp.float32), write, 4 * ff // 16)
-    for d in (2, 1, 3, 0):
-        to = 2 * ((z + d) % 4) + s // 4
-        a = sum_t.at[aligned((z + d) % 4, ff, 16)]
-        b = ft.at[aligned(s % 4, ff, 16)]
-        self_ = to == s
-        if d:
-            copies.remote(a, b, z_t.at[s % 4], g, to)
-        else:
-            copies.remote(a, b, z_t.at[s % 4], g, to, jnp.logical_not(self_))
-            local(a, b, z_t.at[s % 4], self_)
-    for r in range(4):
+                local(src, dst, z_f.at[n, d])
+
+    def sum_third():
+        for r in range(3):
+            arrived(in_t.at[r], xy_t.at[r])
+            local(in_t.at[r], b_v.at[pl.ds(0, hidden), pl.ds(r * wide, wide)], load.at[13 + r])
+        for r in range(3):
+            arrived(b_v.at[pl.ds(0, hidden), pl.ds(r * wide, wide)], load.at[13 + r])
+        mine = w_v.at[pl.ds(2 * hidden, hidden), aligned(g, wide, 128)]
+
+        def read(at):
+            value = mine[at].astype(jnp.float32)
+            for r in range(3):
+                value = value + b_v[at, pl.ds(r * wide, wide)].astype(jnp.float32)
+            return value
+
+        def write(at, value):
+            mine[at] = value.astype(jnp.bfloat16)
+
+        pour(read, write, hidden // 16)
+        for d in (2, 1, 3, 0):
+            chip = (z + d) % 4
+            to = 2 * chip + s // 4
+            src = mine.at[aligned(chip, ff, 16)]
+            dst = ft.at[aligned(s % 4, ff, 16)]
+            if d:
+                last.remote(src, dst, z_t.at[s % 4], g, to)
+            else:
+                last.remote(src, dst, z_t.at[s % 4], g, to, to != s)
+                local(src, dst, z_t.at[s % 4], to == s)
+
+    sum_ff(0, ff_)
+    sum_ff(1, fs)
+
+    sums.finish()
+    fourth = [scatter_of(b, early) for b in range(2)]
+
+    def load_pre(b, j, slot):
+        local(pre_all.at[:, b, :, pl.ds(j * head, head)], pre.at[slot], load.at[16 + slot])
+
+    load_pre(0, 0, 0)
+    load_pre(0, 1, 1)
+    for b in range(2):
+        gather.finish(own.at[b], b)
+        local(da_all.at[b], a_v.at[at_b(b)], load.at[b])
+        for d in range(8):
+            arrived(mix_in.at[b, 0], mix_sem.at[b, d])
+        columns_of(mixed, mix_in, b, rows)
+        live = live_rows(0, length, lengths[b, 0])
+        arrived(a_v.at[at_b(b)], load.at[b])
+        for j in range(2):
+            arrived(pre.at[j], load.at[16 + j])
+            lanes = pl.ds(j * head, head)
+            error = product_right(a_v[at_b(b)], wo_v[pl.ds(j * head, head)])
+            q_pre, k_pre, v_pre, u_pre, o = [pre[j, n] for n in range(5)]
+            sigma = 1.0 / (1.0 + jnp.exp(-u_pre))
+            u = u_pre * sigma
+            scale_g = inverse[at_b(b), :1]
+            nat = u * o * scale_g
+            nat_v[at_b(b), lanes] = nat.astype(jnp.bfloat16)
+            dg = scale_g * (error - nat * mixed[:, :1])
+            dz[3, at_b(b), lanes] = (dg * o * (sigma * (1.0 + u_pre * (1.0 - sigma)))).astype(jnp.bfloat16)
+            do = (dg * u).astype(jnp.bfloat16)
+            q = silu(q_pre).astype(jnp.bfloat16)
+            k = (silu(k_pre) * live).astype(jnp.bfloat16)
+            v = (silu(v_pre) * live).astype(jnp.bfloat16)
+            scores = (product_right(k, q) * table[j]).astype(jnp.bfloat16)
+            dv = product(scores, do)
+            d_scores = (product_right(v, do) * table[j]).astype(jnp.bfloat16)
+            dk = product(d_scores, q)
+            dq = product_left(d_scores, k)
+            dz[0, at_b(b), lanes] = (dq * slope(pre[j, 0])).astype(jnp.bfloat16)
+            dz[1, at_b(b), lanes] = (dk * live * slope(pre[j, 1])).astype(jnp.bfloat16)
+            dz[2, at_b(b), lanes] = (dv * live * slope(pre[j, 2])).astype(jnp.bfloat16)
+            if b == 0:
+                load_pre(1, j, j)
+
+        def body(at, i):
+            value = product_right(dz[0, at_b(b)], wa_v[0, at])
+            for n in range(1, 4):
+                value = value + product_right(dz[n, at_b(b)], wa_v[n, at])
+            part[b, :, at] = value.astype(jnp.bfloat16)
+
+        tiles_of(width, body)
+        fourth[b].begin()
+        fourth[b].ends()
+    sum_third()
+    fourth[0].hop(0)
+    fourth[0].hop(1)
+
+    for b in range(2):
+        local(n1_all.at[b], b_v.at[at_b(b)], load.at[2 + b])
+    turn(turned, lambda t: nat_v[t], tokens // 128, 2 * head)
+
+    def body_o(at, i):
+        go_v[:, at] = product(turned[pl.ds(0, 2 * head)], a_v[:, at]).astype(jnp.bfloat16)
+
+    tiles_of(width, body_o)
+    for r, o in enumerate(others):
+        last.remote(go_v.at[:, aligned(o, wide, 128)], in_o.at[r], xy_o.at[r], o, s)
+    fourth[0].hop(2)
+    fourth[1].hop(0)
+    for b in range(2):
+        arrived(b_v.at[at_b(b)], load.at[2 + b])
+    half = width // 2
+    for n in range(4):
+        turn(turned, lambda t: dz[n, t], tokens // 128, 2 * head)
+        grad = grads_h.at[n]
+
+        def body_h(at, i):
+            place = pl.ds(pl.multiple_of((i % 2) * half + (i // 2) * 256, 256), 256)
+            grad[:, place] = product(turned[pl.ds(0, 2 * head)], b_v[:, at]).astype(jnp.bfloat16)
+
+        tiles_of(width, body_h)
+        for r, o in enumerate(others + (g,)):
+            holds = o // 2 == c
+            for e in range(2):
+                src = grad.at[aligned(o % 2, head, head), pl.ds(e * half, half)]
+                dst = in_h.at[n, r]
+                if r < 3:
+                    last.remote(src, dst, xy_h.at[n, r], o, 2 * z + e, holds)
+                else:
+                    last.remote(src, dst, xy_h.at[n, r], g, 2 * z + e, jnp.logical_and(holds, c != e))
+                    local(src, dst, xy_h.at[n, r], jnp.logical_and(holds, c == e))
+        if n < 2:
+            fourth[1].hop(n + 1)
+    for b in range(2):
+        fourth[b].receive()
+        scatter = fourth[b]
+
+        def finish_x(i, carry):
+            piece = aligned(i, 16, 16)
+            at = aligned(b * (rows // 16) + i, 16, 16)
+            v = x[b, piece].astype(jnp.float32)
+            scale_x = lax.rsqrt(mean_square(v) + EPS)
+            normed = v * scale_x
+            grad = scatter.total(piece)
+            along = jnp.mean(normed * grad, axis=-1, keepdims=True)
+            grad_x[at] = grad_x[at] + scale_x * (grad - normed * along)
+            return carry
+
+        lax.fori_loop(0, rows // 16, finish_x, 0)
+
+    for r in range(3):
         arrived(in_o.at[r], xy_o.at[r])
-
-    def write(piece, value):
-        sum_o[piece] = value
-
-    add_up(lambda r, piece: in_o[r, piece].astype(jnp.float32), write, 2 * head // 16)
+        local(in_o.at[r], b_v.at[pl.ds(0, 2 * head), pl.ds(r * wide, wide)], load.at[13 + r])
+
+    def held(n, r):
+        return a_v.at[pl.ds((2 * n + r // 2) * head, head), pl.ds((r % 2) * half, half)]
+
+    for n in range(4):
+        for r in range(4):
+            arrived(in_h.at[n, r], xy_h.at[n, r])
+            local(in_h.at[n, r], held(n, r), load.at[18 + 4 * n + r])
+    for r in range(3):
+        arrived(b_v.at[pl.ds(0, 2 * head), pl.ds(r * wide, wide)], load.at[13 + r])
+    mine_o = go_v.at[:, aligned(g, wide, 128)]
+
+    def read_o(at):
+        value = mine_o[at].astype(jnp.float32)
+        for r in range(3):
+            value = value + b_v[at, pl.ds(r * wide, wide)].astype(jnp.float32)
+        return value
+
+    def write_o(at, value):
+        mine_o[at] = value.astype(jnp.bfloat16)
+
+    pour(read_o, write_o, 2 * head // 16)
     for j in range(2):
         to = 2 * (2 * c + j) + z // 2
-        a = sum_o.at[pl.ds(j * head, head)]
-        b = fo.at[aligned(z % 2, head, head)]
-        self_ = to == s
-        copies.remote(a, b, z_o.at[z % 2], g, to, jnp.logical_not(self_))
-        local(a, b, z_o.at[z % 2], self_)
-    for n, out in enumerate((fq, fk, fv, fu)):
+        src = mine_o.at[pl.ds(j * head, head)]
+        dst = fo.at[aligned(z % 2, head, head)]
+        last.remote(src, dst, z_o.at[z % 2], g, to, to != s)
+        local(src, dst, z_o.at[z % 2], to == s)
+    for n, result in enumerate((fq, fk, fv, fu)):
         for r in range(4):
-            arrived(in_h.at[n, r], xy_h.at[n, r])
-        total = sum_h.at[n]
-        for q in range(4):
-
-            def write(piece, value):
-                total[q, piece] = value
-
-            add_up(lambda r, piece: in_h[n, r, q, piece].astype(jnp.float32), write, depth // 16)
+            arrived(held(n, r), load.at[18 + 4 * n + r])
+
+        def read_h(at):
+            value = held(n, 0)[at].astype(jnp.float32)
+            for r in range(1, 4):
+                value = value + held(n, r)[at].astype(jnp.float32)
+            return value
+
+        def write_h(at, value):
+            held(n, 0)[at] = value.astype(jnp.bfloat16)
+
+        pour(read_h, write_h, head // 16)
         for d in (2, 1, 3, 0):
-            to = (z + d) % 4
-            a = total.at[to]
-            b = out.at[:, aligned(z, head, head)]
+            chip = (z + d) % 4
+            src = held(n, 0).at[:, aligned(chip, depth, 128)]
+            dst = result.at[aligned(z, head, head)]
             if d:
-                copies.remote(a, b, z_h.at[n, d], g, 2 * to + c)
+                last.remote(src, dst, z_h.at[n, d], g, 2 * chip + c)
             else:
-                local(a, b, z_h.at[n, d])
-    scatter.receive()
-    for b in range(2):
-
-        def finish(i, carry):
-            piece = aligned(i, 16, 16)
-            at = aligned(b * (rows // 16) + i, 16, 16)
-            dn1[at] = scatter.total(b, piece)
-            return carry
-
-        lax.fori_loop(0, rows // 16, finish, 0)
-    for n, out in enumerate((ff_, fs)):
+                local(src, dst, z_h.at[n, d])
+
+    for n, result in enumerate((ff_, fs)):
         for d in range(8):
-            arrived(out.at[pl.ds(0, ff)], z_f.at[n, d])
+            arrived(result.at[pl.ds(0, ff)], z_f.at[n, d])
     for d in range(4):
         arrived(ft.at[pl.ds(0, ff)], z_t.at[d])
     for j in range(2):
         arrived(fo.at[pl.ds(0, head)], z_o.at[j])
-    for n, out in enumerate((fq, fk, fv, fu)):
+    for n, result in enumerate((fq, fk, fv, fu)):
         for d in range(4):
-            arrived(out.at[:, pl.ds(0, head)], z_h.at[n, d])
-    copies.finish()
+            arrived(result.at[pl.ds(0, head)], z_h.at[n, d])
+    early.finish()
+    bulk.finish()
+    last.finish()
 
 
 def call(kernel, number, ins, outs, scratch, name):
@@ -996,7 +1215,7 @@
         out_specs=[spec for _, spec in outs],
         scratch_shapes=scratch,
         compiler_params=pltpu.CompilerParams(
-            collective_id=number, has_side_effects=True, vmem_limit_bytes=48 * 2**20
+            collective_id=number, has_side_effects=True, vmem_limit_bytes=63 * 2**20
         ),
         name=name,
     )(*[value for value, _ in ins])
@@ -1016,12 +1235,10 @@
 
 def scatter_scratch(rows, width):
     return [
-        pltpu.VMEM((4, 2, rows, width), jnp.bfloat16),
-        pltpu.VMEM((4, 2, rows, width), jnp.bfloat16),
-        pltpu.VMEM((3, 2, rows, width), jnp.bfloat16),
-        dma(4),
-        dma(4),
-        dma(3),
+        pltpu.VMEM((2, 4, rows, width), jnp.bfloat16),
+        pltpu.VMEM((2, 2, 3, rows, width), jnp.bfloat16),
+        dma(2, 4),
+        dma(2, 2, 3),
     ]
 
 
@@ -1039,13 +1256,9 @@
     z, c = s // 2, s % 2
     x_low = tokens[:, 0]
     x = x_low.astype(f32).reshape(2 * rows, width)
-    slots = s * rows + jnp.arange(rows)
-    mine = (slots[None] < lengths[:, :1]).astype(f32).reshape(2 * rows, 1)
-    live = (jnp.arange(length)[None] < lengths[:, :1]).astype(f32).reshape(2 * length, 1)
-    dy = cotangent[:, 0].astype(f32).reshape(2 * rows, width) * mine
     in_smem = pl.BlockSpec(memory_space=pltpu.SMEM)
 
-    (n1_all, dm_all, n2_all, q_w, k_w, v_w, u_w, o_w, f_w, s_w, t_w, pre_all, h, branch, scale_all) = call(
+    (n1_all, dm_all, n2_all, q_w, k_w, v_w, u_w, o_w, f_w, s_w, t_w, pre_all, h, scale_all) = call(
         forward_part,
         0,
         [(lengths, in_smem), (decay_rate, in_smem), (x_low, VMEM), (cotangent[:, 0], VMEM)]
@@ -1054,104 +1267,46 @@
         + [(low_array(width, 2 * head), ANY)] * 4
         + [(low_array(2 * head, width), ANY)]
         + [(low_array(hidden, width), ANY)] * 3
-        + [(wide_array(5, 2, length, 2 * head), ANY), (wide_array(2 * rows, width), VMEM), (wide_array(2 * rows, width), VMEM),
-           (wide_array(2, 8, 8, 128), ANY)],
-        [dma(260), dma(3, 2), dma(2, 2, 3), dma(2, 7), dma(2, 2, 3), dma(2, 7), dma(2, 2, 3), dma(2, 7),
+        + [(wide_array(5, 2, length, 2 * head), ANY), (wide_array(2 * rows, width), VMEM), (wide_array(2, 8, 8, 128), ANY)],
+        [dma(280), dma(3, 2), dma(2, 2, 3), dma(2, 7), dma(2, 2, 3), dma(2, 7), dma(2, 2, 3), dma(2, 7),
          dma(4, 4), dma(2), dma(3, 4), dma(4, 3, 4), dma(3), dma(3, 3, 4),
          pltpu.VMEM((2, rows, width), bf16), pltpu.VMEM((2, rows, width), bf16), pltpu.VMEM((2, rows, width), bf16),
          pltpu.VMEM((2, length, width), bf16), pltpu.VMEM((4, width, 2 * head), bf16), pltpu.VMEM((2 * head, width), bf16), dma(7),
          pltpu.VMEM((5, 2, length, 2 * head), f32), dma(),
-         pltpu.VMEM((2, length, width), bf16), pltpu.VMEM((2, 4, rows, width), bf16), pltpu.VMEM((2, 3, rows, width), bf16),
-         dma(2, 4), dma(2, 3),
+         pltpu.VMEM((2, length, width), bf16)] + scatter_scratch(rows, width) + [
          pltpu.VMEM((2, length, length), f32), pltpu.VMEM((2, 8, 8, 128), f32), pltpu.VMEM((2, 8, 8, 128), f32),
          pltpu.VMEM((2, 8, 128), f32), dma(2, 8), dma(2, 8), pltpu.VMEM((2, 128, 128), f32)],
         "forward_part",
     )
-    n1_all = n1_all.reshape(2 * length, width)
-    dm_all = dm_all.reshape(2 * length, width)
-    q_pre, k_pre, v_pre, u_pre, o = [pre_all[n].reshape(2 * length, 2 * head) for n in range(5)]
-
-    def split(values):
-        return values.reshape(2, length, 2, head)
-
-    q = split(jax.nn.silu(q_pre).astype(bf16))
-    live_low = live.astype(bf16)
-    k = split(jax.nn.silu(k_pre).astype(bf16) * live_low)
-    v = split(jax.nn.silu(v_pre).astype(bf16) * live_low)
-    rates = jnp.take(decay_rate, 4 * (2 * c + jnp.arange(2)) + z)
-    places = jnp.arange(length).astype(f32)
-    offset = places[:, None] - places[None, :]
-    weight = jnp.where(offset >= 0, jnp.exp(-rates[:, None, None] * jnp.maximum(offset, 0.0)), 0.0)
-    scores = (jnp.einsum("bihd,bjhd->bhij", q, k, preferred_element_type=f32) * weight).astype(bf16)
-    u = jax.nn.silu(u_pre)
-    g = u * o
-
-    def per_token(values):
-        return values[:, 0].reshape(8, 2, rows).transpose(1, 0, 2).reshape(2 * length, 1)
-
-    n2_all = n2_all.reshape(2 * length, width)
-    h1 = product_right(n2_all, f_w)
-    h2 = product_right(n2_all, s_w)
-    p = (h1 * h2).astype(bf16)
-    part_m = product(p, t_w).astype(bf16).reshape(2, length, width)
-    dp = product_right(dm_all, t_w)
-    dh1 = (dp * h2).astype(bf16)
-    dh2 = (dp * h1).astype(bf16)
-    part = (product(dh1, f_w) + product(dh2, s_w)).astype(bf16).reshape(2, length, width)
-    gf = product_left(dh1, n2_all).astype(bf16)
-    gs = product_left(dh2, n2_all).astype(bf16)
-    gt = product_left(p, dm_all).astype(bf16)
-
-    da_all, dh, out, mix_all = call(
-        ffn_back,
-        2,
-        [(part, ANY), (part_m, ANY), (dy, VMEM), (h, VMEM), (branch, VMEM)],
-        [(low_array(2, length, width), ANY), (wide_array(2 * rows, width), VMEM), (low_array(2 * rows, width), VMEM),
-         (wide_array(8, 8, 2 * rows), ANY)],
-        [dma(80)] + scatter_scratch(rows, width) + scatter_scratch(rows, width)
-        + [pltpu.VMEM((2, rows, width), bf16), pltpu.VMEM((8, 2 * rows), f32), dma(8),
-           dma(2, 2, 3), dma(2, 7), dma(2), pltpu.VMEM((2 * rows, 2 * rows), f32)],
-        "ffn_back",
-    )
-    da_all = da_all.reshape(2 * length, width)
-    inverse = scale_all[:, :, 0, :rows].reshape(2 * length, 1)
-    mix = per_token(mix_all)
-    nat = g * inverse
-    go = product_left(nat.astype(bf16), da_all).astype(bf16)
-    dg = inverse * (product_right(da_all, o_w) - nat * mix)
-    do = split((dg * u).astype(bf16))
-    du_pre = (dg * o * silu_slope(u_pre)).astype(bf16)
-    d_scores = (jnp.einsum("bihe,bjhe->bhij", do, v, preferred_element_type=f32) * weight).astype(bf16)
-    dq = jnp.einsum("bhij,bjhd->bihd", d_scores, k, preferred_element_type=f32).reshape(2 * length, 2 * head)
-    dk = jnp.einsum("bhij,bihd->bjhd", d_scores, q, preferred_element_type=f32).reshape(2 * length, 2 * head)
-    dv = jnp.einsum("bhij,bihe->bjhe", scores, do, preferred_element_type=f32).reshape(2 * length, 2 * head)
-    dq_pre = (dq * silu_slope(q_pre)).astype(bf16)
-    dk_pre = (dk * live * silu_slope(k_pre)).astype(bf16)
-    dv_pre = (dv * live * silu_slope(v_pre)).astype(bf16)
-    part = product_right(dq_pre, q_w) + product_right(dk_pre, k_w)
-    part = (part + product_right(dv_pre, v_w) + product_right(du_pre, u_w)).astype(bf16).reshape(2, length, width)
-    heads = [product_left(n1_all, d).astype(bf16).reshape(4, 2, depth, 2 * head) for d in (dq_pre, dk_pre, dv_pre, du_pre)]
-
-    dn1, fq, fk, fv, fu, fo, ff, fs, ft = call(
-        gradients,
-        3,
-        [(v, ANY) for v in [part] + heads + [go, gf, gs, gt]],
-        [(wide_array(2 * rows, width), VMEM)] + [(low_array(depth, wide), ANY)] * 4 + [(low_array(depth, wide), ANY)]
-        + [(low_array(2 * hidden, depth), ANY)] * 2 + [(low_array(hidden, wide), ANY)],
-        [dma(140)] + scatter_scratch(rows, width)
-        + [pltpu.VMEM((4, 4, 4, depth, head), bf16), pltpu.VMEM((4, 2 * head, wide), bf16),
-           pltpu.VMEM((2, 4, hidden // 4, width), bf16), pltpu.VMEM((4, hidden, wide), bf16),
-           dma(4, 4), dma(4), dma(2, 4), dma(4),
-           pltpu.VMEM((4, 4, depth, head), bf16), pltpu.VMEM((2 * head, wide), bf16),
-           pltpu.VMEM((2, hidden // 4, width), bf16), pltpu.VMEM((hidden, wide), bf16),
-           dma(4, 4), dma(2), dma(2, 8), dma(4)],
-        "gradients",
-    )
-    grad_x = dh + norm_back(x, dn1)
+    da_all, mix_all, out, grad_x, fq, fk, fv, fu, fo, ff, fs, ft, _, _, _, _ = call(
+        backward_part,
+        1,
+        [(lengths, in_smem), (decay_rate, in_smem), (x_low, VMEM), (cotangent[:, 0], VMEM), (h, VMEM)]
+        + [(v, ANY) for v in (n1_all, dm_all, n2_all, q_w, k_w, v_w, u_w, o_w, f_w, s_w, t_w, pre_all, scale_all)],
+        [(low_array(2, length, width), ANY), (wide_array(8, 128), VMEM), (low_array(2 * rows, width), VMEM),
+         (wide_array(2 * rows, width), VMEM)]
+        + [(low_array(wide, depth), ANY)] * 4 + [(low_array(depth, wide), ANY)]
+        + [(low_array(2 * hidden, depth), ANY)] * 2 + [(low_array(hidden, wide), ANY)]
+        + [(low_array(2, 3, hidden // 4, width), ANY), (low_array(3, hidden, wide), ANY), (low_array(3, 2 * head, wide), ANY),
+           (low_array(4, 4, head, width // 2), ANY)],
+        [dma(40), dma(12), dma(120), dma(70), dma(40), dma(2), dma(2, 2, 3), dma(2, 7),
+         pltpu.VMEM((2 * length, width), bf16), pltpu.VMEM((2 * length, width), bf16), pltpu.VMEM((3 * hidden, width), bf16),
+         pltpu.VMEM((4, width, 2 * head), bf16), pltpu.VMEM((2 * head, width), bf16),
+         pltpu.VMEM((3, 2 * length, hidden), bf16), pltpu.VMEM((hidden, 2 * length), bf16),
+         pltpu.VMEM((2, length, width), bf16)]
+        + scatter_scratch(rows, width) + scatter_scratch(rows, width)
+        + [pltpu.VMEM((2, 8, 8, 128), f32), pltpu.VMEM((2, 8, 128), f32), pltpu.VMEM((2, 8, 8, 128), f32), dma(2, 8),
+           pltpu.VMEM((2, 128, 128), f32), pltpu.VMEM((2 * length, 128), f32), pltpu.VMEM((length, 128), f32),
+           pltpu.VMEM((2, rows, width), bf16), pltpu.VMEM((2, length, length), f32), pltpu.VMEM((2, 5, length, head), f32),
+           pltpu.VMEM((4, 2 * length, 2 * head), bf16), pltpu.VMEM((2 * length, 2 * head), bf16),
+           pltpu.VMEM((2 * head, width), bf16), pltpu.VMEM((4, 2 * head, width), bf16),
+           dma(2, 3), dma(3), dma(3), dma(4, 4), dma(2, 8), dma(4), dma(2), dma(4, 4)],
+        "backward_part",
+    )
     return (
         out.reshape(2, 1, rows, width),
         grad_x.reshape(2, 1, rows, width),
-        fq.astype(f32), fk.astype(f32), fv.astype(f32), fu.astype(f32), fo.astype(f32),
+        fq.T.astype(f32), fk.T.astype(f32), fv.T.astype(f32), fu.T.astype(f32), fo.astype(f32),
         ff.T.astype(f32), fs.T.astype(f32), ft.astype(f32),
     )
 

time: 684 us -> 543 us (0.79)
  matrix products: 94.4 us -> 0 us
  other arithmetic: 21.5 us -> 5.88 us
  local copies, waits for them, and re-layouts: 29.4 us -> 14.6 us
  Pallas kernels: 531 us -> 521 us
    dot_general x23 -> x0, matrix products: 94.4 us -> none  [the longest x8 35 us: product_right(): lax.dot_general(left, right, (((1,), (1,)), ((), ())), preferred_element_...]
    convert_element_type x10 -> x2, other arithmetic: 13.9 us -> 1.18 us  [the longest x1 1.1 us: line_shards(): fk.T.astype(f32)]
    pallas_call x3 -> x2, Pallas kernels: 531 us -> 521 us  [call(): pl.pallas_call(kernel, out_shape=[shape for shape, _ in outs], in_specs=[...]
    unnamed x97 -> x21, local copies, waits for them, and re-layouts: 10.4 us -> 14.6 us
where the time goes in v3:
time: 543 us; the launch traced here: 542 us
  Pallas kernels  521 us (96%)
  local copies, waits for them, and re-layouts  14.6 us (3%)
  other arithmetic  5.88 us (1%)
    pallas_call x2, Pallas kernels, call(): pl.pallas_call(kernel, out_shape=[shape for shape, _ in outs], in_specs=[...  521 us
    unnamed x21, local copies, waits for them, and re-layouts  14.6 us

profile of v3, /device:TPU:0, one launch (start us, length us, event | category | flops | bytes accessed | tf_op | source)
XLA Modules:
  0.0 542.4 jit_solution(4105597464204032704)
XLA Ops:
  0.6 1.3 copy.25.lengths
  1.9 2.2 copy.22
  4.2 2.2 copy.23
  6.4 241.9 %forward_part.1 = (bf16[2,512,2048]{2,1,0:T(8,128)(2,1)}, bf16[2,512,2048]{2,1,0:T(8,128)(2,1)}, bf16[2,512,2048]{2,1,0:T(8,128)(2,1)}, bf16[2048,256]{1,0:T(8,1...) custom-call(s32[2,1]{1,0:T(2,128)} %copy.25.lengths, ...), custom_call_target="tpu_custom_call" | custom-call | tf_op jit(solution)/shard_map/forward_part/pallas_call | solution.py:1211
  248.3 279.3 %backward_part.1 = (bf16[2,512,2048]{2,1,0:T(8,128)(2,1)}, f32[8,128]{1,0:T(8,128)}, bf16[128,2048]{1,0:T(8,128)(2,1)}, f32[128,2048]{1,0:T(8,128)}, bf16[512,25...) custom-call(s32[2,1]{1,0:T(2,128)} %copy.25.lengths, ...), custom_call_target="tpu_custom_call" | custom-call | tf_op jit(solution)/shard_map/backward_part/pallas_call | solution.py:1211
  527.6 0.0 copy-start.3
  527.6 0.0 copy-start.4
  527.7 1.9 convert_element_type.50
  529.5 1.1 convert_bitcast_fusion.4
  530.6 0.0 copy-start.1
  530.6 1.0 copy.29
  531.6 1.0 copy.28
  532.6 0.0 copy-done.3
  532.6 0.0 copy-done.4
  532.6 0.1 convert_bitcast_fusion.2
  532.7 1.0 copy.31
  533.7 1.0 copy.30
  534.7 0.0 copy-done.1
  534.7 1.3 convert_element_type.55
  536.0 1.5 convert_bitcast_fusion
  537.6 0.0 copy-start.2
  537.6 1.5 copy.33
  539.1 0.0 copy-start
  539.1 1.5 copy.32
  540.6 0.0 copy-done.2
  540.6 0.8 copy.36
  541.4 0.0 copy-done
  541.4 1.0 copy.37
Async XLA Ops:
  527.6 5.0 copy-start.3
  527.6 5.0 copy-start.4
  530.6 4.1 copy-start.1
  537.6 3.1 copy-start.2
  539.1 2.3 copy-start

commit v4 on v3

--- a/solution.py
+++ b/solution.py
@@ -299,14 +299,19 @@
             copy.start()
         else:
             pl.when(when)(copy.start)
+        return self.pending[-1]
+
+    def settle(self, entry):
+        self.pending = [other for other in self.pending if other is not entry]
+        copy, when = entry
+        if when is None:
+            copy.wait_send()
+        else:
+            pl.when(when)(copy.wait_send)
 
     def finish(self):
-        for copy, when in self.pending:
-            if when is None:
-                copy.wait_send()
-            else:
-                pl.when(when)(copy.wait_send)
-        self.pending = []
+        while self.pending:
+            self.settle(self.pending[0])
 
 
 def local(src, dst, sem, when=None):
@@ -419,8 +424,8 @@
 
 
 class LineScatter:
-    def __init__(self, copies, part, rows, side, inbox, side_sem, line_sem):
-        self.copies, self.part, self.rows = copies, part, rows
+    def __init__(self, copies, part, rows, side, inbox, side_sem, line_sem, queue):
+        self.copies, self.part, self.rows, self.queue = copies, part, rows, queue
         self.side, self.inbox, self.side_sem, self.line_sem = side, inbox, side_sem, line_sem
         self.g, self.s, _, _, self.z, self.c = where_am_i()
 
@@ -434,40 +439,69 @@
                 self.part.at[theirs], self.side.at[chip], self.side_sem.at[chip], self.g, self.s + 1 - 2 * self.c
             )
 
-    def pass_on(self, chip, way, edge):
-        z = self.z
+    def add_on(self, chip, way):
+        own, side = self.mine(chip), self.side.at[chip]
         slot = chip - 1 if way == 0 else chip
-        own, side, come = self.mine(chip), self.side.at[chip], self.inbox.at[way, slot]
-        before = (z < chip) if way == 0 else (z > chip)
-        first = (z == 0) if way == 0 else (z == 3)
-        go = jnp.logical_and(before, first if edge else jnp.logical_not(first))
+        come = self.inbox.at[way, slot]
+        arrived(side, self.side_sem.at[chip])
+        arrived(come, self.line_sem.at[way, slot])
+
+        def three(at):
+            return own[at].astype(jnp.float32) + side[at].astype(jnp.float32) + come[at].astype(jnp.float32)
 
         def write(at, value):
             own[at] = value.astype(jnp.bfloat16)
 
+        pour(three, write, self.rows // 16)
+
+    def push(self, chip, way, when):
+        slot = chip - 1 if way == 0 else chip
+        to = (self.s + 2) % 8 if way == 0 else (self.s + 6) % 8
+        return self.copies.remote(
+            self.mine(chip), self.inbox.at[way, slot], self.line_sem.at[way, slot], self.g, to, when
+        )
+
+    def pass_on(self, chip, way):
+        end = self.z == (0 if way == 0 else 3)
+        own, side = self.mine(chip), self.side.at[chip]
+
         def two(at):
             return own[at].astype(jnp.float32) + side[at].astype(jnp.float32)
 
-        @pl.when(go)
+        def write(at, value):
+            own[at] = value.astype(jnp.bfloat16)
+
+        @pl.when(end)
         def _():
             arrived(side, self.side_sem.at[chip])
-            if edge:
-                pour(two, write, self.rows // 16)
+            pour(two, write, self.rows // 16)
+
+        if way in self.queue:
+            self.copies.settle(self.queue.pop(way))
+        self.queue[way] = self.push(chip, way, end)
+
+    def start(self, i):
+        self.pass_on(3 - i, 0)
+        self.pass_on(i, 1)
+
+    def hop(self, i):
+        z = self.z
+        for inner in (1, 2):
+
+            @pl.when(z == inner)
+            def _():
+                near = inner == 1
+                if i < 2:
+                    self.add_on(3 - i if near else i, 0 if near else 1)
+                else:
+                    self.add_on(0 if near else 3, 1 if near else 0)
+
+        for inner in (1, 2):
+            near = inner == 1
+            if i < 2:
+                self.push(3 - i if near else i, 0 if near else 1, z == inner)
             else:
-                arrived(come, self.line_sem.at[way, slot])
-                pour(lambda at: two(at) + come[at].astype(jnp.float32), write, self.rows // 16)
-
-        to = (self.s + 2) % 8 if way == 0 else (self.s + 6) % 8
-        self.copies.remote(own, come, self.line_sem.at[way, slot], self.g, to, go)
-
-    def ends(self):
-        for i in range(3):
-            self.pass_on(3 - i, 0, True)
-            self.pass_on(i, 1, True)
-
-    def hop(self, i):
-        self.pass_on(3 - i, 0, False)
-        self.pass_on(i, 1, False)
+                self.push(0 if near else 3, 1 if near else 0, z == inner)
 
     def receive(self):
         z = self.z
@@ -501,7 +535,7 @@
 def forward_part(
     lengths, decay, x, cot, wq, wk, wv, wu, wo, w1, w2, w3,
     n1_all, dm_all, n2_all, q_all, k_all, v_all, u_all, o_all, f_all, s_all, t_all, pre_all, h, scale_all,
-    send, own, hop_n, side_n, hop_d, side_d, hop_m, side_m, z_head, z_out, z_ff, xy_head, xy_out, xy_ff,
+    w1_t, w2_t, send, own, hop_n, side_n, hop_d, side_d, hop_m, side_m, z_head, z_out, z_ff, xy_head, xy_out, xy_ff,
     n1, dm, n2, n1_v, w_v, wo_v, load, pre_v, pre_sem, part, side, inbox, side_sem, line_sem,
     table, squares, inbox_sq, scale, sq_sem, sc_sem, column,
 ):
@@ -559,7 +593,7 @@
             copies.remote(block, block, xy_out.at[r], o, s)
 
     def send_ff(n):
-        src, dst = ((w1, f_all), (w2, s_all))[n]
+        src, dst = ((w1_t, f_all), (w2_t, s_all))[n]
         for d in (4, 3, 5, 2, 6, 1, 7, 0):
             to = (s + d) % 8
             a = src.at[aligned(to, ff, 16)]
@@ -612,28 +646,31 @@
 
         def masked(i, carry):
             at = aligned(i, 16, 16)
-            live = live_rows(first + i * 16, 16, lengths[b, 0])
+            live = live_rows(first + i * 16, 16, lengths[0, b])
             dm[b, at] = (cot[b, at].astype(jnp.float32) * live).astype(jnp.bfloat16)
             return carry
 
         lax.fori_loop(0, rows // 16, masked, 0)
+    for src, dst in ((w1, w1_t), (w2, w2_t)):
+        dst[...] = src[...].T
     pass_heads(0)
     send_heads(2)
     pass_heads(1)
     send_heads(3)
-    for b in range(2):
-        gather_n.begin(n1.at[b], own.at[0, b], b)
-    send_out()
+    send_ff(0)
     pass_heads(2)
     pass_heads(3)
-    gather_n.step(0, 1)
-    gather_n.step(1, 1)
+    send_out()
+    send_ff(1)
+    pass_ff(0)
+    for b in range(2):
+        gather_n.begin(n1.at[b], own.at[0, b], b)
     pass_out()
-    gather_n.step(0, 2)
-    gather_n.step(1, 2)
-    send_ff(0)
-    gather_n.step(0, 3)
-    gather_n.step(1, 3)
+    pass_ff(1)
+    for k in (1, 2, 3):
+        gather_n.step(0, k)
+        gather_n.step(1, k)
+    send_third()
     for r, o in enumerate(others):
         from_here = (o // 2) == c
         for n, (_, dst) in enumerate(heads):
@@ -652,10 +689,13 @@
     for n in range(4):
         arrived(w_v.at[n], load.at[n])
     arrived(wo_v, load.at[4])
-    scatters = []
+    queue = {}
+    scatters = [
+        LineScatter(copies, part.at[b], rows, side.at[b], inbox.at[b], side_sem.at[b], line_sem.at[b], queue) for b in range(2)
+    ]
+    half = length // 2
     for b in range(2):
         arrived(n1_v.at[b], load.at[5 + b])
-        half = length // 2
 
         def project(i, carry):
             at = aligned(i, half, 16)
@@ -664,7 +704,9 @@
             return carry
 
         lax.fori_loop(0, 2, project, 0)
-        live = live_rows(0, length, lengths[b, 0])
+        if b == 1:
+            scatters[0].start(1)
+        live = live_rows(0, length, lengths[0, b])
         for j in range(2):
             lanes = pl.ds(j * head, head)
             q = silu(pre_v[0, b, :, lanes]).astype(jnp.bfloat16)
@@ -677,6 +719,8 @@
         row = jnp.broadcast_to(square, (length, 128)).T[:8]
         for to in range(8):
             squares[b, to, :, :rows] = row[:, to * rows : (to + 1) * rows]
+        everyone_on_line(copies, squares, inbox_sq.at[b], sq_sem.at[b], g, s, lambda to: squares.at[b, to])
+        local(squares.at[b, s], inbox_sq.at[b, s], sq_sem.at[b, 7])
         low = gated.astype(jnp.bfloat16)
 
         def out_part(i, carry):
@@ -685,20 +729,27 @@
             return carry
 
         lax.fori_loop(0, width // 256, out_part, 0)
-        scatter = LineScatter(copies, part.at[b], rows, side.at[b], inbox.at[b], side_sem.at[b], line_sem.at[b])
-        scatter.begin()
-        scatter.ends()
-        everyone_on_line(copies, squares, inbox_sq.at[b], sq_sem.at[b], g, s, lambda to: squares.at[b, to])
-        local(squares.at[b, s], inbox_sq.at[b, s], sq_sem.at[b, 7])
-        scatters.append(scatter)
+        scatters[b].begin()
+        if b == 0:
+            scatters[0].start(0)
     local(pre_v, pre_all, pre_sem)
+    for b in range(2):
+        gather_d.begin(dm.at[b], own.at[1, b], b)
     scatters[0].hop(0)
+    scatters[0].start(2)
     scatters[0].hop(1)
+    scatters[1].start(0)
+    scatters[0].hop(2)
+    gather_d.step(0, 1)
+    gather_d.step(1, 1)
+    scatters[1].start(1)
     scatters[1].hop(0)
-    scatters[0].hop(2)
+    pass_third()
+    scatters[1].start(2)
     scatters[1].hop(1)
+    gather_d.step(0, 2)
     scatters[1].hop(2)
-    pass_ff(0)
+    gather_d.step(1, 2)
     for b in range(2):
         for d in range(8):
             arrived(inbox_sq.at[b, 0], sq_sem.at[b, d])
@@ -707,17 +758,10 @@
             total = total + inbox_sq[b, d]
         row = lax.rsqrt(total / width + EPS)
         scale[b] = row
-        for d in range(1, 8):
-            copies.remote(scale.at[b], scale_all.at[b, s], sc_sem.at[b, d - 1], g, (s + d) % 8)
-        local(scale.at[b], scale_all.at[b, s], sc_sem.at[b, 7])
         column[b] = jnp.broadcast_to(row[:1], (128, 128)).T
     for b in range(2):
         scatter = scatters[b]
         scatter.receive()
-        if b == 0:
-            send_ff(1)
-        else:
-            send_third()
 
         def finish(i, carry):
             piece = aligned(i, 16, 16)
@@ -731,20 +775,14 @@
         lax.fori_loop(0, rows // 16, finish, 0)
         gather_m.begin(n2.at[b], own.at[2, b], b)
     for b in range(2):
-        gather_d.begin(dm.at[b], own.at[1, b], b)
-    gather_m.step(0, 1)
-    gather_m.step(1, 1)
-    pass_ff(1)
-    gather_m.step(0, 2)
-    gather_m.step(1, 2)
-    gather_d.step(0, 1)
-    gather_d.step(1, 1)
-    pass_third()
-    gather_m.step(0, 3)
-    gather_m.step(1, 3)
-    for k in (2, 3):
-        for b in range(2):
-            gather_d.step(b, k)
+        for d in range(1, 8):
+            copies.remote(scale.at[b], scale_all.at[b, s], sc_sem.at[b, d - 1], g, (s + d) % 8)
+        local(scale.at[b], scale_all.at[b, s], sc_sem.at[b, 7])
+    gather_d.step(0, 3)
+    gather_d.step(1, 3)
+    for k in (1, 2, 3):
+        gather_m.step(0, k)
+        gather_m.step(1, k)
 
     for b in range(2):
         gather_d.finish(own.at[1, b], b)
@@ -856,11 +894,14 @@
         tiles_of(width, body)
 
     def scatter_of(b, copies):
-        return LineScatter(copies, part.at[b], rows, side.at[b], inbox.at[b], side_sem.at[b], line_sem.at[b])
+        return LineScatter(copies, part.at[b], rows, side.at[b], inbox.at[b], side_sem.at[b], line_sem.at[b], queue)
 
     def scatter_m_of(b, copies):
-        return LineScatter(copies, part.at[b], rows, side_m.at[b], inbox_m.at[b], side_sem_m.at[b], line_sem_m.at[b])
-
+        return LineScatter(
+            copies, part.at[b], rows, side_m.at[b], inbox_m.at[b], side_sem_m.at[b], line_sem_m.at[b], queue_m
+        )
+
+    queue, queue_m = {}, {}
     second = [scatter_of(b, early) for b in range(2)]
     for n in (0, 4, 5, 2, 6):
         ref = {0: a_v.at[at_b(0)], 2: b_v.at[at_b(0)], 4: w1, 5: w2, 6: w3}[n]
@@ -868,16 +909,18 @@
     feed_forward(0)
     norm_part(0)
     second[0].begin()
-    second[0].ends()
+    second[0].start(0)
     arrived(a_v.at[at_b(1)], load.at[1])
     arrived(b_v.at[at_b(1)], load.at[3])
     feed_forward(1)
+    second[0].start(1)
     second[0].hop(0)
     norm_part(1)
     second[1].begin()
-    second[1].ends()
+    second[0].start(2)
     second[0].hop(1)
     second[0].hop(2)
+    second[1].start(0)
 
     def weight_part(n, operand):
         turn(turned, lambda t: p_v[n, t], tokens // 128, hidden)
@@ -893,14 +936,18 @@
                 bulk.remote(w_v.at[pl.ds(n * hidden, hidden), aligned(o, wide, 128)], in_t.at[r], xy_t.at[r], o, s)
 
     weight_part(0, a_v)
+    second[1].start(1)
     second[1].hop(0)
+    weight_part(1, a_v)
+    second[1].start(2)
     second[1].hop(1)
-    weight_part(1, a_v)
     second[1].hop(2)
 
     for b in range(2):
         second[b].receive()
         scatter = second[b]
+        if b == 1:
+            queue.clear()
 
         def finish(i, carry):
             piece = aligned(i, 16, 16)
@@ -910,7 +957,7 @@
             normed = hidden_state * scale_h
             grad = scatter.total(piece)
             along = jnp.mean(normed * grad, axis=-1, keepdims=True)
-            live = live_rows(s * rows + i * 16, 16, lengths[b, 0])
+            live = live_rows(s * rows + i * 16, 16, lengths[0, b])
             upstream = cot[b, piece].astype(jnp.float32) * live
             grad_hidden = upstream + scale_h * (grad - normed * along)
             grad_x[at] = grad_hidden
@@ -936,20 +983,25 @@
 
         tiles_of(width, body)
         third[b].begin()
+    third[0].start(0)
     gather.step(0, 1)
     gather.step(1, 1)
-    for b in range(2):
-        third[b].ends()
+    third[0].start(1)
+    third[0].hop(0)
     weight_part(2, b_v)
     gather.step(0, 2)
+    third[0].start(2)
+    third[0].hop(1)
+    third[0].hop(2)
+    third[1].start(0)
     gather.step(1, 2)
-    third[0].hop(0)
+    third[1].start(1)
     third[1].hop(0)
     gather.step(0, 3)
+    third[1].start(2)
+    third[1].hop(1)
+    third[1].hop(2)
     gather.step(1, 3)
-    for i in (1, 2):
-        third[0].hop(i)
-        third[1].hop(i)
     for b in range(2):
         third[b].receive()
         scatter = third[b]
@@ -1030,6 +1082,7 @@
     sum_ff(1, fs)
 
     sums.finish()
+    queue = {}
     fourth = [scatter_of(b, early) for b in range(2)]
 
     def load_pre(b, j, slot):
@@ -1043,7 +1096,7 @@
         for d in range(8):
             arrived(mix_in.at[b, 0], mix_sem.at[b, d])
         columns_of(mixed, mix_in, b, rows)
-        live = live_rows(0, length, lengths[b, 0])
+        live = live_rows(0, length, lengths[0, b])
         arrived(a_v.at[at_b(b)], load.at[b])
         for j in range(2):
             arrived(pre.at[j], load.at[16 + j])
@@ -1080,10 +1133,16 @@
 
         tiles_of(width, body)
         fourth[b].begin()
-        fourth[b].ends()
+        if b == 0:
+            fourth[0].start(0)
+        else:
+            fourth[0].start(1)
+            fourth[0].hop(0)
     sum_third()
-    fourth[0].hop(0)
+    fourth[0].start(2)
     fourth[0].hop(1)
+    fourth[0].hop(2)
+    fourth[1].start(0)
 
     for b in range(2):
         local(n1_all.at[b], b_v.at[at_b(b)], load.at[2 + b])
@@ -1095,7 +1154,7 @@
     tiles_of(width, body_o)
     for r, o in enumerate(others):
         last.remote(go_v.at[:, aligned(o, wide, 128)], in_o.at[r], xy_o.at[r], o, s)
-    fourth[0].hop(2)
+    fourth[1].start(1)
     fourth[1].hop(0)
     for b in range(2):
         arrived(b_v.at[at_b(b)], load.at[2 + b])
@@ -1119,8 +1178,11 @@
                 else:
                     last.remote(src, dst, xy_h.at[n, r], g, 2 * z + e, jnp.logical_and(holds, c != e))
                     local(src, dst, xy_h.at[n, r], jnp.logical_and(holds, c == e))
-        if n < 2:
-            fourth[1].hop(n + 1)
+        if n == 0:
+            fourth[1].start(2)
+            fourth[1].hop(1)
+        if n == 1:
+            fourth[1].hop(2)
     for b in range(2):
         fourth[b].receive()
         scatter = fourth[b]
@@ -1261,14 +1323,15 @@
     (n1_all, dm_all, n2_all, q_w, k_w, v_w, u_w, o_w, f_w, s_w, t_w, pre_all, h, scale_all) = call(
         forward_part,
         0,
-        [(lengths, in_smem), (decay_rate, in_smem), (x_low, VMEM), (cotangent[:, 0], VMEM)]
-        + [(v, ANY) for v in (w_query, w_key, w_value, w_gate, w_out, w_first.T, w_second.T, w_third)],
+        [(lengths.T, in_smem), (decay_rate, in_smem), (x_low, VMEM), (cotangent[:, 0], VMEM)]
+        + [(v, ANY) for v in (w_query, w_key, w_value, w_gate, w_out)]
+        + [(w_first, VMEM), (w_second, VMEM), (w_third, ANY)],
         [(low_array(2, length, width), ANY)] * 3
         + [(low_array(width, 2 * head), ANY)] * 4
         + [(low_array(2 * head, width), ANY)]
         + [(low_array(hidden, width), ANY)] * 3
         + [(wide_array(5, 2, length, 2 * head), ANY), (wide_array(2 * rows, width), VMEM), (wide_array(2, 8, 8, 128), ANY)],
-        [dma(280), dma(3, 2), dma(2, 2, 3), dma(2, 7), dma(2, 2, 3), dma(2, 7), dma(2, 2, 3), dma(2, 7),
+        [pltpu.VMEM((2 * hidden, depth), bf16), pltpu.VMEM((2 * hidden, depth), bf16), dma(280), dma(3, 2), dma(2, 2, 3), dma(2, 7), dma(2, 2, 3), dma(2, 7), dma(2, 2, 3), dma(2, 7),
          dma(4, 4), dma(2), dma(3, 4), dma(4, 3, 4), dma(3), dma(3, 3, 4),
          pltpu.VMEM((2, rows, width), bf16), pltpu.VMEM((2, rows, width), bf16), pltpu.VMEM((2, rows, width), bf16),
          pltpu.VMEM((2, length, width), bf16), pltpu.VMEM((4, width, 2 * head), bf16), pltpu.VMEM((2 * head, width), bf16), dma(7),
@@ -1281,7 +1344,7 @@
     da_all, mix_all, out, grad_x, fq, fk, fv, fu, fo, ff, fs, ft, _, _, _, _ = call(
         backward_part,
         1,
-        [(lengths, in_smem), (decay_rate, in_smem), (x_low, VMEM), (cotangent[:, 0], VMEM), (h, VMEM)]
+        [(lengths.T, in_smem), (decay_rate, in_smem), (x_low, VMEM), (cotangent[:, 0], VMEM), (h, VMEM)]
         + [(v, ANY) for v in (n1_all, dm_all, n2_all, q_w, k_w, v_w, u_w, o_w, f_w, s_w, t_w, pre_all, scale_all)],
         [(low_array(2, length, width), ANY), (wide_array(8, 128), VMEM), (low_array(2 * rows, width), VMEM),
          (wide_array(2 * rows, width), VMEM)]

time: 543 us -> 495 us (0.912)
  Pallas kernels: 521 us -> 475 us
  local copies, waits for them, and re-layouts: 14.6 us -> 8.84 us
    pallas_call x2, Pallas kernels: 521 us -> 475 us  [call(): pl.pallas_call(kernel, out_shape=[shape for shape, _ in outs], in_specs=[...]
    unnamed x21 -> x18, local copies, waits for them, and re-layouts: 14.6 us -> 8.84 us
where the time goes in v4:
time: 495 us; the launch traced here: 490 us
  Pallas kernels  475 us (96%)
  local copies, waits for them, and re-layouts  8.84 us (2%)
  other arithmetic  5.88 us (1%)
    pallas_call x2, Pallas kernels, call(): pl.pallas_call(kernel, out_shape=[shape for shape, _ in outs], in_specs=[...  475 us

profile of v4, /device:TPU:0, one launch (start us, length us, event | category | flops | bytes accessed | tf_op | source)
XLA Modules:
  0.0 490.0 jit_solution(8132796636878188602)
XLA Ops:
  0.6 226.1 %forward_part.1 = (bf16[2,512,2048]{2,1,0:T(8,128)(2,1)}, bf16[2,512,2048]{2,1,0:T(8,128)(2,1)}, bf16[2,512,2048]{2,1,0:T(8,128)(2,1)}, bf16[2048,256]{1,0:T(8,1...) custom-call(s32[1,2]{1,0:T(1,128)} %bitcast.27, ...), custom_call_target="tpu_custom_call" | custom-call | tf_op jit(solution)/shard_map/forward_part/pallas_call | solution.py:1273
  226.7 248.4 %backward_part.1 = (bf16[2,512,2048]{2,1,0:T(8,128)(2,1)}, f32[8,128]{1,0:T(8,128)}, bf16[128,2048]{1,0:T(8,128)(2,1)}, f32[128,2048]{1,0:T(8,128)}, bf16[512,25...) custom-call(s32[1,2]{1,0:T(1,128)} %bitcast.28, ...), custom_call_target="tpu_custom_call" | custom-call | tf_op jit(solution)/shard_map/backward_part/pallas_call | solution.py:1273
  475.2 0.0 copy-start.3
  475.2 0.0 copy-start.4
  475.2 1.9 convert_element_type.50
  477.0 1.1 convert_bitcast_fusion.4
  478.2 0.0 copy-start.1
  478.2 1.0 copy.25
  479.2 1.0 copy.24
  480.2 0.0 copy-done.3
  480.2 0.0 copy-done.4
  480.2 0.1 convert_bitcast_fusion.2
  480.2 1.0 copy.27
  481.2 1.0 copy.26
  482.2 0.0 copy-done.1
  482.2 1.3 convert_element_type.55
  483.5 1.5 convert_bitcast_fusion
  485.1 0.0 copy-start.2
  485.1 1.5 copy.29
  486.6 0.0 copy-start
  486.6 1.5 copy.28
  488.2 0.0 copy-done.2
  488.2 0.8 copy.32
  489.0 0.0 copy-done
  489.0 1.0 copy.33
Async XLA Ops:
  475.2 5.0 %copy-start.3 = (bf16[512,256]{1,0:T(8,128)(2,1)S(1)}, bf16[512,256]{1,0:T(8,128)(2,1)}, u32[]{:S(2)}) copy-start(bf16[512,256]{1,0:T(8,128)(2,1)} %get-tuple-element.52) | copy-start | bytes 786436
  475.2 5.0 %copy-start.4 = (bf16[512,256]{1,0:T(8,128)(2,1)S(1)}, bf16[512,256]{1,0:T(8,128)(2,1)}, u32[]{:S(2)}) copy-start(bf16[512,256]{1,0:T(8,128)(2,1)} %get-tuple-element.53) | copy-start | bytes 786436
  478.2 4.1 copy-start.1
  485.1 3.1 copy-start.2
  486.6 2.3 copy-start

commit v5 on v4

--- a/solution.py
+++ b/solution.py
@@ -1,3 +1,5 @@
+import functools
+
 import jax
 import jax.numpy as jnp
 from jax import lax
@@ -277,24 +279,27 @@
     )
 
 
+class Spare:
+    def __init__(self, sems):
+        self.sems, self.free = sems, list(range(sems.shape[0]))
+
+
 class Copies:
-    def __init__(self, sems):
-        self.sems = sems
-        self.used = 0
+    def __init__(self, spare):
+        self.spare = spare
         self.pending = []
 
     def remote(self, src, dst, recv_sem, group, place, when=None):
-        assert self.used < self.sems.shape[0]
+        number = self.spare.free.pop(0)
         copy = pltpu.make_async_remote_copy(
             src_ref=src,
             dst_ref=dst,
-            send_sem=self.sems.at[self.used],
+            send_sem=self.spare.sems.at[number],
             recv_sem=recv_sem,
             device_id=(group, place),
             device_id_type=MESH,
         )
-        self.used += 1
-        self.pending.append((copy, when))
+        self.pending.append((copy, when, number))
         if when is None:
             copy.start()
         else:
@@ -302,12 +307,15 @@
         return self.pending[-1]
 
     def settle(self, entry):
+        if not any(other is entry for other in self.pending):
+            return
         self.pending = [other for other in self.pending if other is not entry]
-        copy, when = entry
+        copy, when, number = entry
         if when is None:
             copy.wait_send()
         else:
             pl.when(when)(copy.wait_send)
+        self.spare.free.append(number)
 
     def finish(self):
         while self.pending:
@@ -477,8 +485,9 @@
             pour(two, write, self.rows // 16)
 
         if way in self.queue:
-            self.copies.settle(self.queue.pop(way))
-        self.queue[way] = self.push(chip, way, end)
+            copies, entry = self.queue.pop(way)
+            copies.settle(entry)
+        self.queue[way] = (self.copies, self.push(chip, way, end))
 
     def start(self, i):
         self.pass_on(3 - i, 0)
@@ -532,30 +541,88 @@
     return ((first + lax.broadcasted_iota(jnp.int32, (count, 1), 0)) < length).astype(jnp.float32)
 
 
-def forward_part(
+def slope(values):
+    sigma = 1.0 / (1.0 + jnp.exp(-values))
+    return sigma * (1.0 + values * (1.0 - sigma))
+
+
+def turned_table(rate, length):
+    offset = lax.broadcasted_iota(jnp.int32, (length, length), 1) - lax.broadcasted_iota(jnp.int32, (length, length), 0)
+    steps = jnp.maximum(offset, 0).astype(jnp.float32)
+    return jnp.where(offset >= 0, jnp.exp(-rate * steps), 0.0)
+
+
+def columns_of(out, tiles, b, rows):
+    for owner in range(8):
+        out[pl.ds(owner * rows, rows)] = jnp.broadcast_to(tiles[b, owner, :1], (128, 128)).T[:rows]
+
+
+def turn(dst, read, count, columns):
+    def block(i, carry):
+        dst[pl.ds(0, columns), aligned(i, 128, 128)] = read(aligned(i, 128, 128)).T
+        return carry
+
+    lax.fori_loop(0, count, block, 0)
+
+
+def tiles_of(width, body):
+    def tile(i, carry):
+        body(aligned(i, 256, 256), i)
+        return carry
+
+    lax.fori_loop(0, width // 256, tile, 0)
+
+
+def layer_part(
     lengths, decay, x, cot, wq, wk, wv, wu, wo, w1, w2, w3,
-    n1_all, dm_all, n2_all, q_all, k_all, v_all, u_all, o_all, f_all, s_all, t_all, pre_all, h, scale_all,
-    w1_t, w2_t, send, own, hop_n, side_n, hop_d, side_d, hop_m, side_m, z_head, z_out, z_ff, xy_head, xy_out, xy_ff,
-    n1, dm, n2, n1_v, w_v, wo_v, load, pre_v, pre_sem, part, side, inbox, side_sem, line_sem,
-    table, squares, inbox_sq, scale, sq_sem, sc_sem, column,
+    out, grad_x, fq, fk, fv, fu, fo, ff_, fs, ft,
+    n1_all, dm_all, n2_all, da_all, q_all, k_all, v_all, u_all, o_all, f_all, s_all, t_all, pre_all, in_f, in_t, in_o, in_h,
+    send, load, own, hop_n, side_n, hop_d, side_d, hop_m, side_m_, hop_a, side_a, z_head, z_out, z_ff, xy_head, xy_out, xy_ff,
+    n1, dm, n2, da, h, a_v, b_v, w_v, wa_v, wo_v, p_v, turned, part, side, inbox, side_sem, line_sem,
+    side_m, inbox_m, side_sem_m, line_sem_m, table, squares, inbox_sq, scale, scale_in, sq_sem, sc_sem, column,
+    mix, mix_in, mix_sem, inverse, mixed, pre, pre_sem, go_v, grads_h,
+    xy_f, xy_t, xy_o, xy_h, z_f, z_t, z_o, z_h,
 ):
     g, s, y, x_, z, c = where_am_i()
     others = across(y, x_)
-    greet(line_partners(g, s) + [(o, s) for o in others])
-    copies = Copies(send)
+    plane = [(o, 2 * z + e) for o in others for e in range(2)]
     rows, width = x.shape[1], x.shape[2]
     length = 8 * rows
-    gather_n = Gather(copies, n1_all, rows, hop_n, side_n)
-    gather_d = Gather(copies, dm_all, rows, hop_d, side_d)
-    gather_m = Gather(copies, n2_all, rows, hop_m, side_m)
-    heads = list(zip((wq, wk, wv, wu), (q_all, k_all, v_all, u_all)))
+    tokens = 2 * length
     depth, wide = wq.shape
     head = q_all.shape[1] // 2
     ff = f_all.shape[0] // 4
+    hidden = 4 * ff
+    half = length // 2
     target = g // 2
     mine = aligned(g % 2, head, head)
     here = c == target
     order = [(z + d) % 4 for d in (0, 1, 3, 2)]
+    spare = Spare(send)
+    copies, turned_out, bulk, last = [Copies(spare) for _ in range(4)]
+    early, sums = [[Copies(spare) for _ in range(2)] for _ in range(2)]
+    gather_n = Gather(copies, n1_all, rows, hop_n, side_n)
+    gather_d = Gather(copies, dm_all, rows, hop_d, side_d)
+    gather_m = Gather(copies, n2_all, rows, hop_m, side_m_)
+    gather_a = Gather(last, da_all, rows, hop_a, side_a)
+    heads = list(zip((wq, wk, wv, wu), (q_all, k_all, v_all, u_all)))
+    w1_f, w2_f, w3_f = [w_v.at[pl.ds(n * hidden, hidden)] for n in range(3)]
+    w1_in, w2_in = [w_v.at[pl.ds(n * depth, depth), pl.ds(512, 2 * hidden)] for n in range(2)]
+    w1_t, w2_t = [w_v.at[pl.ds(0, 2 * hidden), pl.ds(n * depth, depth)] for n in range(2)]
+    low_v = p_v.at[2, pl.ds(0, length), pl.ds(0, 2 * head)]
+
+    def at_b(b):
+        return pl.ds(b * length, length)
+
+    def dz(n, at):
+        return p_v.at[n // 2, at, pl.ds((n % 2) * 2 * head, 2 * head)]
+
+    def nat_v(at):
+        return p_v.at[2, at, pl.ds(0, 2 * head)]
+
+    local(w1, w1_in, load.at[0])
+    local(w2, w2_in, load.at[1])
+    greet(line_partners(g, s) + plane)
 
     def send_heads(n):
         src, dst = heads[n]
@@ -599,15 +666,19 @@
             a = src.at[aligned(to, ff, 16)]
             b = dst.at[aligned(g, ff, 16), aligned(s, depth, 128)]
             if d:
-                copies.remote(a, b, z_ff.at[n, z], g, to)
+                turned_out.remote(a, b, z_ff.at[n, z], g, to)
             else:
                 local(a, b, z_ff.at[n, z])
+
+    def arrive_ff(n):
+        dst = (f_all, s_all)[n]
+        for zs in order:
+            arrived(dst.at[aligned(g, ff, 16), aligned(zs, 2 * depth, 128)], z_ff.at[n, zs])
 
     def pass_ff(n):
         dst = (f_all, s_all)[n]
         for zs in order:
             block = dst.at[aligned(g, ff, 16), aligned(zs, 2 * depth, 128)]
-            arrived(block, z_ff.at[n, zs])
             for r, o in enumerate(others):
                 copies.remote(block, block, xy_ff.at[n, r, zs], o, s)
 
@@ -651,7 +722,8 @@
             return carry
 
         lax.fori_loop(0, rows // 16, masked, 0)
-    for src, dst in ((w1, w1_t), (w2, w2_t)):
+    for n, (src, dst) in enumerate(((w1_in, w1_t), (w2_in, w2_t))):
+        arrived(src, load.at[n])
         dst[...] = src[...].T
     pass_heads(0)
     send_heads(2)
@@ -662,14 +734,20 @@
     pass_heads(3)
     send_out()
     send_ff(1)
+    for n in range(2):
+        arrive_ff(n)
+        if n == 0:
+            for b in range(2):
+                gather_n.begin(n1.at[b], own.at[0, b], b)
+            pass_out()
+    gather_n.step(0, 1)
+    gather_n.step(1, 1)
     pass_ff(0)
-    for b in range(2):
-        gather_n.begin(n1.at[b], own.at[0, b], b)
-    pass_out()
+    gather_n.step(0, 2)
+    gather_n.step(1, 2)
     pass_ff(1)
-    for k in (1, 2, 3):
-        gather_n.step(0, k)
-        gather_n.step(1, k)
+    gather_n.step(0, 3)
+    gather_n.step(1, 3)
     send_third()
     for r, o in enumerate(others):
         from_here = (o // 2) == c
@@ -679,78 +757,70 @@
                 arrived(block, xy_head.at[n, r, zs], from_here)
         arrived(o_all.at[:, aligned(o, wide, 128)], xy_out.at[r])
     for n, (_, dst) in enumerate(heads):
-        local(dst, w_v.at[n], load.at[n])
+        local(dst, wa_v.at[n], load.at[n])
     local(o_all, wo_v, load.at[4])
     for b in range(2):
         gather_n.finish(own.at[0, b], b)
-        local(n1_all.at[b], n1_v.at[b], load.at[5 + b])
+        local(n1_all.at[b], a_v.at[at_b(b)], load.at[5 + b])
     for j in range(2):
         table[j] = decay_table(decay[4 * (2 * c + j) + z], length)
     for n in range(4):
-        arrived(w_v.at[n], load.at[n])
+        arrived(wa_v.at[n], load.at[n])
     arrived(wo_v, load.at[4])
-    queue = {}
-    scatters = [
-        LineScatter(copies, part.at[b], rows, side.at[b], inbox.at[b], side_sem.at[b], line_sem.at[b], queue) for b in range(2)
-    ]
-    half = length // 2
+
+    def scatters_of(copies, first, queue):
+        kept = (side, inbox, side_sem, line_sem) if first else (side_m, inbox_m, side_sem_m, line_sem_m)
+        return [LineScatter(copies[b], part.at[b], rows, *[k.at[b] for k in kept], queue) for b in range(2)]
+
+    scatters = scatters_of(early, True, {})
     for b in range(2):
-        arrived(n1_v.at[b], load.at[5 + b])
+        arrived(a_v.at[at_b(b)], load.at[5 + b])
+        if b == 1:
+            for j in range(2):
+                arrived(pre.at[j], pre_sem.at[j])
 
         def project(i, carry):
             at = aligned(i, half, 16)
+            from_ = aligned(2 * b + i, half, 16)
             for n in range(4):
-                pre_v[n, b, at] = product(n1_v[b, at], w_v[n])
+                value = product(a_v[from_], wa_v[n])
+                for j in range(2):
+                    pre[j, n, at] = value[:, j * head : (j + 1) * head]
             return carry
 
         lax.fori_loop(0, 2, project, 0)
         if b == 1:
             scatters[0].start(1)
         live = live_rows(0, length, lengths[0, b])
+        square = 0.0
         for j in range(2):
-            lanes = pl.ds(j * head, head)
-            q = silu(pre_v[0, b, :, lanes]).astype(jnp.bfloat16)
-            k = (silu(pre_v[1, b, :, lanes]) * live).astype(jnp.bfloat16)
-            v = (silu(pre_v[2, b, :, lanes]) * live).astype(jnp.bfloat16)
+            q = silu(pre[j, 0]).astype(jnp.bfloat16)
+            k = (silu(pre[j, 1]) * live).astype(jnp.bfloat16)
+            v = (silu(pre[j, 2]) * live).astype(jnp.bfloat16)
             scores = (product_right(q, k) * table[j]).astype(jnp.bfloat16)
-            pre_v[4, b, :, lanes] = product(scores, v)
-        gated = silu(pre_v[3, b]) * pre_v[4, b]
-        square = jnp.sum(gated * gated, axis=-1, keepdims=True)
+            attended = product(scores, v)
+            pre[j, 4] = attended
+            gated = silu(pre[j, 3]) * attended
+            square = square + jnp.sum(gated * gated, axis=-1, keepdims=True)
+            low_v[:, pl.ds(j * head, head)] = gated.astype(jnp.bfloat16)
+            local(pre.at[j], pre_all.at[b, j], pre_sem.at[j])
         row = jnp.broadcast_to(square, (length, 128)).T[:8]
         for to in range(8):
             squares[b, to, :, :rows] = row[:, to * rows : (to + 1) * rows]
         everyone_on_line(copies, squares, inbox_sq.at[b], sq_sem.at[b], g, s, lambda to: squares.at[b, to])
         local(squares.at[b, s], inbox_sq.at[b, s], sq_sem.at[b, 7])
-        low = gated.astype(jnp.bfloat16)
 
         def out_part(i, carry):
             at = aligned(i, 256, 256)
-            part[b, :, at] = product(low, wo_v[:, at]).astype(jnp.bfloat16)
+            part[b, :, at] = product(low_v[...], wo_v[:, at]).astype(jnp.bfloat16)
             return carry
 
         lax.fori_loop(0, width // 256, out_part, 0)
         scatters[b].begin()
         if b == 0:
             scatters[0].start(0)
-    local(pre_v, pre_all, pre_sem)
-    for b in range(2):
-        gather_d.begin(dm.at[b], own.at[1, b], b)
-    scatters[0].hop(0)
-    scatters[0].start(2)
-    scatters[0].hop(1)
-    scatters[1].start(0)
-    scatters[0].hop(2)
-    gather_d.step(0, 1)
-    gather_d.step(1, 1)
-    scatters[1].start(1)
-    scatters[1].hop(0)
-    pass_third()
-    scatters[1].start(2)
-    scatters[1].hop(1)
-    gather_d.step(0, 2)
-    scatters[1].hop(2)
-    gather_d.step(1, 2)
-    for b in range(2):
+
+    def hidden_state(b):
         for d in range(8):
             arrived(inbox_sq.at[b, 0], sq_sem.at[b, d])
         total = inbox_sq[b, 0]
@@ -759,7 +829,6 @@
         row = lax.rsqrt(total / width + EPS)
         scale[b] = row
         column[b] = jnp.broadcast_to(row[:1], (128, 128)).T
-    for b in range(2):
         scatter = scatters[b]
         scatter.receive()
 
@@ -767,118 +836,60 @@
             piece = aligned(i, 16, 16)
             at = aligned(b * (rows // 16) + i, 16, 16)
             a = scatter.total(piece) * column[b, piece, :1]
-            hidden = x[b, piece].astype(jnp.float32) + a
-            h[at] = hidden
-            n2[b, piece] = (hidden * lax.rsqrt(mean_square(hidden) + EPS)).astype(jnp.bfloat16)
+            value = x[b, piece].astype(jnp.float32) + a
+            h[at] = value
+            n2[b, piece] = (value * lax.rsqrt(mean_square(value) + EPS)).astype(jnp.bfloat16)
             return carry
 
         lax.fori_loop(0, rows // 16, finish, 0)
         gather_m.begin(n2.at[b], own.at[2, b], b)
+
+    gather_d.begin(dm.at[0], own.at[1, 0], 0)
+    scatters[0].hop(0)
+    scatters[0].start(2)
+    scatters[0].hop(1)
+    scatters[1].start(0)
+    scatters[0].hop(2)
+    gather_d.step(0, 1)
+    hidden_state(0)
+    scatters[1].start(1)
+    scatters[1].hop(0)
+    pass_third()
+    gather_d.step(0, 2)
+    scatters[1].start(2)
+    scatters[1].hop(1)
+    gather_m.step(0, 1)
+    scatters[1].hop(2)
+    gather_d.step(0, 3)
+    gather_m.step(0, 2)
+    gather_d.begin(dm.at[1], own.at[1, 1], 1)
+    hidden_state(1)
+    gather_m.step(0, 3)
+    gather_d.finish(own.at[1, 0], 0)
+    local(dm_all.at[0], b_v.at[at_b(0)], load.at[2])
+    gather_m.finish(own.at[2, 0], 0)
+    local(n2_all.at[0], a_v.at[at_b(0)], load.at[0])
+    gather_d.step(1, 1)
+    gather_m.step(1, 1)
+    turned_out.finish()
+    for n, (dst, room) in enumerate(((f_all, w1_f), (s_all, w2_f), (t_all, w3_f))):
+        for r, o in enumerate(others):
+            for zs in range(4):
+                if n < 2:
+                    block = dst.at[aligned(o, ff, 16), pl.ds(zs * 2 * depth, 2 * depth)]
+                else:
+                    block = dst.at[pl.ds(zs * ff, ff), aligned(o, wide, 128)]
+                arrived(block, xy_ff.at[n, r, zs])
+        local(dst, room, load.at[4 + n])
     for b in range(2):
-        for d in range(1, 8):
-            copies.remote(scale.at[b], scale_all.at[b, s], sc_sem.at[b, d - 1], g, (s + d) % 8)
-        local(scale.at[b], scale_all.at[b, s], sc_sem.at[b, 7])
-    gather_d.step(0, 3)
-    gather_d.step(1, 3)
-    for k in (1, 2, 3):
-        gather_m.step(0, k)
-        gather_m.step(1, k)
-
-    for b in range(2):
-        gather_d.finish(own.at[1, b], b)
-        gather_m.finish(own.at[2, b], b)
-    for r, o in enumerate(others):
-        for n, dst in enumerate((f_all, s_all)):
-            for zs in range(4):
-                arrived(dst.at[aligned(o, ff, 16), pl.ds(zs * 2 * depth, 2 * depth)], xy_ff.at[n, r, zs])
-        for zs in range(4):
-            arrived(t_all.at[pl.ds(zs * ff, ff), aligned(o, wide, 128)], xy_ff.at[2, r, zs])
-    for b in range(2):
-        for d in range(8):
-            arrived(scale.at[b], sc_sem.at[b, d])
-    arrived(pre_v, pre_sem)
-    copies.finish()
-
-
-def slope(values):
-    sigma = 1.0 / (1.0 + jnp.exp(-values))
-    return sigma * (1.0 + values * (1.0 - sigma))
-
-
-def turned_table(rate, length):
-    offset = lax.broadcasted_iota(jnp.int32, (length, length), 1) - lax.broadcasted_iota(jnp.int32, (length, length), 0)
-    steps = jnp.maximum(offset, 0).astype(jnp.float32)
-    return jnp.where(offset >= 0, jnp.exp(-rate * steps), 0.0)
-
-
-def columns_of(out, tiles, b, rows):
-    for owner in range(8):
-        out[pl.ds(owner * rows, rows)] = jnp.broadcast_to(tiles[b, owner, :1], (128, 128)).T[:rows]
-
-
-def turn(dst, read, count, columns):
-    def block(i, carry):
-        dst[pl.ds(0, columns), aligned(i, 128, 128)] = read(aligned(i, 128, 128)).T
-        return carry
-
-    lax.fori_loop(0, count, block, 0)
-
-
-def tiles_of(width, body):
-    def tile(i, carry):
-        body(aligned(i, 256, 256), i)
-        return carry
-
-    lax.fori_loop(0, width // 256, tile, 0)
-
-
-def backward_part(
-    lengths, decay, x, cot, h, n1_all, dm_all, n2_all, q_all, k_all, v_all, u_all, o_all, f_all, s_all, t_all, pre_all, scale_all,
-    da_all, mix_all, out, grad_x, fq, fk, fv, fu, fo, ff_, fs, ft, in_f, in_t, in_o, in_h,
-    send_a, send_b, send_c, send_d, load, own, hop, hside,
-    a_v, b_v, w_v, wa_v, wo_v, p_v, turned, part, side, inbox, side_sem, line_sem, side_m, inbox_m, side_sem_m, line_sem_m,
-    scale, mix, mix_in, mix_sem, column, inverse, mixed, da, table, pre, dz, nat_v, go_v, grads_h,
-    xy_f, xy_t, xy_o, xy_h, z_f, z_t, z_o, z_h,
-):
-    g, s, y, x_, z, c = where_am_i()
-    others = across(y, x_)
-    plane = [(o, 2 * z + e) for o in others for e in range(2)]
-    rows, width = x.shape[1], x.shape[2]
-    length = 8 * rows
-    tokens = 2 * length
-    ff = in_f.shape[2]
-    hidden = 4 * ff
-    head = dz.shape[2] // 2
-    wide, depth = fo.shape[1], fo.shape[0]
-
-    def at_b(b):
-        return pl.ds(b * length, length)
-
-    for b in range(2):
-        local(n2_all.at[b], a_v.at[at_b(b)], load.at[b])
-        local(dm_all.at[b], b_v.at[at_b(b)], load.at[2 + b])
-    for n, src in enumerate((f_all, s_all, t_all)):
-        local(src, w_v.at[pl.ds(n * hidden, hidden)], load.at[4 + n])
-    for n, src in enumerate((q_all, k_all, v_all, u_all)):
-        local(src, wa_v.at[n], load.at[7 + n])
-    local(o_all, wo_v, load.at[11])
-    local(scale_all, scale, load.at[12])
-    greet(line_partners(g, s) + plane)
-    sums = Copies(send_a)
-    bulk = Copies(send_b)
-    last = Copies(send_c)
-    early = Copies(send_d)
-    gather = Gather(last, da_all, rows, hop, hside)
-    w1 = w_v.at[pl.ds(0, hidden)]
-    w2 = w_v.at[pl.ds(hidden, hidden)]
-    w3 = w_v.at[pl.ds(2 * hidden, hidden)]
+        early[b].finish()
 
     def feed_forward(b):
         def tile(i, carry):
-            at = aligned(b * 2 + i, length // 2, 16)
-            first = product_right(a_v[at], w1[...])
-            second = product_right(a_v[at], w2[...])
-            back = product_right(b_v[at], w3[...])
+            at = aligned(b * 2 + i, half, 16)
+            first = product_right(a_v[at], w1_f[...])
+            second = product_right(a_v[at], w2_f[...])
+            back = product_right(b_v[at], w3_f[...])
             p_v[0, at] = (back * second).astype(jnp.bfloat16)
             p_v[1, at] = (back * first).astype(jnp.bfloat16)
             p_v[2, at] = (first * second).astype(jnp.bfloat16)
@@ -888,39 +899,16 @@
 
     def norm_part(b):
         def body(at, i):
-            value = product(p_v[0, at_b(b)], w1[:, at]) + product(p_v[1, at_b(b)], w2[:, at])
+            value = product(p_v[0, at_b(b)], w1_f[:, at]) + product(p_v[1, at_b(b)], w2_f[:, at])
             part[b, :, at] = value.astype(jnp.bfloat16)
 
         tiles_of(width, body)
 
-    def scatter_of(b, copies):
-        return LineScatter(copies, part.at[b], rows, side.at[b], inbox.at[b], side_sem.at[b], line_sem.at[b], queue)
-
-    def scatter_m_of(b, copies):
-        return LineScatter(
-            copies, part.at[b], rows, side_m.at[b], inbox_m.at[b], side_sem_m.at[b], line_sem_m.at[b], queue_m
-        )
-
-    queue, queue_m = {}, {}
-    second = [scatter_of(b, early) for b in range(2)]
-    for n in (0, 4, 5, 2, 6):
-        ref = {0: a_v.at[at_b(0)], 2: b_v.at[at_b(0)], 4: w1, 5: w2, 6: w3}[n]
-        arrived(ref, load.at[n])
-    feed_forward(0)
-    norm_part(0)
-    second[0].begin()
-    second[0].start(0)
-    arrived(a_v.at[at_b(1)], load.at[1])
-    arrived(b_v.at[at_b(1)], load.at[3])
-    feed_forward(1)
-    second[0].start(1)
-    second[0].hop(0)
-    norm_part(1)
-    second[1].begin()
-    second[0].start(2)
-    second[0].hop(1)
-    second[0].hop(2)
-    second[1].start(0)
+    def mixed_part(b):
+        def body(at, i):
+            part[b, :, at] = product(p_v[2, at_b(b)], w3_f[:, at]).astype(jnp.bfloat16)
+
+        tiles_of(width, body)
 
     def weight_part(n, operand):
         turn(turned, lambda t: p_v[n, t], tokens // 128, hidden)
@@ -935,26 +923,16 @@
             else:
                 bulk.remote(w_v.at[pl.ds(n * hidden, hidden), aligned(o, wide, 128)], in_t.at[r], xy_t.at[r], o, s)
 
-    weight_part(0, a_v)
-    second[1].start(1)
-    second[1].hop(0)
-    weight_part(1, a_v)
-    second[1].start(2)
-    second[1].hop(1)
-    second[1].hop(2)
-
-    for b in range(2):
-        second[b].receive()
+    def hidden_gradient(b):
         scatter = second[b]
-        if b == 1:
-            queue.clear()
+        scatter.receive()
 
         def finish(i, carry):
             piece = aligned(i, 16, 16)
             at = aligned(b * (rows // 16) + i, 16, 16)
-            hidden_state = h[at]
-            scale_h = lax.rsqrt(mean_square(hidden_state) + EPS)
-            normed = hidden_state * scale_h
+            value = h[at]
+            scale_h = lax.rsqrt(mean_square(value) + EPS)
+            normed = value * scale_h
             grad = scatter.total(piece)
             along = jnp.mean(normed * grad, axis=-1, keepdims=True)
             live = live_rows(s * rows + i * 16, 16, lengths[0, b])
@@ -963,45 +941,141 @@
             grad_x[at] = grad_hidden
             low = grad_hidden.astype(jnp.bfloat16)
             da[b, piece] = low
-            dot = jnp.mean(low.astype(jnp.float32) * (hidden_state - x[b, piece].astype(jnp.float32)), axis=-1, keepdims=True)
+            dot = jnp.mean(low.astype(jnp.float32) * (value - x[b, piece].astype(jnp.float32)), axis=-1, keepdims=True)
             column[b, piece] = jnp.broadcast_to(dot, (16, 128))
             return carry
 
         lax.fori_loop(0, rows // 16, finish, 0)
-        gather.begin(da.at[b], own.at[b], b)
+        gather_a.begin(da.at[b], own.at[3, b], b)
         mix[b, :, :rows] = column[b].T[:8, :rows]
         for d in range(1, 8):
             last.remote(mix.at[b], mix_in.at[b, s], mix_sem.at[b, d - 1], g, (s + d) % 8)
         local(mix.at[b], mix_in.at[b, s], mix_sem.at[b, 7])
-    early.finish()
-
-    third = [scatter_m_of(b, sums) for b in range(2)]
+
+    second = scatters_of(early, True, {})
+    for n in (0, 4, 5, 2, 6):
+        ref = {0: a_v.at[at_b(0)], 2: b_v.at[at_b(0)], 4: w1_f, 5: w2_f, 6: w3_f}[n]
+        arrived(ref, load.at[n])
+    feed_forward(0)
+    gather_m.step(1, 2)
+    gather_d.step(1, 2)
+    norm_part(0)
+    second[0].begin()
+    second[0].start(0)
+    gather_m.step(1, 3)
+    gather_d.step(1, 3)
+    gather_d.finish(own.at[1, 1], 1)
+    local(dm_all.at[1], b_v.at[at_b(1)], load.at[3])
+    gather_m.finish(own.at[2, 1], 1)
+    local(n2_all.at[1], a_v.at[at_b(1)], load.at[1])
     for b in range(2):
-
+        for d in range(1, 8):
+            copies.remote(scale.at[b], scale_in.at[b, s], sc_sem.at[b, d - 1], g, (s + d) % 8)
+        local(scale.at[b], scale_in.at[b, s], sc_sem.at[b, 7])
+    second[0].start(1)
+    second[0].hop(0)
+    arrived(a_v.at[at_b(1)], load.at[1])
+    arrived(b_v.at[at_b(1)], load.at[3])
+    feed_forward(1)
+    second[0].start(2)
+    second[0].hop(1)
+    second[0].hop(2)
+    norm_part(1)
+    def load_pre(b, j):
+        local(pre_all.at[b, j], pre.at[j], pre_sem.at[j])
+
+    def attention_back(b):
+        gather_a.finish(own.at[3, b], b)
+        local(da_all.at[b], a_v.at[at_b(b)], load.at[b])
+        for d in range(8):
+            arrived(mix_in.at[b, 0], mix_sem.at[b, d])
+        columns_of(mixed, mix_in, b, rows)
+        live = live_rows(0, length, lengths[0, b])
+        arrived(a_v.at[at_b(b)], load.at[b])
+        for j in range(2):
+            arrived(pre.at[j], pre_sem.at[j])
+            lanes = pl.ds(j * head, head)
+            error = product_right(a_v[at_b(b)], wo_v[pl.ds(j * head, head)])
+            q_pre, k_pre, v_pre, u_pre, o = [pre[j, n] for n in range(5)]
+            sigma = 1.0 / (1.0 + jnp.exp(-u_pre))
+            u = u_pre * sigma
+            scale_g = inverse[at_b(b), :1]
+            nat = u * o * scale_g
+            nat_v(at_b(b))[:, lanes] = nat.astype(jnp.bfloat16)
+            dg = scale_g * (error - nat * mixed[:, :1])
+            dz(3, at_b(b))[:, lanes] = (dg * o * (sigma * (1.0 + u_pre * (1.0 - sigma)))).astype(jnp.bfloat16)
+            do = (dg * u).astype(jnp.bfloat16)
+            q = silu(q_pre).astype(jnp.bfloat16)
+            k = (silu(k_pre) * live).astype(jnp.bfloat16)
+            v = (silu(v_pre) * live).astype(jnp.bfloat16)
+            scores = (product_right(k, q) * table[j]).astype(jnp.bfloat16)
+            dv = product(scores, do)
+            d_scores = (product_right(v, do) * table[j]).astype(jnp.bfloat16)
+            dk = product(d_scores, q)
+            dq = product_left(d_scores, k)
+            dz(0, at_b(b))[:, lanes] = (dq * slope(pre[j, 0])).astype(jnp.bfloat16)
+            dz(1, at_b(b))[:, lanes] = (dk * live * slope(pre[j, 1])).astype(jnp.bfloat16)
+            dz(2, at_b(b))[:, lanes] = (dv * live * slope(pre[j, 2])).astype(jnp.bfloat16)
+            if b == 0:
+                load_pre(1, j)
+
+    def first_part(b):
         def body(at, i):
-            part[b, :, at] = product(p_v[2, at_b(b)], w3[:, at]).astype(jnp.bfloat16)
+            value = product_right(dz(0, at_b(b))[...], wa_v[0, at])
+            for n in range(1, 4):
+                value = value + product_right(dz(n, at_b(b))[...], wa_v[n, at])
+            part[b, :, at] = value.astype(jnp.bfloat16)
 
         tiles_of(width, body)
-        third[b].begin()
+
+    second[1].begin()
+    second[1].start(0)
+    hidden_gradient(0)
+    weight_part(0, a_v)
+    second[1].start(1)
+    second[1].hop(0)
+    gather_a.step(0, 1)
+    third = scatters_of(sums, False, {})
+    early[0].finish()
+    mixed_part(0)
+    third[0].begin()
     third[0].start(0)
-    gather.step(0, 1)
-    gather.step(1, 1)
+    second[1].start(2)
+    second[1].hop(1)
+    second[1].hop(2)
     third[0].start(1)
     third[0].hop(0)
-    weight_part(2, b_v)
-    gather.step(0, 2)
+    gather_a.step(0, 2)
+    weight_part(1, a_v)
+    hidden_gradient(1)
     third[0].start(2)
     third[0].hop(1)
+    gather_a.step(0, 3)
     third[0].hop(2)
+    early[1].finish()
+    mixed_part(1)
+    third[1].begin()
     third[1].start(0)
-    gather.step(1, 2)
+    for j in range(2):
+        table[j] = turned_table(decay[4 * (2 * c + j) + z], length)
+    for b in range(2):
+        for d in range(8):
+            arrived(scale.at[b], sc_sem.at[b, d])
+        columns_of(inverse.at[at_b(b)], scale_in, b, rows)
+
+    for j in range(2):
+        arrived(pre.at[j], pre_sem.at[j])
+        load_pre(0, j)
+    gather_a.step(1, 1)
     third[1].start(1)
     third[1].hop(0)
-    gather.step(0, 3)
+    weight_part(2, b_v)
+    gather_a.step(1, 2)
     third[1].start(2)
     third[1].hop(1)
     third[1].hop(2)
-    gather.step(1, 3)
+    attention_back(0)
+    gather_a.step(1, 3)
     for b in range(2):
         third[b].receive()
         scatter = third[b]
@@ -1013,15 +1087,6 @@
             return carry
 
         lax.fori_loop(0, rows // 16, result, 0)
-    for j in range(2):
-        table[j] = turned_table(decay[4 * (2 * c + j) + z], length)
-    arrived(scale, load.at[12])
-    for b in range(2):
-        columns_of(inverse.at[at_b(b)], scale, b, rows)
-    for n in range(4):
-        arrived(wa_v.at[n], load.at[7 + n])
-    arrived(wo_v, load.at[11])
-
     def sum_ff(n, result):
         for r in range(3):
             arrived(in_f.at[n, r], xy_f.at[n, r])
@@ -1078,89 +1143,27 @@
                 last.remote(src, dst, z_t.at[s % 4], g, to, to != s)
                 local(src, dst, z_t.at[s % 4], to == s)
 
+    for b in range(2):
+        sums[b].finish()
+    fourth = scatters_of(early, True, {})
+    first_part(0)
+    fourth[0].begin()
+    fourth[0].start(0)
     sum_ff(0, ff_)
+    fourth[0].start(1)
+    fourth[0].hop(0)
+    attention_back(1)
     sum_ff(1, fs)
-
-    sums.finish()
-    queue = {}
-    fourth = [scatter_of(b, early) for b in range(2)]
-
-    def load_pre(b, j, slot):
-        local(pre_all.at[:, b, :, pl.ds(j * head, head)], pre.at[slot], load.at[16 + slot])
-
-    load_pre(0, 0, 0)
-    load_pre(0, 1, 1)
-    for b in range(2):
-        gather.finish(own.at[b], b)
-        local(da_all.at[b], a_v.at[at_b(b)], load.at[b])
-        for d in range(8):
-            arrived(mix_in.at[b, 0], mix_sem.at[b, d])
-        columns_of(mixed, mix_in, b, rows)
-        live = live_rows(0, length, lengths[0, b])
-        arrived(a_v.at[at_b(b)], load.at[b])
-        for j in range(2):
-            arrived(pre.at[j], load.at[16 + j])
-            lanes = pl.ds(j * head, head)
-            error = product_right(a_v[at_b(b)], wo_v[pl.ds(j * head, head)])
-            q_pre, k_pre, v_pre, u_pre, o = [pre[j, n] for n in range(5)]
-            sigma = 1.0 / (1.0 + jnp.exp(-u_pre))
-            u = u_pre * sigma
-            scale_g = inverse[at_b(b), :1]
-            nat = u * o * scale_g
-            nat_v[at_b(b), lanes] = nat.astype(jnp.bfloat16)
-            dg = scale_g * (error - nat * mixed[:, :1])
-            dz[3, at_b(b), lanes] = (dg * o * (sigma * (1.0 + u_pre * (1.0 - sigma)))).astype(jnp.bfloat16)
-            do = (dg * u).astype(jnp.bfloat16)
-            q = silu(q_pre).astype(jnp.bfloat16)
-            k = (silu(k_pre) * live).astype(jnp.bfloat16)
-            v = (silu(v_pre) * live).astype(jnp.bfloat16)
-            scores = (product_right(k, q) * table[j]).astype(jnp.bfloat16)
-            dv = product(scores, do)
-            d_scores = (product_right(v, do) * table[j]).astype(jnp.bfloat16)
-            dk = product(d_scores, q)
-            dq = product_left(d_scores, k)
-            dz[0, at_b(b), lanes] = (dq * slope(pre[j, 0])).astype(jnp.bfloat16)
-            dz[1, at_b(b), lanes] = (dk * live * slope(pre[j, 1])).astype(jnp.bfloat16)
-            dz[2, at_b(b), lanes] = (dv * live * slope(pre[j, 2])).astype(jnp.bfloat16)
-            if b == 0:
-                load_pre(1, j, j)
-
-        def body(at, i):
-            value = product_right(dz[0, at_b(b)], wa_v[0, at])
-            for n in range(1, 4):
-                value = value + product_right(dz[n, at_b(b)], wa_v[n, at])
-            part[b, :, at] = value.astype(jnp.bfloat16)
-
-        tiles_of(width, body)
-        fourth[b].begin()
-        if b == 0:
-            fourth[0].start(0)
-        else:
-            fourth[0].start(1)
-            fourth[0].hop(0)
-    sum_third()
-    fourth[0].start(2)
-    fourth[0].hop(1)
-    fourth[0].hop(2)
-    fourth[1].start(0)
+    first_part(1)
+    fourth[1].begin()
 
     for b in range(2):
         local(n1_all.at[b], b_v.at[at_b(b)], load.at[2 + b])
-    turn(turned, lambda t: nat_v[t], tokens // 128, 2 * head)
-
-    def body_o(at, i):
-        go_v[:, at] = product(turned[pl.ds(0, 2 * head)], a_v[:, at]).astype(jnp.bfloat16)
-
-    tiles_of(width, body_o)
-    for r, o in enumerate(others):
-        last.remote(go_v.at[:, aligned(o, wide, 128)], in_o.at[r], xy_o.at[r], o, s)
-    fourth[1].start(1)
-    fourth[1].hop(0)
     for b in range(2):
         arrived(b_v.at[at_b(b)], load.at[2 + b])
     half = width // 2
     for n in range(4):
-        turn(turned, lambda t: dz[n, t], tokens // 128, 2 * head)
+        turn(turned, lambda t: dz(n, t)[...], tokens // 128, 2 * head)
         grad = grads_h.at[n]
 
         def body_h(at, i):
@@ -1178,11 +1181,25 @@
                 else:
                     last.remote(src, dst, xy_h.at[n, r], g, 2 * z + e, jnp.logical_and(holds, c != e))
                     local(src, dst, xy_h.at[n, r], jnp.logical_and(holds, c == e))
-        if n == 0:
-            fourth[1].start(2)
-            fourth[1].hop(1)
-        if n == 1:
-            fourth[1].hop(2)
+        if n == 2:
+            fourth[0].start(2)
+            fourth[0].hop(1)
+    turn(turned, lambda t: nat_v(t)[...], tokens // 128, 2 * head)
+
+    def body_o(at, i):
+        go_v[:, at] = product(turned[pl.ds(0, 2 * head)], a_v[:, at]).astype(jnp.bfloat16)
+
+    tiles_of(width, body_o)
+    for r, o in enumerate(others):
+        last.remote(go_v.at[:, aligned(o, wide, 128)], in_o.at[r], xy_o.at[r], o, s)
+    fourth[0].hop(2)
+    fourth[1].start(0)
+    fourth[1].start(1)
+    fourth[1].hop(0)
+    sum_third()
+    fourth[1].start(2)
+    fourth[1].hop(1)
+    fourth[1].hop(2)
     for b in range(2):
         fourth[b].receive()
         scatter = fourth[b]
@@ -1264,9 +1281,11 @@
     for n, result in enumerate((fq, fk, fv, fu)):
         for d in range(4):
             arrived(result.at[pl.ds(0, head)], z_h.at[n, d])
-    early.finish()
+    for b in range(2):
+        early[b].finish()
     bulk.finish()
     last.finish()
+    copies.finish()
 
 
 def call(kernel, number, ins, outs, scratch, name):
@@ -1277,10 +1296,52 @@
         out_specs=[spec for _, spec in outs],
         scratch_shapes=scratch,
         compiler_params=pltpu.CompilerParams(
-            collective_id=number, has_side_effects=True, vmem_limit_bytes=63 * 2**20
+            collective_id=number, has_side_effects=True, vmem_limit_bytes=64 * 2**20 - 2**17
         ),
         name=name,
     )(*[value for value, _ in ins])
+
+
+def finish_arrays(count, turned_count, *refs):
+    ins, outs, held, done = refs[:count], refs[count : 2 * count], refs[2 * count : 3 * count], refs[3 * count : 4 * count]
+    in_sem, out_sem = refs[4 * count :]
+    for i in range(count):
+        local(ins[i], held[i], in_sem.at[i])
+    for i in range(count):
+        arrived(held[i], in_sem.at[i])
+        if i < 2:
+            local(held[i], outs[i], out_sem.at[i])
+            continue
+        if i < 2 + turned_count:
+            done[i][...] = held[i][...].T.astype(jnp.float32)
+        else:
+
+            def write(at, value):
+                done[i][at] = value
+
+            pour(lambda at: held[i][at].astype(jnp.float32), write, held[i].shape[0] // 16)
+        local(done[i], outs[i], out_sem.at[i])
+    for i in range(count):
+        arrived(outs[i], out_sem.at[i])
+
+
+def finished(out, grad_x, turned, straight):
+    arrays = [out, grad_x] + turned + straight
+    shapes = [jax.ShapeDtypeStruct(v.shape, v.dtype) for v in (out, grad_x)]
+    shapes += [wide_array(*v.shape[::-1]) for v in turned] + [wide_array(*v.shape) for v in straight]
+    count = len(arrays)
+    small = jax.ShapeDtypeStruct((8, 128), jnp.float32)
+    done = [small, small] + shapes[2:]
+    return pl.pallas_call(
+        functools.partial(finish_arrays, count, len(turned)),
+        out_shape=shapes,
+        in_specs=[ANY] * count,
+        out_specs=[ANY] * count,
+        scratch_shapes=[pltpu.VMEM(v.shape, v.dtype) for v in arrays] + [pltpu.VMEM(v.shape, v.dtype) for v in done]
+        + [dma(count), dma(count)],
+        compiler_params=pltpu.CompilerParams(vmem_limit_bytes=62 * 2**20),
+        name="finish_arrays",
+    )(*arrays)
 
 
 def low_array(*shape):
@@ -1314,64 +1375,45 @@
     head = width // decay_rate.shape[0]
     hidden = w_third.shape[0]
     length = 8 * rows
-    s = lax.axis_index("seq")
-    z, c = s // 2, s % 2
     x_low = tokens[:, 0]
-    x = x_low.astype(f32).reshape(2 * rows, width)
     in_smem = pl.BlockSpec(memory_space=pltpu.SMEM)
-
-    (n1_all, dm_all, n2_all, q_w, k_w, v_w, u_w, o_w, f_w, s_w, t_w, pre_all, h, scale_all) = call(
-        forward_part,
+    gathered = low_array(2, length, width)
+    out, grad_x, fq, fk, fv, fu, fo, ff, fs, ft = call(
+        layer_part,
         0,
         [(lengths.T, in_smem), (decay_rate, in_smem), (x_low, VMEM), (cotangent[:, 0], VMEM)]
-        + [(v, ANY) for v in (w_query, w_key, w_value, w_gate, w_out)]
-        + [(w_first, VMEM), (w_second, VMEM), (w_third, ANY)],
-        [(low_array(2, length, width), ANY)] * 3
+        + [(v, ANY) for v in (w_query, w_key, w_value, w_gate, w_out, w_first, w_second, w_third)],
+        [(low_array(2 * rows, width), VMEM), (wide_array(2 * rows, width), VMEM)]
+        + [(low_array(wide, depth), ANY)] * 4 + [(low_array(depth, wide), ANY)]
+        + [(low_array(2 * hidden, depth), ANY)] * 2 + [(low_array(hidden, wide), ANY)]
+        + [(gathered, ANY)] * 4
         + [(low_array(width, 2 * head), ANY)] * 4
         + [(low_array(2 * head, width), ANY)]
         + [(low_array(hidden, width), ANY)] * 3
-        + [(wide_array(5, 2, length, 2 * head), ANY), (wide_array(2 * rows, width), VMEM), (wide_array(2, 8, 8, 128), ANY)],
-        [pltpu.VMEM((2 * hidden, depth), bf16), pltpu.VMEM((2 * hidden, depth), bf16), dma(280), dma(3, 2), dma(2, 2, 3), dma(2, 7), dma(2, 2, 3), dma(2, 7), dma(2, 2, 3), dma(2, 7),
-         dma(4, 4), dma(2), dma(3, 4), dma(4, 3, 4), dma(3), dma(3, 3, 4),
-         pltpu.VMEM((2, rows, width), bf16), pltpu.VMEM((2, rows, width), bf16), pltpu.VMEM((2, rows, width), bf16),
-         pltpu.VMEM((2, length, width), bf16), pltpu.VMEM((4, width, 2 * head), bf16), pltpu.VMEM((2 * head, width), bf16), dma(7),
-         pltpu.VMEM((5, 2, length, 2 * head), f32), dma(),
-         pltpu.VMEM((2, length, width), bf16)] + scatter_scratch(rows, width) + [
-         pltpu.VMEM((2, length, length), f32), pltpu.VMEM((2, 8, 8, 128), f32), pltpu.VMEM((2, 8, 8, 128), f32),
-         pltpu.VMEM((2, 8, 128), f32), dma(2, 8), dma(2, 8), pltpu.VMEM((2, 128, 128), f32)],
-        "forward_part",
-    )
-    da_all, mix_all, out, grad_x, fq, fk, fv, fu, fo, ff, fs, ft, _, _, _, _ = call(
-        backward_part,
-        1,
-        [(lengths.T, in_smem), (decay_rate, in_smem), (x_low, VMEM), (cotangent[:, 0], VMEM), (h, VMEM)]
-        + [(v, ANY) for v in (n1_all, dm_all, n2_all, q_w, k_w, v_w, u_w, o_w, f_w, s_w, t_w, pre_all, scale_all)],
-        [(low_array(2, length, width), ANY), (wide_array(8, 128), VMEM), (low_array(2 * rows, width), VMEM),
-         (wide_array(2 * rows, width), VMEM)]
-        + [(low_array(wide, depth), ANY)] * 4 + [(low_array(depth, wide), ANY)]
-        + [(low_array(2 * hidden, depth), ANY)] * 2 + [(low_array(hidden, wide), ANY)]
+        + [(wide_array(2, 2, 5, length, head), ANY)]
         + [(low_array(2, 3, hidden // 4, width), ANY), (low_array(3, hidden, wide), ANY), (low_array(3, 2 * head, wide), ANY),
            (low_array(4, 4, head, width // 2), ANY)],
-        [dma(40), dma(12), dma(120), dma(70), dma(40), dma(2), dma(2, 2, 3), dma(2, 7),
-         pltpu.VMEM((2 * length, width), bf16), pltpu.VMEM((2 * length, width), bf16), pltpu.VMEM((3 * hidden, width), bf16),
-         pltpu.VMEM((4, width, 2 * head), bf16), pltpu.VMEM((2 * head, width), bf16),
-         pltpu.VMEM((3, 2 * length, hidden), bf16), pltpu.VMEM((hidden, 2 * length), bf16),
-         pltpu.VMEM((2, length, width), bf16)]
+        [dma(360), dma(40), dma(4, 2)] + [dma(2, 2, 3), dma(2, 7)] * 4
+        + [dma(4, 4), dma(2), dma(3, 4), dma(4, 3, 4), dma(3), dma(3, 3, 4)]
+        + [pltpu.VMEM((2, rows, width), bf16)] * 4
+        + [pltpu.VMEM((2 * rows, width), f32),
+           pltpu.VMEM((2 * length, width), bf16), pltpu.VMEM((2 * length, width), bf16), pltpu.VMEM((3 * hidden, width), bf16),
+           pltpu.VMEM((4, width, 2 * head), bf16), pltpu.VMEM((2 * head, width), bf16),
+           pltpu.VMEM((3, 2 * length, hidden), bf16), pltpu.VMEM((hidden, 2 * length), bf16),
+           pltpu.VMEM((2, length, width), bf16)]
         + scatter_scratch(rows, width) + scatter_scratch(rows, width)
-        + [pltpu.VMEM((2, 8, 8, 128), f32), pltpu.VMEM((2, 8, 128), f32), pltpu.VMEM((2, 8, 8, 128), f32), dma(2, 8),
-           pltpu.VMEM((2, 128, 128), f32), pltpu.VMEM((2 * length, 128), f32), pltpu.VMEM((length, 128), f32),
-           pltpu.VMEM((2, rows, width), bf16), pltpu.VMEM((2, length, length), f32), pltpu.VMEM((2, 5, length, head), f32),
-           pltpu.VMEM((4, 2 * length, 2 * head), bf16), pltpu.VMEM((2 * length, 2 * head), bf16),
+        + [pltpu.VMEM((2, length, length), f32), pltpu.VMEM((2, 8, 8, 128), f32), pltpu.VMEM((2, 8, 8, 128), f32),
+           pltpu.VMEM((2, 8, 128), f32), pltpu.VMEM((2, 8, 8, 128), f32), dma(2, 8), dma(2, 8), pltpu.VMEM((2, 128, 128), f32),
+           pltpu.VMEM((2, 8, 128), f32), pltpu.VMEM((2, 8, 8, 128), f32), dma(2, 8),
+           pltpu.VMEM((2 * length, 128), f32), pltpu.VMEM((length, 128), f32),
+           pltpu.VMEM((2, 5, length, head), f32), dma(2),
            pltpu.VMEM((2 * head, width), bf16), pltpu.VMEM((4, 2 * head, width), bf16),
            dma(2, 3), dma(3), dma(3), dma(4, 4), dma(2, 8), dma(4), dma(2), dma(4, 4)],
-        "backward_part",
-    )
-    return (
-        out.reshape(2, 1, rows, width),
-        grad_x.reshape(2, 1, rows, width),
-        fq.T.astype(f32), fk.T.astype(f32), fv.T.astype(f32), fu.T.astype(f32), fo.astype(f32),
-        ff.T.astype(f32), fs.T.astype(f32), ft.astype(f32),
-    )
+        "layer_part",
+    )[:10]
+    results = finished(out, grad_x, [fq, fk, fv, fu, ff, fs], [fo, ft])
+    out, grad_x, fq, fk, fv, fu, ff, fs, fo, ft = results
+    return (out.reshape(2, 1, rows, width), grad_x.reshape(2, 1, rows, width), fq, fk, fv, fu, fo, ff, fs, ft)
 
 
 def solution(mesh):

time: 495 us -> 431 us (0.87)
  Pallas kernels: 475 us -> 430 us
  local copies, waits for them, and re-layouts: 8.84 us -> 0 us
  other arithmetic: 5.88 us -> 0 us
    pallas_call x2 -> x1, Pallas kernels: 475 us -> 425 us  [call(): pl.pallas_call(kernel, out_shape=[shape for shape, _ in outs], in_specs=[...]
    unnamed x18 -> x0, local copies, waits for them, and re-layouts: 8.84 us -> none
    convert_element_type x5 -> x0, other arithmetic: 5.88 us -> none  [the longest x1 1.86 us: line_shards(): fo.astype(f32)]
where the time goes in v5:
time: 431 us
  Pallas kernels  430 us (100%)
    pallas_call x1, Pallas kernels, call(): pl.pallas_call(kernel, out_shape=[shape for shape, _ in outs], in_specs=[...  425 us

profile of v5, /device:TPU:0, one launch (start us, length us, event | category | flops | bytes accessed | tf_op | source)
XLA Modules:
  0.0 430.9 jit_solution(7840836273591009538)
XLA Ops:
  0.6 425.2 %layer_part.1 = (bf16[128,2048]{1,0:T(8,128)(2,1)}, f32[128,2048]{1,0:T(8,128)}, bf16[512,256]{1,0:T(8,128)(2,1)}, bf16[512,256]{1,0:T(8,128)(2,1)}, bf16[512,25...) custom-call(s32[1,2]{1,0:T(1,128)} %bitcast.11, ...), custom_call_target="tpu_custom_call" | custom-call | tf_op jit(solution)/shard_map/layer_part/pallas_call | solution.py:1292
  425.8 4.9 %finish_arrays.1 = (bf16[128,2048]{1,0:T(8,128)(2,1)}, f32[128,2048]{1,0:T(8,128)}, f32[256,512]{1,0:T(8,128)}, f32[256,512]{1,0:T(8,128)}, f32[256,512]{1,0:T(8...) custom-call(bf16[128,2048]{1,0:T(8,128)(2,1)} %get-tuple-element.30., ...), custom_call_target="tpu_custom_call" | custom-call | tf_op jit(solution)/shard_map/finish_arrays/pallas_call | solution.py:1335

commit v6 on v5

--- a/solution.py
+++ b/solution.py
@@ -576,8 +576,8 @@
 def layer_part(
     lengths, decay, x, cot, wq, wk, wv, wu, wo, w1, w2, w3,
     out, grad_x, fq, fk, fv, fu, fo, ff_, fs, ft,
-    n1_all, dm_all, n2_all, da_all, q_all, k_all, v_all, u_all, o_all, f_all, s_all, t_all, pre_all, in_f, in_t, in_o, in_h,
-    send, load, own, hop_n, side_n, hop_d, side_d, hop_m, side_m_, hop_a, side_a, z_head, z_out, z_ff, xy_head, xy_out, xy_ff,
+    n1_all, dm_all, n2_all, da_all, q_all, k_all, v_all, u_all, o_all, f_all, s_all, t_all, pre_all, in_f, in_t, in_o, in_h, x_f, y_f,
+    send, load, own, hop_n, side_n, hop_d, side_d, hop_m, side_m_, hop_a, side_a, z_head, z_out, z_ff, xy_head, xy_out, xy_ff, spread_f, join_f,
     n1, dm, n2, da, h, a_v, b_v, w_v, wa_v, wo_v, p_v, turned, part, side, inbox, side_sem, line_sem,
     side_m, inbox_m, side_sem_m, line_sem_m, table, squares, inbox_sq, scale, scale_in, sq_sem, sc_sem, column,
     mix, mix_in, mix_sem, inverse, mixed, pre, pre_sem, go_v, grads_h,
@@ -591,8 +591,8 @@
     tokens = 2 * length
     depth, wide = wq.shape
     head = q_all.shape[1] // 2
-    ff = f_all.shape[0] // 4
-    hidden = 4 * ff
+    hidden = f_all.shape[0]
+    quarter = hidden // 2
     half = length // 2
     target = g // 2
     mine = aligned(g % 2, head, head)
@@ -640,8 +640,17 @@
         for zs in order:
             block = dst.at[aligned(zs, 2 * depth, 16), mine]
             arrived(block, z_head.at[n, zs], here)
-            for r, o in enumerate(others):
+            for r, o in enumerate(others[:2]):
                 copies.remote(block, block, xy_head.at[n, r, zs], o, s, here)
+
+    def relay_heads(n):
+        dst = heads[n][1]
+        for zs in order:
+            for r, when in ((0, here), (1, jnp.logical_not(here))):
+                lanes = aligned(others[r] % 2, head, head)
+                arrived(dst.at[aligned(zs, 2 * depth, 16), lanes], xy_head.at[n, r, zs], when)
+                part_ = dst.at[aligned(2 * zs + r, depth, 16), lanes]
+                copies.remote(part_, part_, xy_head.at[n, 2, zs], others[1 - r], s, when)
 
     def send_out():
         for i in range(2):
@@ -656,50 +665,65 @@
         for j in range(2):
             arrived(o_all.at[pl.ds(j * head, head), aligned(g, wide, 128)], z_out.at[j])
         block = o_all.at[:, aligned(g, wide, 128)]
+        for r, o in enumerate(others[:2]):
+            copies.remote(block, block, xy_out.at[r], o, s)
+
+    def relay_out():
+        for r in range(2):
+            lanes = aligned(others[r], wide, 128)
+            arrived(o_all.at[:, lanes], xy_out.at[r])
+            part_ = o_all.at[pl.ds(r * head, head), lanes]
+            copies.remote(part_, part_, xy_out.at[2], others[1 - r], s)
+
+    def spread_ff():
+        for n, src in enumerate((w1_t, w2_t)):
+            for r, o in enumerate(others):
+                turned_out.remote(src.at[aligned(o, quarter, 16)], x_f.at[n, g], spread_f.at[n, r], o, s)
+            local(src.at[aligned(g, quarter, 16)], x_f.at[n, g], spread_f.at[n, 3])
+
+    def ff_block(n, group, zs):
+        return (f_all, s_all)[n].at[aligned(group % 2, quarter, 16), aligned(zs, 2 * depth, 128)]
+
+    def send_ff(n):
         for r, o in enumerate(others):
-            copies.remote(block, block, xy_out.at[r], o, s)
-
-    def send_ff(n):
-        src, dst = ((w1_t, f_all), (w2_t, s_all))[n]
-        for d in (4, 3, 5, 2, 6, 1, 7, 0):
-            to = (s + d) % 8
-            a = src.at[aligned(to, ff, 16)]
-            b = dst.at[aligned(g, ff, 16), aligned(s, depth, 128)]
+            arrived(x_f.at[n, o], spread_f.at[n, r])
+        arrived(x_f.at[n, g], spread_f.at[n, 3])
+        b = (f_all, s_all)[n].at[aligned(g % 2, quarter, 16), aligned(s, depth, 128)]
+        for d in (2, 1, 3, 0):
+            to = (z + d) % 4
+            a = x_f.at[n, to]
             if d:
-                turned_out.remote(a, b, z_ff.at[n, z], g, to)
+                copies.remote(a, b, z_ff.at[n, z], g, 2 * to + target)
             else:
-                local(a, b, z_ff.at[n, z])
-
-    def arrive_ff(n):
-        dst = (f_all, s_all)[n]
+                copies.remote(a, b, z_ff.at[n, z], g, 2 * to + target, c != target)
+                local(a, b, z_ff.at[n, z], here)
+
+    def pass_ff(n):
         for zs in order:
-            arrived(dst.at[aligned(g, ff, 16), aligned(zs, 2 * depth, 128)], z_ff.at[n, zs])
-
-    def pass_ff(n):
-        dst = (f_all, s_all)[n]
+            block = ff_block(n, g, zs)
+            arrived(block, z_ff.at[n, zs], here)
+            for r, o in enumerate(others[:2]):
+                copies.remote(block, block, xy_ff.at[n, r, zs], o, s, here)
+
+    def relay_ff(n):
         for zs in order:
-            block = dst.at[aligned(g, ff, 16), aligned(zs, 2 * depth, 128)]
-            for r, o in enumerate(others):
-                copies.remote(block, block, xy_ff.at[n, r, zs], o, s)
+            for r, when in ((0, here), (1, jnp.logical_not(here))):
+                arrived(ff_block(n, others[r], zs), xy_ff.at[n, r, zs], when)
+                part_ = (f_all, s_all)[n].at[aligned(others[r] % 2, quarter, 16), aligned(2 * zs + r, depth, 128)]
+                copies.remote(part_, part_, xy_ff.at[n, 2, zs], others[1 - r], s, when)
 
     def send_third():
-        for d in (2, 1, 3, 0):
-            to = 4 * c + (s + d) % 4
-            a = w3.at[aligned(to % 4, ff, 16)]
-            b = t_all.at[aligned(z, ff, 16), aligned(g, wide, 128)]
-            if d:
-                copies.remote(a, b, z_ff.at[2, z], g, to)
-            else:
-                self_ = s // 4 == c
-                copies.remote(a, b, z_ff.at[2, z], g, to, jnp.logical_not(self_))
-                local(a, b, z_ff.at[2, z], self_)
-
-    def pass_third():
-        for zs in order:
-            block = t_all.at[aligned(zs, ff, 16), aligned(g, wide, 128)]
-            arrived(block, z_ff.at[2, zs])
-            for r, o in enumerate(others):
-                copies.remote(block, block, xy_ff.at[2, r, zs], o, s)
+        block = t_all.at[:, aligned(g, wide, 128)]
+        for r, o in enumerate(others[:2]):
+            copies.remote(w3, block, xy_ff.at[2, r, 0], o, s)
+        local(w3, block, z_ff.at[2, 0])
+
+    def relay_third():
+        for r in range(2):
+            lanes = aligned(others[r], wide, 128)
+            arrived(t_all.at[:, lanes], xy_ff.at[2, r, 0])
+            part_ = t_all.at[pl.ds(r * quarter, quarter), lanes]
+            copies.remote(part_, part_, xy_ff.at[2, 2, 0], others[1 - r], s)
 
     send_heads(0)
     send_heads(1)
@@ -725,37 +749,37 @@
     for n, (src, dst) in enumerate(((w1_in, w1_t), (w2_in, w2_t))):
         arrived(src, load.at[n])
         dst[...] = src[...].T
+    spread_ff()
     pass_heads(0)
     send_heads(2)
     pass_heads(1)
     send_heads(3)
-    send_ff(0)
+    for b in range(2):
+        gather_n.begin(n1.at[b], own.at[0, b], b)
     pass_heads(2)
+    relay_heads(0)
     pass_heads(3)
     send_out()
-    send_ff(1)
-    for n in range(2):
-        arrive_ff(n)
-        if n == 0:
-            for b in range(2):
-                gather_n.begin(n1.at[b], own.at[0, b], b)
-            pass_out()
+    relay_heads(1)
     gather_n.step(0, 1)
     gather_n.step(1, 1)
-    pass_ff(0)
+    pass_out()
+    relay_heads(2)
     gather_n.step(0, 2)
     gather_n.step(1, 2)
-    pass_ff(1)
+    relay_heads(3)
+    relay_out()
     gather_n.step(0, 3)
     gather_n.step(1, 3)
+    send_ff(0)
+    send_ff(1)
     send_third()
-    for r, o in enumerate(others):
-        from_here = (o // 2) == c
-        for n, (_, dst) in enumerate(heads):
-            for zs in range(4):
-                block = dst.at[pl.ds(zs * 2 * depth, 2 * depth), aligned(o % 2, head, head)]
-                arrived(block, xy_head.at[n, r, zs], from_here)
-        arrived(o_all.at[:, aligned(o, wide, 128)], xy_out.at[r])
+    over = others[2]
+    for n, (_, dst) in enumerate(heads):
+        for zs in range(4):
+            block = dst.at[pl.ds(zs * 2 * depth, 2 * depth), aligned(over % 2, head, head)]
+            arrived(block, xy_head.at[n, 2, zs], over // 2 == c)
+    arrived(o_all.at[:, aligned(over, wide, 128)], xy_out.at[2])
     for n, (_, dst) in enumerate(heads):
         local(dst, wa_v.at[n], load.at[n])
     local(o_all, wo_v, load.at[4])
@@ -846,15 +870,18 @@
 
     gather_d.begin(dm.at[0], own.at[1, 0], 0)
     scatters[0].hop(0)
+    relay_third()
     scatters[0].start(2)
     scatters[0].hop(1)
+    pass_ff(0)
     scatters[1].start(0)
     scatters[0].hop(2)
+    pass_ff(1)
     gather_d.step(0, 1)
     hidden_state(0)
     scatters[1].start(1)
     scatters[1].hop(0)
-    pass_third()
+    relay_ff(0)
     gather_d.step(0, 2)
     scatters[1].start(2)
     scatters[1].hop(1)
@@ -865,6 +892,7 @@
     gather_d.begin(dm.at[1], own.at[1, 1], 1)
     hidden_state(1)
     gather_m.step(0, 3)
+    relay_ff(1)
     gather_d.finish(own.at[1, 0], 0)
     local(dm_all.at[0], b_v.at[at_b(0)], load.at[2])
     gather_m.finish(own.at[2, 0], 0)
@@ -873,13 +901,13 @@
     gather_m.step(1, 1)
     turned_out.finish()
     for n, (dst, room) in enumerate(((f_all, w1_f), (s_all, w2_f), (t_all, w3_f))):
-        for r, o in enumerate(others):
+        if n < 2:
             for zs in range(4):
-                if n < 2:
-                    block = dst.at[aligned(o, ff, 16), pl.ds(zs * 2 * depth, 2 * depth)]
-                else:
-                    block = dst.at[pl.ds(zs * ff, ff), aligned(o, wide, 128)]
-                arrived(block, xy_ff.at[n, r, zs])
+                arrived(ff_block(n, over, zs), xy_ff.at[n, 2, zs], over // 2 == c)
+        else:
+            arrived(dst.at[:, aligned(over, wide, 128)], xy_ff.at[2, 2, 0])
+        if n == 2:
+            arrived(dst.at[:, aligned(g, wide, 128)], z_ff.at[2, 0])
         local(dst, room, load.at[4 + n])
     for b in range(2):
         early[b].finish()
@@ -910,17 +938,37 @@
 
         tiles_of(width, body)
 
+    half_w = width // 2
+    sent_f = [[], []]
+
+    def spread_place(i):
+        return pl.ds(pl.multiple_of((i % 2) * half_w + (i // 2) * 256, 256), 256)
+
+    def to_groups(copies, block, inbox_ref, sem):
+        entries = []
+        for r, o in enumerate(others + (g,)):
+            holds = o // 2 == c
+            for e in range(2):
+                src = block(o).at[:, pl.ds(e * half_w, half_w)]
+                if r < 3:
+                    entries.append(copies.remote(src, inbox_ref.at[r], sem.at[r], o, 2 * z + e, holds))
+                else:
+                    entries.append(copies.remote(src, inbox_ref.at[r], sem.at[r], g, 2 * z + e, jnp.logical_and(holds, c != e)))
+                    local(src, inbox_ref.at[r], sem.at[r], jnp.logical_and(holds, c == e))
+        return entries
+
     def weight_part(n, operand):
         turn(turned, lambda t: p_v[n, t], tokens // 128, hidden)
 
         def body(at, i):
-            w_v[pl.ds(n * hidden, hidden), at] = product(turned[...], operand[:, at]).astype(jnp.bfloat16)
+            place = spread_place(i) if n < 2 else at
+            w_v[pl.ds(n * hidden, hidden), place] = product(turned[...], operand[:, at]).astype(jnp.bfloat16)
 
         tiles_of(width, body)
-        for r, o in enumerate(others):
-            if n < 2:
-                bulk.remote(w_v.at[aligned(4 * n + o, ff, 16)], in_f.at[n, r], xy_f.at[n, r], o, s)
-            else:
+        if n < 2:
+            sent_f[n] = to_groups(bulk, lambda o: w_v.at[aligned(2 * n + o % 2, quarter, 16)], in_f.at[n], xy_f.at[n])
+        else:
+            for r, o in enumerate(others):
                 bulk.remote(w_v.at[pl.ds(n * hidden, hidden), aligned(o, wide, 128)], in_t.at[r], xy_t.at[r], o, s)
 
     def hidden_gradient(b):
@@ -1087,32 +1135,45 @@
             return carry
 
         lax.fori_loop(0, rows // 16, result, 0)
-    def sum_ff(n, result):
-        for r in range(3):
+    def sum_ff(n):
+        def room(r):
+            return b_v.at[pl.ds((r // 2) * quarter, quarter), pl.ds((r % 2) * half_w, half_w)]
+
+        for r in range(4):
             arrived(in_f.at[n, r], xy_f.at[n, r])
-            local(in_f.at[n, r], b_v.at[pl.ds(r * ff, ff)], load.at[13 + r])
-        for r in range(3):
-            arrived(b_v.at[pl.ds(r * ff, ff)], load.at[13 + r])
-        mine = w_v.at[aligned(4 * n + g, ff, 16)]
+            local(in_f.at[n, r], room(r), load.at[13 + r])
+        for entry in sent_f[n]:
+            bulk.settle(entry)
+        for r in range(4):
+            arrived(room(r), load.at[13 + r])
+        total = w_v.at[pl.ds(n * hidden, quarter), pl.ds(0, half_w)]
 
         def read(at):
-            value = mine[at].astype(jnp.float32)
-            for r in range(3):
-                value = value + b_v.at[pl.ds(r * ff, ff)][at].astype(jnp.float32)
+            value = room(0)[at].astype(jnp.float32)
+            for r in range(1, 4):
+                value = value + room(r)[at].astype(jnp.float32)
             return value
 
         def write(at, value):
-            mine[at] = value.astype(jnp.bfloat16)
-
-        pour(read, write, ff // 16)
-        for d in (4, 3, 5, 2, 6, 1, 7, 0):
-            to = (s + d) % 8
-            src = mine.at[:, aligned(to, depth, 128)]
-            dst = result.at[aligned(s, ff, 16)]
+            total[at] = value.astype(jnp.bfloat16)
+
+        pour(read, write, quarter // 16)
+        for d in (2, 1, 3, 0):
+            chip = (z + d) % 4
+            src = total.at[:, aligned(chip, depth, 128)]
             if d:
-                last.remote(src, dst, z_f.at[n, d], g, to)
+                last.remote(src, y_f.at[n, z], z_f.at[n, z], g, 2 * chip + c)
             else:
-                local(src, dst, z_f.at[n, d])
+                local(src, y_f.at[n, z], z_f.at[n, z])
+
+    def join_ff(n, result):
+        for r, o in enumerate(others + (g,)):
+            arrived(y_f.at[n, o], z_f.at[n, o])
+            dst = result.at[aligned(g, quarter, 16)]
+            if r < 3:
+                last.remote(y_f.at[n, o], dst, join_f.at[n, r], o, s)
+            else:
+                local(y_f.at[n, o], dst, join_f.at[n, r])
 
     def sum_third():
         for r in range(3):
@@ -1132,16 +1193,7 @@
             mine[at] = value.astype(jnp.bfloat16)
 
         pour(read, write, hidden // 16)
-        for d in (2, 1, 3, 0):
-            chip = (z + d) % 4
-            to = 2 * chip + s // 4
-            src = mine.at[aligned(chip, ff, 16)]
-            dst = ft.at[aligned(s % 4, ff, 16)]
-            if d:
-                last.remote(src, dst, z_t.at[s % 4], g, to)
-            else:
-                last.remote(src, dst, z_t.at[s % 4], g, to, to != s)
-                local(src, dst, z_t.at[s % 4], to == s)
+        local(mine, ft, z_t)
 
     for b in range(2):
         sums[b].finish()
@@ -1149,11 +1201,11 @@
     first_part(0)
     fourth[0].begin()
     fourth[0].start(0)
-    sum_ff(0, ff_)
+    sum_ff(0)
     fourth[0].start(1)
     fourth[0].hop(0)
     attention_back(1)
-    sum_ff(1, fs)
+    sum_ff(1)
     first_part(1)
     fourth[1].begin()
 
@@ -1161,45 +1213,111 @@
         local(n1_all.at[b], b_v.at[at_b(b)], load.at[2 + b])
     for b in range(2):
         arrived(b_v.at[at_b(b)], load.at[2 + b])
-    half = width // 2
-    for n in range(4):
+    sent_h = []
+
+    def head_part(n):
         turn(turned, lambda t: dz(n, t)[...], tokens // 128, 2 * head)
+
+        def body(at, i):
+            grads_h[n, :, spread_place(i)] = product(turned[pl.ds(0, 2 * head)], b_v[:, at]).astype(jnp.bfloat16)
+
+        tiles_of(width, body)
+
+    def send_head(n):
+        if n >= 2:
+            for entry in sent_h[n - 2]:
+                last.settle(entry)
         grad = grads_h.at[n]
-
-        def body_h(at, i):
-            place = pl.ds(pl.multiple_of((i % 2) * half + (i // 2) * 256, 256), 256)
-            grad[:, place] = product(turned[pl.ds(0, 2 * head)], b_v[:, at]).astype(jnp.bfloat16)
-
-        tiles_of(width, body_h)
-        for r, o in enumerate(others + (g,)):
-            holds = o // 2 == c
-            for e in range(2):
-                src = grad.at[aligned(o % 2, head, head), pl.ds(e * half, half)]
-                dst = in_h.at[n, r]
-                if r < 3:
-                    last.remote(src, dst, xy_h.at[n, r], o, 2 * z + e, holds)
-                else:
-                    last.remote(src, dst, xy_h.at[n, r], g, 2 * z + e, jnp.logical_and(holds, c != e))
-                    local(src, dst, xy_h.at[n, r], jnp.logical_and(holds, c == e))
-        if n == 2:
-            fourth[0].start(2)
-            fourth[0].hop(1)
-    turn(turned, lambda t: nat_v(t)[...], tokens // 128, 2 * head)
-
-    def body_o(at, i):
-        go_v[:, at] = product(turned[pl.ds(0, 2 * head)], a_v[:, at]).astype(jnp.bfloat16)
-
-    tiles_of(width, body_o)
+        sent_h.append(to_groups(last, lambda o: grad.at[aligned(o % 2, head, head)], in_h.at[n], xy_h.at[n]))
+
+    def out_weight():
+        turn(turned, lambda t: nat_v(t)[...], tokens // 128, 2 * head)
+
+        def body(at, i):
+            go_v[:, at] = product(turned[pl.ds(0, 2 * head)], a_v[:, at]).astype(jnp.bfloat16)
+
+        tiles_of(width, body)
+
+    head_part(0)
+    send_head(0)
+    head_part(1)
+    send_head(1)
+    head_part(2)
+    fourth[0].start(2)
+    fourth[0].hop(1)
+    send_head(2)
+    head_part(3)
+    fourth[0].hop(2)
+    fourth[1].start(0)
+    send_head(3)
+    out_weight()
+    fourth[1].start(1)
+    fourth[1].hop(0)
+    for entry in sent_h[2]:
+        last.settle(entry)
     for r, o in enumerate(others):
         last.remote(go_v.at[:, aligned(o, wide, 128)], in_o.at[r], xy_o.at[r], o, s)
-    fourth[0].hop(2)
-    fourth[1].start(0)
-    fourth[1].start(1)
-    fourth[1].hop(0)
     sum_third()
     fourth[1].start(2)
     fourth[1].hop(1)
     fourth[1].hop(2)
+
+    def held(n, r):
+        return a_v.at[pl.ds((2 * n + r // 2) * head, head), pl.ds((r % 2) * half_w, half_w)]
+
+    def sum_head(n, result):
+        for r in range(4):
+            arrived(in_h.at[n, r], xy_h.at[n, r])
+            local(in_h.at[n, r], held(n, r), load.at[18 + 4 * n + r])
+        for r in range(4):
+            arrived(held(n, r), load.at[18 + 4 * n + r])
+
+        def read(at):
+            value = held(n, 0)[at].astype(jnp.float32)
+            for r in range(1, 4):
+                value = value + held(n, r)[at].astype(jnp.float32)
+            return value
+
+        def write(at, value):
+            held(n, 0)[at] = value.astype(jnp.bfloat16)
+
+        pour(read, write, head // 16)
+        for d in (2, 1, 3, 0):
+            chip = (z + d) % 4
+            src = held(n, 0).at[:, aligned(chip, depth, 128)]
+            dst = result.at[aligned(z, head, head)]
+            if d:
+                last.remote(src, dst, z_h.at[n, d], g, 2 * chip + c)
+            else:
+                local(src, dst, z_h.at[n, d])
+
+    def sum_out():
+        for r in range(3):
+            arrived(in_o.at[r], xy_o.at[r])
+            local(in_o.at[r], b_v.at[pl.ds(0, 2 * head), pl.ds(r * wide, wide)], load.at[13 + r])
+        for r in range(3):
+            arrived(b_v.at[pl.ds(0, 2 * head), pl.ds(r * wide, wide)], load.at[13 + r])
+        mine_o = go_v.at[:, aligned(g, wide, 128)]
+
+        def read(at):
+            value = mine_o[at].astype(jnp.float32)
+            for r in range(3):
+                value = value + b_v[at, pl.ds(r * wide, wide)].astype(jnp.float32)
+            return value
+
+        def write(at, value):
+            mine_o[at] = value.astype(jnp.bfloat16)
+
+        pour(read, write, 2 * head // 16)
+        for j in range(2):
+            to = 2 * (2 * c + j) + z // 2
+            src = mine_o.at[pl.ds(j * head, head)]
+            dst = fo.at[aligned(z % 2, head, head)]
+            last.remote(src, dst, z_o.at[z % 2], g, to, to != s)
+            local(src, dst, z_o.at[z % 2], to == s)
+
+    sum_head(0, fq)
+    sum_head(1, fk)
     for b in range(2):
         fourth[b].receive()
         scatter = fourth[b]
@@ -1217,65 +1335,16 @@
 
         lax.fori_loop(0, rows // 16, finish_x, 0)
 
-    for r in range(3):
-        arrived(in_o.at[r], xy_o.at[r])
-        local(in_o.at[r], b_v.at[pl.ds(0, 2 * head), pl.ds(r * wide, wide)], load.at[13 + r])
-
-    def held(n, r):
-        return a_v.at[pl.ds((2 * n + r // 2) * head, head), pl.ds((r % 2) * half, half)]
-
-    for n in range(4):
+    sum_head(2, fv)
+    join_ff(0, ff_)
+    join_ff(1, fs)
+    sum_head(3, fu)
+    sum_out()
+
+    for n, result in enumerate((ff_, fs)):
         for r in range(4):
-            arrived(in_h.at[n, r], xy_h.at[n, r])
-            local(in_h.at[n, r], held(n, r), load.at[18 + 4 * n + r])
-    for r in range(3):
-        arrived(b_v.at[pl.ds(0, 2 * head), pl.ds(r * wide, wide)], load.at[13 + r])
-    mine_o = go_v.at[:, aligned(g, wide, 128)]
-
-    def read_o(at):
-        value = mine_o[at].astype(jnp.float32)
-        for r in range(3):
-            value = value + b_v[at, pl.ds(r * wide, wide)].astype(jnp.float32)
-        return value
-
-    def write_o(at, value):
-        mine_o[at] = value.astype(jnp.bfloat16)
-
-    pour(read_o, write_o, 2 * head // 16)
-    for j in range(2):
-        to = 2 * (2 * c + j) + z // 2
-        src = mine_o.at[pl.ds(j * head, head)]
-        dst = fo.at[aligned(z % 2, head, head)]
-        last.remote(src, dst, z_o.at[z % 2], g, to, to != s)
-        local(src, dst, z_o.at[z % 2], to == s)
-    for n, result in enumerate((fq, fk, fv, fu)):
-        for r in range(4):
-            arrived(held(n, r), load.at[18 + 4 * n + r])
-
-        def read_h(at):
-            value = held(n, 0)[at].astype(jnp.float32)
-            for r in range(1, 4):
-                value = value + held(n, r)[at].astype(jnp.float32)
-            return value
-
-        def write_h(at, value):
-            held(n, 0)[at] = value.astype(jnp.bfloat16)
-
-        pour(read_h, write_h, head // 16)
-        for d in (2, 1, 3, 0):
-            chip = (z + d) % 4
-            src = held(n, 0).at[:, aligned(chip, depth, 128)]
-            dst = result.at[aligned(z, head, head)]
-            if d:
-                last.remote(src, dst, z_h.at[n, d], g, 2 * chip + c)
-            else:
-                local(src, dst, z_h.at[n, d])
-
-    for n, result in enumerate((ff_, fs)):
-        for d in range(8):
-            arrived(result.at[pl.ds(0, ff)], z_f.at[n, d])
-    for d in range(4):
-        arrived(ft.at[pl.ds(0, ff)], z_t.at[d])
+            arrived(result.at[pl.ds(0, quarter)], join_f.at[n, r])
+    arrived(ft, z_t)
     for j in range(2):
         arrived(fo.at[pl.ds(0, head)], z_o.at[j])
     for n, result in enumerate((fq, fk, fv, fu)):
@@ -1391,10 +1460,11 @@
         + [(low_array(2 * head, width), ANY)]
         + [(low_array(hidden, width), ANY)] * 3
         + [(wide_array(2, 2, 5, length, head), ANY)]
-        + [(low_array(2, 3, hidden // 4, width), ANY), (low_array(3, hidden, wide), ANY), (low_array(3, 2 * head, wide), ANY),
-           (low_array(4, 4, head, width // 2), ANY)],
-        [dma(360), dma(40), dma(4, 2)] + [dma(2, 2, 3), dma(2, 7)] * 4
-        + [dma(4, 4), dma(2), dma(3, 4), dma(4, 3, 4), dma(3), dma(3, 3, 4)]
+        + [(low_array(2, 4, hidden // 2, width // 2), ANY), (low_array(3, hidden, wide), ANY), (low_array(3, 2 * head, wide), ANY),
+           (low_array(4, 4, head, width // 2), ANY)]
+        + [(low_array(2, 4, hidden // 2, depth), ANY)] * 2,
+        [dma(480), dma(40), dma(4, 2)] + [dma(2, 2, 3), dma(2, 7)] * 4
+        + [dma(4, 4), dma(2), dma(3, 4), dma(4, 3, 4), dma(3), dma(3, 3, 4), dma(2, 4), dma(2, 4)]
         + [pltpu.VMEM((2, rows, width), bf16)] * 4
         + [pltpu.VMEM((2 * rows, width), f32),
            pltpu.VMEM((2 * length, width), bf16), pltpu.VMEM((2 * length, width), bf16), pltpu.VMEM((3 * hidden, width), bf16),
@@ -1408,7 +1478,7 @@
            pltpu.VMEM((2 * length, 128), f32), pltpu.VMEM((length, 128), f32),
            pltpu.VMEM((2, 5, length, head), f32), dma(2),
            pltpu.VMEM((2 * head, width), bf16), pltpu.VMEM((4, 2 * head, width), bf16),
-           dma(2, 3), dma(3), dma(3), dma(4, 4), dma(2, 8), dma(4), dma(2), dma(4, 4)],
+           dma(2, 4), dma(3), dma(3), dma(4, 4), dma(2, 4), dma(), dma(2), dma(4, 4)],
         "layer_part",
     )[:10]
     results = finished(out, grad_x, [fq, fk, fv, fu, ff, fs], [fo, ft])

time: 431 us -> 398 us (0.923)
  Pallas kernels: 430 us -> 397 us
    pallas_call x1, Pallas kernels: 425 us -> 392 us  [call(): pl.pallas_call(kernel, out_shape=[shape for shape, _ in outs], in_specs=[...]
where the time goes in v6:
time: 398 us
  Pallas kernels  397 us (100%)
    pallas_call x1, Pallas kernels, call(): pl.pallas_call(kernel, out_shape=[shape for shape, _ in outs], in_specs=[...  392 us

profile of v6, /device:TPU:0, one launch (start us, length us, event | category | flops | bytes accessed | tf_op | source)
XLA Modules:
  0.0 397.9 jit_solution(12764634097645319793)
XLA Ops:
  0.6 392.2 %layer_part.1 = (bf16[128,2048]{1,0:T(8,128)(2,1)}, f32[128,2048]{1,0:T(8,128)}, bf16[512,256]{1,0:T(8,128)(2,1)}, bf16[512,256]{1,0:T(8,128)(2,1)}, bf16[512,25...) custom-call(s32[1,2]{1,0:T(1,128)} %bitcast.11, ...), custom_call_target="tpu_custom_call" | custom-call | tf_op jit(solution)/shard_map/layer_part/pallas_call | solution.py:1361
  392.9 4.9 %finish_arrays.1 = (bf16[128,2048]{1,0:T(8,128)(2,1)}, f32[128,2048]{1,0:T(8,128)}, f32[256,512]{1,0:T(8,128)}, f32[256,512]{1,0:T(8,128)}, f32[256,512]{1,0:T(8...) custom-call(bf16[128,2048]{1,0:T(8,128)(2,1)} %get-tuple-element.30., ...), custom_call_target="tpu_custom_call" | custom-call | tf_op jit(solution)/shard_map/finish_arrays/pallas_call | solution.py:1404

commit v7 on v6

--- a/solution.py
+++ b/solution.py
@@ -412,6 +412,116 @@
     return [(g, (s + d) % 8) for d in range(1, 8)]
 
 
+def add_rows(target, room):
+    def write(at, value):
+        target[at] = value.astype(jnp.bfloat16)
+
+    pour(lambda at: target[at].astype(jnp.float32) + room[at].astype(jnp.float32), write, target.shape[0] // 16)
+
+
+class GroupSum:
+    def __init__(self, copies, grad, inbox, sem):
+        self.copies, self.grad, self.inbox, self.sem = copies, grad, inbox, sem
+        self.g, self.s, self.y, self.x, self.z, self.c = where_am_i()
+        self.rows, self.half = grad.shape[0] // 2, grad.shape[1] // 2
+        self.entries = []
+
+    def block(self, x, core):
+        return self.grad.at[aligned(x, self.rows, 16), pl.ds(core * self.half, self.half)]
+
+    def slot(self, first, count=1):
+        return self.inbox.at[pl.ds(first * self.rows, count * self.rows)]
+
+    def remote(self, *args):
+        self.entries.append(self.copies.remote(*args))
+
+    def depart(self):
+        gx, gy, _ = across(self.y, self.x)
+        self.remote(self.grad.at[:, pl.ds(0, self.half)], self.slot(0, 2), self.sem.at[0], gy, self.s, self.c != self.y)
+        self.remote(self.block(1 - self.x, 1), self.slot(2), self.sem.at[1], gx, self.s)
+
+    def middle(self, room, small, load):
+        gx, gy, _ = across(self.y, self.x)
+        mine = self.c == self.y
+        arrived(self.slot(0, 2), self.sem.at[0], mine)
+        local(self.slot(0, 2), room, load.at[0], mine)
+        arrived(self.slot(2), self.sem.at[1])
+        local(self.slot(2), small, load.at[1])
+        arrived(room, load.at[0], mine)
+
+        @pl.when(mine)
+        def _():
+            add_rows(self.grad.at[:, pl.ds(0, self.half)], room)
+
+        arrived(small, load.at[1])
+        add_rows(self.block(self.x, 1), small)
+        for core in range(2):
+            block = self.block(self.x, core)
+            self.remote(
+                block, self.slot(3), self.sem.at[2], self.g, 2 * self.z + core, jnp.logical_and(mine, self.c != core)
+            )
+            local(block, self.slot(3), self.sem.at[2], jnp.logical_and(mine, self.c == core))
+        self.remote(self.block(1 - self.x, 0), self.slot(4), self.sem.at[3], gx, 2 * self.z, mine)
+        self.remote(self.block(self.x, 1), self.slot(4), self.sem.at[3], gy, 2 * self.z + 1, jnp.logical_not(mine))
+
+    def final(self, room, small, load):
+        for i, ref in enumerate((room, small)):
+            arrived(self.slot(3 + i), self.sem.at[2 + i])
+            local(self.slot(3 + i), ref, load.at[i])
+        for i, ref in enumerate((room, small)):
+            arrived(ref, load.at[i])
+        add_rows(room, small)
+
+    def settle(self):
+        for entry in self.entries:
+            self.copies.settle(entry)
+
+
+class ColumnSum:
+    def __init__(self, copies, grad, inbox, sem):
+        self.copies, self.grad, self.inbox, self.sem = copies, grad, inbox, sem
+        self.g, self.s, y, x, _, _ = where_am_i()
+        self.others = across(y, x)
+        self.rows, self.wide = grad.shape[0] // 2, grad.shape[1] // 4
+
+    def block(self, group, i):
+        return self.grad.at[pl.ds(i * self.rows, self.rows), aligned(group, self.wide, 128)]
+
+    def depart(self):
+        for i in range(2):
+            to = self.others[i]
+            for k, group in enumerate((to, self.others[2])):
+                self.copies.remote(self.block(group, i), self.inbox.at[i, k], self.sem.at[i, k], to, self.s)
+
+    def middle(self, rooms, load):
+        for i in range(2):
+            arrived(self.inbox.at[i, 1], self.sem.at[i, 1])
+            local(self.inbox.at[i, 1], rooms[i], load.at[i])
+        for i in range(2):
+            arrived(rooms[i], load.at[i])
+            to = self.others[1 - i]
+            add_rows(self.block(to, i), rooms[i])
+            self.copies.remote(self.block(to, i), self.inbox.at[i, 2], self.sem.at[i, 2], to, self.s)
+
+    def final(self, rooms, load):
+        for i in range(2):
+            for k in range(2):
+                arrived(self.inbox.at[i, 2 * k], self.sem.at[i, 2 * k])
+                local(self.inbox.at[i, 2 * k], rooms[2 * i + k], load.at[2 * i + k])
+        for i in range(2):
+            for k in range(2):
+                arrived(rooms[2 * i + k], load.at[2 * i + k])
+            mine, first, second = self.block(self.g, i), rooms[2 * i], rooms[2 * i + 1]
+
+            def read(at):
+                return mine[at].astype(jnp.float32) + first[at].astype(jnp.float32) + second[at].astype(jnp.float32)
+
+            def write(at, value):
+                mine[at] = value.astype(jnp.bfloat16)
+
+            pour(read, write, self.rows // 16)
+
+
 def everyone_on_line(copies, src, dst, sem, g, s, to_rows):
     for d in range(1, 8):
         to = (s + d) % 8
@@ -599,11 +709,11 @@
     here = c == target
     order = [(z + d) % 4 for d in (0, 1, 3, 2)]
     spare = Spare(send)
-    copies, turned_out, bulk, last = [Copies(spare) for _ in range(4)]
+    copies, later, turned_out, bulk, last = [Copies(spare) for _ in range(5)]
     early, sums = [[Copies(spare) for _ in range(2)] for _ in range(2)]
     gather_n = Gather(copies, n1_all, rows, hop_n, side_n)
-    gather_d = Gather(copies, dm_all, rows, hop_d, side_d)
-    gather_m = Gather(copies, n2_all, rows, hop_m, side_m_)
+    gather_d = Gather(later, dm_all, rows, hop_d, side_d)
+    gather_m = Gather(later, n2_all, rows, hop_m, side_m_)
     gather_a = Gather(last, da_all, rows, hop_a, side_a)
     heads = list(zip((wq, wk, wv, wu), (q_all, k_all, v_all, u_all)))
     w1_f, w2_f, w3_f = [w_v.at[pl.ds(n * hidden, hidden)] for n in range(3)]
@@ -693,9 +803,9 @@
             to = (z + d) % 4
             a = x_f.at[n, to]
             if d:
-                copies.remote(a, b, z_ff.at[n, z], g, 2 * to + target)
+                later.remote(a, b, z_ff.at[n, z], g, 2 * to + target)
             else:
-                copies.remote(a, b, z_ff.at[n, z], g, 2 * to + target, c != target)
+                later.remote(a, b, z_ff.at[n, z], g, 2 * to + target, c != target)
                 local(a, b, z_ff.at[n, z], here)
 
     def pass_ff(n):
@@ -703,19 +813,19 @@
             block = ff_block(n, g, zs)
             arrived(block, z_ff.at[n, zs], here)
             for r, o in enumerate(others[:2]):
-                copies.remote(block, block, xy_ff.at[n, r, zs], o, s, here)
+                later.remote(block, block, xy_ff.at[n, r, zs], o, s, here)
 
     def relay_ff(n):
         for zs in order:
             for r, when in ((0, here), (1, jnp.logical_not(here))):
                 arrived(ff_block(n, others[r], zs), xy_ff.at[n, r, zs], when)
                 part_ = (f_all, s_all)[n].at[aligned(others[r] % 2, quarter, 16), aligned(2 * zs + r, depth, 128)]
-                copies.remote(part_, part_, xy_ff.at[n, 2, zs], others[1 - r], s, when)
+                later.remote(part_, part_, xy_ff.at[n, 2, zs], others[1 - r], s, when)
 
     def send_third():
         block = t_all.at[:, aligned(g, wide, 128)]
         for r, o in enumerate(others[:2]):
-            copies.remote(w3, block, xy_ff.at[2, r, 0], o, s)
+            later.remote(w3, block, xy_ff.at[2, r, 0], o, s)
         local(w3, block, z_ff.at[2, 0])
 
     def relay_third():
@@ -723,7 +833,7 @@
             lanes = aligned(others[r], wide, 128)
             arrived(t_all.at[:, lanes], xy_ff.at[2, r, 0])
             part_ = t_all.at[pl.ds(r * quarter, quarter), lanes]
-            copies.remote(part_, part_, xy_ff.at[2, 2, 0], others[1 - r], s)
+            later.remote(part_, part_, xy_ff.at[2, 2, 0], others[1 - r], s)
 
     send_heads(0)
     send_heads(1)
@@ -796,6 +906,7 @@
         kept = (side, inbox, side_sem, line_sem) if first else (side_m, inbox_m, side_sem_m, line_sem_m)
         return [LineScatter(copies[b], part.at[b], rows, *[k.at[b] for k in kept], queue) for b in range(2)]
 
+    copies.finish()
     scatters = scatters_of(early, True, {})
     for b in range(2):
         arrived(a_v.at[at_b(b)], load.at[5 + b])
@@ -831,7 +942,7 @@
         row = jnp.broadcast_to(square, (length, 128)).T[:8]
         for to in range(8):
             squares[b, to, :, :rows] = row[:, to * rows : (to + 1) * rows]
-        everyone_on_line(copies, squares, inbox_sq.at[b], sq_sem.at[b], g, s, lambda to: squares.at[b, to])
+        everyone_on_line(later, squares, inbox_sq.at[b], sq_sem.at[b], g, s, lambda to: squares.at[b, to])
         local(squares.at[b, s], inbox_sq.at[b, s], sq_sem.at[b, 7])
 
         def out_part(i, carry):
@@ -939,23 +1050,14 @@
         tiles_of(width, body)
 
     half_w = width // 2
-    sent_f = [[], []]
+    groups_f = [GroupSum(bulk, w_v.at[pl.ds(n * hidden, hidden)], in_f.at[n], xy_f.at[n]) for n in range(2)]
+    groups_t = ColumnSum(bulk, w_v.at[pl.ds(2 * hidden, hidden)], in_t, xy_t)
+
+    def rooms_ff(ref):
+        return ref.at[pl.ds(0, hidden), pl.ds(0, half_w)], ref.at[pl.ds(0, quarter), pl.ds(half_w, half_w)]
 
     def spread_place(i):
         return pl.ds(pl.multiple_of((i % 2) * half_w + (i // 2) * 256, 256), 256)
-
-    def to_groups(copies, block, inbox_ref, sem):
-        entries = []
-        for r, o in enumerate(others + (g,)):
-            holds = o // 2 == c
-            for e in range(2):
-                src = block(o).at[:, pl.ds(e * half_w, half_w)]
-                if r < 3:
-                    entries.append(copies.remote(src, inbox_ref.at[r], sem.at[r], o, 2 * z + e, holds))
-                else:
-                    entries.append(copies.remote(src, inbox_ref.at[r], sem.at[r], g, 2 * z + e, jnp.logical_and(holds, c != e)))
-                    local(src, inbox_ref.at[r], sem.at[r], jnp.logical_and(holds, c == e))
-        return entries
 
     def weight_part(n, operand):
         turn(turned, lambda t: p_v[n, t], tokens // 128, hidden)
@@ -966,10 +1068,9 @@
 
         tiles_of(width, body)
         if n < 2:
-            sent_f[n] = to_groups(bulk, lambda o: w_v.at[aligned(2 * n + o % 2, quarter, 16)], in_f.at[n], xy_f.at[n])
+            groups_f[n].depart()
         else:
-            for r, o in enumerate(others):
-                bulk.remote(w_v.at[pl.ds(n * hidden, hidden), aligned(o, wide, 128)], in_t.at[r], xy_t.at[r], o, s)
+            groups_t.depart()
 
     def hidden_gradient(b):
         scatter = second[b]
@@ -1018,7 +1119,7 @@
     local(n2_all.at[1], a_v.at[at_b(1)], load.at[1])
     for b in range(2):
         for d in range(1, 8):
-            copies.remote(scale.at[b], scale_in.at[b, s], sc_sem.at[b, d - 1], g, (s + d) % 8)
+            later.remote(scale.at[b], scale_in.at[b, s], sc_sem.at[b, d - 1], g, (s + d) % 8)
         local(scale.at[b], scale_in.at[b, s], sc_sem.at[b, 7])
     second[0].start(1)
     second[0].hop(0)
@@ -1098,6 +1199,7 @@
     hidden_gradient(1)
     third[0].start(2)
     third[0].hop(1)
+    groups_f[0].middle(*rooms_ff(a_v), load.at[pl.ds(13, 2)])
     gather_a.step(0, 3)
     third[0].hop(2)
     early[1].finish()
@@ -1122,42 +1224,17 @@
     third[1].start(2)
     third[1].hop(1)
     third[1].hop(2)
+    groups_f[1].middle(*rooms_ff(b_v), load.at[pl.ds(13, 2)])
+    for b in range(2):
+        local(n1_all.at[b], b_v.at[at_b(b)], load.at[2 + b])
+    later.finish()
     attention_back(0)
     gather_a.step(1, 3)
-    for b in range(2):
-        third[b].receive()
-        scatter = third[b]
-
-        def result(i, carry):
-            piece = aligned(i, 16, 16)
-            at = aligned(b * (rows // 16) + i, 16, 16)
-            out[at] = (h[at] + scatter.total(piece)).astype(jnp.bfloat16)
-            return carry
-
-        lax.fori_loop(0, rows // 16, result, 0)
     def sum_ff(n):
-        def room(r):
-            return b_v.at[pl.ds((r // 2) * quarter, quarter), pl.ds((r % 2) * half_w, half_w)]
-
-        for r in range(4):
-            arrived(in_f.at[n, r], xy_f.at[n, r])
-            local(in_f.at[n, r], room(r), load.at[13 + r])
-        for entry in sent_f[n]:
-            bulk.settle(entry)
-        for r in range(4):
-            arrived(room(r), load.at[13 + r])
+        small = w_v.at[pl.ds(n * hidden, quarter), pl.ds(half_w, half_w)]
+        groups_f[n].settle()
         total = w_v.at[pl.ds(n * hidden, quarter), pl.ds(0, half_w)]
-
-        def read(at):
-            value = room(0)[at].astype(jnp.float32)
-            for r in range(1, 4):
-                value = value + room(r)[at].astype(jnp.float32)
-            return value
-
-        def write(at, value):
-            total[at] = value.astype(jnp.bfloat16)
-
-        pour(read, write, quarter // 16)
+        groups_f[n].final(total, small, load.at[pl.ds(13, 2)])
         for d in (2, 1, 3, 0):
             chip = (z + d) % 4
             src = total.at[:, aligned(chip, depth, 128)]
@@ -1175,149 +1252,120 @@
             else:
                 local(y_f.at[n, o], dst, join_f.at[n, r])
 
+    def rooms_column(rows):
+        return [b_v.at[pl.ds(0, rows), pl.ds(i * wide, wide)] for i in range(4)]
+
     def sum_third():
-        for r in range(3):
-            arrived(in_t.at[r], xy_t.at[r])
-            local(in_t.at[r], b_v.at[pl.ds(0, hidden), pl.ds(r * wide, wide)], load.at[13 + r])
-        for r in range(3):
-            arrived(b_v.at[pl.ds(0, hidden), pl.ds(r * wide, wide)], load.at[13 + r])
-        mine = w_v.at[pl.ds(2 * hidden, hidden), aligned(g, wide, 128)]
-
-        def read(at):
-            value = mine[at].astype(jnp.float32)
-            for r in range(3):
-                value = value + b_v[at, pl.ds(r * wide, wide)].astype(jnp.float32)
-            return value
-
-        def write(at, value):
-            mine[at] = value.astype(jnp.bfloat16)
-
-        pour(read, write, hidden // 16)
-        local(mine, ft, z_t)
-
+        groups_t.final(rooms_column(quarter), load.at[pl.ds(13, 4)])
+        local(w_v.at[pl.ds(2 * hidden, hidden), aligned(g, wide, 128)], ft, z_t)
+
+    groups_h = [GroupSum(last, grads_h.at[n], in_h.at[n], xy_h.at[n]) for n in range(4)]
+    groups_o = ColumnSum(last, go_v, in_o, xy_o)
+
+    def room_h(first, count):
+        return w_v.at[pl.ds(first * head, count * head), pl.ds(half_w, half_w)]
+
+    def middle_head(n):
+        groups_h[n].middle(room_h(3 * (n % 2), 2), room_h(3 * (n % 2) + 2, 1), load.at[pl.ds(18, 2)])
+
+    def head_part(n):
+        turn(turned, lambda t: dz(n, t)[...], tokens // 128, 2 * head)
+
+        def body(at, i):
+            grads_h[n, :, spread_place(i)] = product(turned[pl.ds(0, 2 * head)], b_v[:, at]).astype(jnp.bfloat16)
+
+        tiles_of(width, body)
+
+    def out_weight():
+        turn(turned, lambda t: nat_v(t)[...], tokens // 128, 2 * head)
+
+        def body(at, i):
+            go_v[:, at] = product(turned[pl.ds(0, 2 * head)], a_v[:, at]).astype(jnp.bfloat16)
+
+        tiles_of(width, body)
+
+    def sum_head(n, result):
+        total = room_h(6 + n, 1)
+        groups_h[n].final(total, room_h(10, 1), load.at[pl.ds(18, 2)])
+        for d in (2, 1, 3, 0):
+            chip = (z + d) % 4
+            src = total.at[:, aligned(chip, depth, 128)]
+            dst = result.at[aligned(z, head, head)]
+            if d:
+                last.remote(src, dst, z_h.at[n, d], g, 2 * chip + c)
+            else:
+                local(src, dst, z_h.at[n, d])
+
+    def sum_out():
+        groups_o.final(rooms_column(head), load.at[pl.ds(13, 4)])
+        mine_o = go_v.at[:, aligned(g, wide, 128)]
+        for j in range(2):
+            to = 2 * (2 * c + j) + z // 2
+            src = mine_o.at[pl.ds(j * head, head)]
+            dst = fo.at[aligned(z % 2, head, head)]
+            last.remote(src, dst, z_o.at[z % 2], g, to, to != s)
+            local(src, dst, z_o.at[z % 2], to == s)
+
+    sum_ff(0)
+    attention_back(1)
+    for b in range(2):
+        arrived(b_v.at[at_b(b)], load.at[2 + b])
+    head_part(0)
+    groups_h[0].depart()
+    for b in range(2):
+        third[b].receive()
+        scatter = third[b]
+
+        def result(i, carry):
+            piece = aligned(i, 16, 16)
+            at = aligned(b * (rows // 16) + i, 16, 16)
+            out[at] = (h[at] + scatter.total(piece)).astype(jnp.bfloat16)
+            return carry
+
+        lax.fori_loop(0, rows // 16, result, 0)
     for b in range(2):
         sums[b].finish()
     fourth = scatters_of(early, True, {})
     first_part(0)
     fourth[0].begin()
     fourth[0].start(0)
-    sum_ff(0)
+    head_part(1)
+    groups_h[1].depart()
+    sum_ff(1)
+    groups_t.middle(
+        [w_v.at[pl.ds(0, quarter), pl.ds(half_w + k * wide, wide)] for k in range(2)], load.at[pl.ds(13, 2)]
+    )
+    first_part(1)
     fourth[0].start(1)
     fourth[0].hop(0)
-    attention_back(1)
-    sum_ff(1)
-    first_part(1)
     fourth[1].begin()
-
-    for b in range(2):
-        local(n1_all.at[b], b_v.at[at_b(b)], load.at[2 + b])
-    for b in range(2):
-        arrived(b_v.at[at_b(b)], load.at[2 + b])
-    sent_h = []
-
-    def head_part(n):
-        turn(turned, lambda t: dz(n, t)[...], tokens // 128, 2 * head)
-
-        def body(at, i):
-            grads_h[n, :, spread_place(i)] = product(turned[pl.ds(0, 2 * head)], b_v[:, at]).astype(jnp.bfloat16)
-
-        tiles_of(width, body)
-
-    def send_head(n):
-        if n >= 2:
-            for entry in sent_h[n - 2]:
-                last.settle(entry)
-        grad = grads_h.at[n]
-        sent_h.append(to_groups(last, lambda o: grad.at[aligned(o % 2, head, head)], in_h.at[n], xy_h.at[n]))
-
-    def out_weight():
-        turn(turned, lambda t: nat_v(t)[...], tokens // 128, 2 * head)
-
-        def body(at, i):
-            go_v[:, at] = product(turned[pl.ds(0, 2 * head)], a_v[:, at]).astype(jnp.bfloat16)
-
-        tiles_of(width, body)
-
-    head_part(0)
-    send_head(0)
-    head_part(1)
-    send_head(1)
     head_part(2)
     fourth[0].start(2)
     fourth[0].hop(1)
-    send_head(2)
+    middle_head(0)
+    groups_h[2].depart()
     head_part(3)
+    middle_head(1)
+    groups_h[3].depart()
     fourth[0].hop(2)
     fourth[1].start(0)
-    send_head(3)
     out_weight()
+    groups_o.depart()
+    middle_head(2)
     fourth[1].start(1)
     fourth[1].hop(0)
-    for entry in sent_h[2]:
-        last.settle(entry)
-    for r, o in enumerate(others):
-        last.remote(go_v.at[:, aligned(o, wide, 128)], in_o.at[r], xy_o.at[r], o, s)
-    sum_third()
+    middle_head(3)
+    sum_head(0, fq)
+    groups_o.middle(rooms_column(head), load.at[pl.ds(13, 2)])
+    join_ff(0, ff_)
+    join_ff(1, fs)
+    sum_head(1, fk)
     fourth[1].start(2)
     fourth[1].hop(1)
     fourth[1].hop(2)
-
-    def held(n, r):
-        return a_v.at[pl.ds((2 * n + r // 2) * head, head), pl.ds((r % 2) * half_w, half_w)]
-
-    def sum_head(n, result):
-        for r in range(4):
-            arrived(in_h.at[n, r], xy_h.at[n, r])
-            local(in_h.at[n, r], held(n, r), load.at[18 + 4 * n + r])
-        for r in range(4):
-            arrived(held(n, r), load.at[18 + 4 * n + r])
-
-        def read(at):
-            value = held(n, 0)[at].astype(jnp.float32)
-            for r in range(1, 4):
-                value = value + held(n, r)[at].astype(jnp.float32)
-            return value
-
-        def write(at, value):
-            held(n, 0)[at] = value.astype(jnp.bfloat16)
-
-        pour(read, write, head // 16)
-        for d in (2, 1, 3, 0):
-            chip = (z + d) % 4
-            src = held(n, 0).at[:, aligned(chip, depth, 128)]
-            dst = result.at[aligned(z, head, head)]
-            if d:
-                last.remote(src, dst, z_h.at[n, d], g, 2 * chip + c)
-            else:
-                local(src, dst, z_h.at[n, d])
-
-    def sum_out():
-        for r in range(3):
-            arrived(in_o.at[r], xy_o.at[r])
-            local(in_o.at[r], b_v.at[pl.ds(0, 2 * head), pl.ds(r * wide, wide)], load.at[13 + r])
-        for r in range(3):
-            arrived(b_v.at[pl.ds(0, 2 * head), pl.ds(r * wide, wide)], load.at[13 + r])
-        mine_o = go_v.at[:, aligned(g, wide, 128)]
-
-        def read(at):
-            value = mine_o[at].astype(jnp.float32)
-            for r in range(3):
-                value = value + b_v[at, pl.ds(r * wide, wide)].astype(jnp.float32)
-            return value
-
-        def write(at, value):
-            mine_o[at] = value.astype(jnp.bfloat16)
-
-        pour(read, write, 2 * head // 16)
-        for j in range(2):
-            to = 2 * (2 * c + j) + z // 2
-            src = mine_o.at[pl.ds(j * head, head)]
-            dst = fo.at[aligned(z % 2, head, head)]
-            last.remote(src, dst, z_o.at[z % 2], g, to, to != s)
-            local(src, dst, z_o.at[z % 2], to == s)
-
-    sum_head(0, fq)
-    sum_head(1, fk)
+    sum_third()
+    sum_head(2, fv)
+    sum_head(3, fu)
     for b in range(2):
         fourth[b].receive()
         scatter = fourth[b]
@@ -1335,10 +1383,6 @@
 
         lax.fori_loop(0, rows // 16, finish_x, 0)
 
-    sum_head(2, fv)
-    join_ff(0, ff_)
-    join_ff(1, fs)
-    sum_head(3, fu)
     sum_out()
 
     for n, result in enumerate((ff_, fs)):
@@ -1460,10 +1504,10 @@
         + [(low_array(2 * head, width), ANY)]
         + [(low_array(hidden, width), ANY)] * 3
         + [(wide_array(2, 2, 5, length, head), ANY)]
-        + [(low_array(2, 4, hidden // 2, width // 2), ANY), (low_array(3, hidden, wide), ANY), (low_array(3, 2 * head, wide), ANY),
-           (low_array(4, 4, head, width // 2), ANY)]
+        + [(low_array(2, 5 * hidden // 2, width // 2), ANY), (low_array(2, 3, hidden // 2, wide), ANY), (low_array(2, 3, head, wide), ANY),
+           (low_array(4, 5 * head, width // 2), ANY)]
         + [(low_array(2, 4, hidden // 2, depth), ANY)] * 2,
-        [dma(480), dma(40), dma(4, 2)] + [dma(2, 2, 3), dma(2, 7)] * 4
+        [dma(200), dma(26), dma(4, 2)] + [dma(2, 2, 3), dma(2, 7)] * 4
         + [dma(4, 4), dma(2), dma(3, 4), dma(4, 3, 4), dma(3), dma(3, 3, 4), dma(2, 4), dma(2, 4)]
         + [pltpu.VMEM((2, rows, width), bf16)] * 4
         + [pltpu.VMEM((2 * rows, width), f32),
@@ -1478,7 +1522,7 @@
            pltpu.VMEM((2 * length, 128), f32), pltpu.VMEM((length, 128), f32),
            pltpu.VMEM((2, 5, length, head), f32), dma(2),
            pltpu.VMEM((2 * head, width), bf16), pltpu.VMEM((4, 2 * head, width), bf16),
-           dma(2, 4), dma(3), dma(3), dma(4, 4), dma(2, 4), dma(), dma(2), dma(4, 4)],
+           dma(2, 4), dma(2, 3), dma(2, 3), dma(4, 4), dma(2, 4), dma(), dma(2), dma(4, 4)],
         "layer_part",
     )[:10]
     results = finished(out, grad_x, [fq, fk, fv, fu, ff, fs], [fo, ft])

time: 398 us -> 386 us (0.970); the launches traced: 398 us -> 379 us
  Pallas kernels: 397 us -> 378 us
    pallas_call x1, Pallas kernels: 392 us -> 373 us  [call(): pl.pallas_call(kernel, out_shape=[shape for shape, _ in outs], in_specs=[...]
where the time goes in v7:
time: 386 us; the launch traced here: 379 us
  Pallas kernels  378 us (98%)
    pallas_call x1, Pallas kernels, call(): pl.pallas_call(kernel, out_shape=[shape for shape, _ in outs], in_specs=[...  373 us

profile of v7, /device:TPU:0, one launch (start us, length us, event | category | flops | bytes accessed | tf_op | source)
XLA Modules:
  0.0 379.0 jit_solution(9594739052630956336)
XLA Ops:
  0.6 373.3 %layer_part.1 = (bf16[128,2048]{1,0:T(8,128)(2,1)}, f32[128,2048]{1,0:T(8,128)}, bf16[512,256]{1,0:T(8,128)(2,1)}, bf16[512,256]{1,0:T(8,128)(2,1)}, bf16[512,25...) custom-call(s32[1,2]{1,0:T(1,128)} %bitcast.11, ...), custom_call_target="tpu_custom_call" | custom-call | tf_op jit(solution)/shard_map/layer_part/pallas_call | solution.py:1405
  374.0 4.9 %finish_arrays.1 = (bf16[128,2048]{1,0:T(8,128)(2,1)}, f32[128,2048]{1,0:T(8,128)}, f32[256,512]{1,0:T(8,128)}, f32[256,512]{1,0:T(8,128)}, f32[256,512]{1,0:T(8...) custom-call(bf16[128,2048]{1,0:T(8,128)(2,1)} %get-tuple-element.30., ...), custom_call_target="tpu_custom_call" | custom-call | tf_op jit(solution)/shard_map/finish_arrays/pallas_call | solution.py:1448

commit v8 on v7

--- a/solution.py
+++ b/solution.py
@@ -281,7 +281,7 @@
 
 class Spare:
     def __init__(self, sems):
-        self.sems, self.free = sems, list(range(sems.shape[0]))
+        self.sems, self.free, self.order = sems, list(range(sems.shape[0])), []
 
 
 class Copies:
@@ -290,6 +290,9 @@
         self.pending = []
 
     def remote(self, src, dst, recv_sem, group, place, when=None):
+        while not self.spare.free:
+            owner, entry = self.spare.order.pop(0)
+            owner.settle(entry)
         number = self.spare.free.pop(0)
         copy = pltpu.make_async_remote_copy(
             src_ref=src,
@@ -300,6 +303,7 @@
             device_id_type=MESH,
         )
         self.pending.append((copy, when, number))
+        self.spare.order.append((self, self.pending[-1]))
         if when is None:
             copy.start()
         else:
@@ -525,7 +529,7 @@
 def everyone_on_line(copies, src, dst, sem, g, s, to_rows):
     for d in range(1, 8):
         to = (s + d) % 8
-        copies.remote(to_rows(to), dst.at[s], sem.at[d - 1], g, to)
+        copies.remote(to_rows(to), dst.at[s], sem, g, to)
 
 
 def mean_square(values):
@@ -687,7 +691,7 @@
     lengths, decay, x, cot, wq, wk, wv, wu, wo, w1, w2, w3,
     out, grad_x, fq, fk, fv, fu, fo, ff_, fs, ft,
     n1_all, dm_all, n2_all, da_all, q_all, k_all, v_all, u_all, o_all, f_all, s_all, t_all, pre_all, in_f, in_t, in_o, in_h, x_f, y_f,
-    send, load, own, hop_n, side_n, hop_d, side_d, hop_m, side_m_, hop_a, side_a, z_head, z_out, z_ff, xy_head, xy_out, xy_ff, spread_f, join_f,
+    send, load, own, hop_n, side_n, hop_d, side_d, z_head, z_out, z_ff, xy_head, xy_out, xy_ff, spread_f, join_f,
     n1, dm, n2, da, h, a_v, b_v, w_v, wa_v, wo_v, p_v, turned, part, side, inbox, side_sem, line_sem,
     side_m, inbox_m, side_sem_m, line_sem_m, table, squares, inbox_sq, scale, scale_in, sq_sem, sc_sem, column,
     mix, mix_in, mix_sem, inverse, mixed, pre, pre_sem, go_v, grads_h,
@@ -713,8 +717,8 @@
     early, sums = [[Copies(spare) for _ in range(2)] for _ in range(2)]
     gather_n = Gather(copies, n1_all, rows, hop_n, side_n)
     gather_d = Gather(later, dm_all, rows, hop_d, side_d)
-    gather_m = Gather(later, n2_all, rows, hop_m, side_m_)
-    gather_a = Gather(last, da_all, rows, hop_a, side_a)
+    gather_m = Gather(later, n2_all, rows, hop_n, side_n)
+    gather_a = Gather(last, da_all, rows, hop_d, side_d)
     heads = list(zip((wq, wk, wv, wu), (q_all, k_all, v_all, u_all)))
     w1_f, w2_f, w3_f = [w_v.at[pl.ds(n * hidden, hidden)] for n in range(3)]
     w1_in, w2_in = [w_v.at[pl.ds(n * depth, depth), pl.ds(512, 2 * hidden)] for n in range(2)]
@@ -880,7 +884,6 @@
     relay_heads(3)
     relay_out()
     gather_n.step(0, 3)
-    gather_n.step(1, 3)
     send_ff(0)
     send_ff(1)
     send_third()
@@ -893,9 +896,8 @@
     for n, (_, dst) in enumerate(heads):
         local(dst, wa_v.at[n], load.at[n])
     local(o_all, wo_v, load.at[4])
-    for b in range(2):
-        gather_n.finish(own.at[0, b], b)
-        local(n1_all.at[b], a_v.at[at_b(b)], load.at[5 + b])
+    gather_n.finish(own.at[0, 0], 0)
+    local(n1_all.at[0], a_v.at[at_b(0)], load.at[5])
     for j in range(2):
         table[j] = decay_table(decay[4 * (2 * c + j) + z], length)
     for n in range(4):
@@ -906,9 +908,12 @@
         kept = (side, inbox, side_sem, line_sem) if first else (side_m, inbox_m, side_sem_m, line_sem_m)
         return [LineScatter(copies[b], part.at[b], rows, *[k.at[b] for k in kept], queue) for b in range(2)]
 
-    copies.finish()
     scatters = scatters_of(early, True, {})
     for b in range(2):
+        if b == 1:
+            gather_n.step(1, 3)
+            gather_n.finish(own.at[0, 1], 1)
+            local(n1_all.at[1], a_v.at[at_b(1)], load.at[6])
         arrived(a_v.at[at_b(b)], load.at[5 + b])
         if b == 1:
             for j in range(2):
@@ -943,7 +948,7 @@
         for to in range(8):
             squares[b, to, :, :rows] = row[:, to * rows : (to + 1) * rows]
         everyone_on_line(later, squares, inbox_sq.at[b], sq_sem.at[b], g, s, lambda to: squares.at[b, to])
-        local(squares.at[b, s], inbox_sq.at[b, s], sq_sem.at[b, 7])
+        local(squares.at[b, s], inbox_sq.at[b, s], sq_sem.at[b])
 
         def out_part(i, carry):
             at = aligned(i, 256, 256)
@@ -956,8 +961,7 @@
             scatters[0].start(0)
 
     def hidden_state(b):
-        for d in range(8):
-            arrived(inbox_sq.at[b, 0], sq_sem.at[b, d])
+        arrived(inbox_sq.at[b], sq_sem.at[b])
         total = inbox_sq[b, 0]
         for d in range(1, 8):
             total = total + inbox_sq[b, d]
@@ -992,12 +996,12 @@
     hidden_state(0)
     scatters[1].start(1)
     scatters[1].hop(0)
-    relay_ff(0)
     gather_d.step(0, 2)
     scatters[1].start(2)
     scatters[1].hop(1)
     gather_m.step(0, 1)
     scatters[1].hop(2)
+    relay_ff(0)
     gather_d.step(0, 3)
     gather_m.step(0, 2)
     gather_d.begin(dm.at[1], own.at[1, 1], 1)
@@ -1098,8 +1102,8 @@
         gather_a.begin(da.at[b], own.at[3, b], b)
         mix[b, :, :rows] = column[b].T[:8, :rows]
         for d in range(1, 8):
-            last.remote(mix.at[b], mix_in.at[b, s], mix_sem.at[b, d - 1], g, (s + d) % 8)
-        local(mix.at[b], mix_in.at[b, s], mix_sem.at[b, 7])
+            last.remote(mix.at[b], mix_in.at[b, s], mix_sem.at[b], g, (s + d) % 8)
+        local(mix.at[b], mix_in.at[b, s], mix_sem.at[b])
 
     second = scatters_of(early, True, {})
     for n in (0, 4, 5, 2, 6):
@@ -1119,8 +1123,8 @@
     local(n2_all.at[1], a_v.at[at_b(1)], load.at[1])
     for b in range(2):
         for d in range(1, 8):
-            later.remote(scale.at[b], scale_in.at[b, s], sc_sem.at[b, d - 1], g, (s + d) % 8)
-        local(scale.at[b], scale_in.at[b, s], sc_sem.at[b, 7])
+            later.remote(scale.at[b], scale_in.at[b, s], sc_sem.at[b], g, (s + d) % 8)
+        local(scale.at[b], scale_in.at[b, s], sc_sem.at[b])
     second[0].start(1)
     second[0].hop(0)
     arrived(a_v.at[at_b(1)], load.at[1])
@@ -1136,8 +1140,7 @@
     def attention_back(b):
         gather_a.finish(own.at[3, b], b)
         local(da_all.at[b], a_v.at[at_b(b)], load.at[b])
-        for d in range(8):
-            arrived(mix_in.at[b, 0], mix_sem.at[b, d])
+        arrived(mix_in.at[b], mix_sem.at[b])
         columns_of(mixed, mix_in, b, rows)
         live = live_rows(0, length, lengths[0, b])
         arrived(a_v.at[at_b(b)], load.at[b])
@@ -1209,8 +1212,7 @@
     for j in range(2):
         table[j] = turned_table(decay[4 * (2 * c + j) + z], length)
     for b in range(2):
-        for d in range(8):
-            arrived(scale.at[b], sc_sem.at[b, d])
+        arrived(scale_in.at[b], sc_sem.at[b])
         columns_of(inverse.at[at_b(b)], scale_in, b, rows)
 
     for j in range(2):
@@ -1340,32 +1342,33 @@
     fourth[0].hop(0)
     fourth[1].begin()
     head_part(2)
+    groups_h[2].depart()
+    middle_head(0)
+    head_part(3)
+    groups_h[3].depart()
+    middle_head(1)
     fourth[0].start(2)
     fourth[0].hop(1)
-    middle_head(0)
-    groups_h[2].depart()
-    head_part(3)
-    middle_head(1)
-    groups_h[3].depart()
-    fourth[0].hop(2)
-    fourth[1].start(0)
     out_weight()
     groups_o.depart()
     middle_head(2)
+    fourth[0].hop(2)
+    fourth[1].start(0)
+    middle_head(3)
+    sum_head(0, fq)
     fourth[1].start(1)
     fourth[1].hop(0)
-    middle_head(3)
-    sum_head(0, fq)
     groups_o.middle(rooms_column(head), load.at[pl.ds(13, 2)])
+    sum_head(1, fk)
     join_ff(0, ff_)
     join_ff(1, fs)
-    sum_head(1, fk)
     fourth[1].start(2)
     fourth[1].hop(1)
+    sum_head(2, fv)
     fourth[1].hop(2)
+    sum_head(3, fu)
+    sum_out()
     sum_third()
-    sum_head(2, fv)
-    sum_head(3, fu)
     for b in range(2):
         fourth[b].receive()
         scatter = fourth[b]
@@ -1383,7 +1386,6 @@
 
         lax.fori_loop(0, rows // 16, finish_x, 0)
 
-    sum_out()
 
     for n, result in enumerate((ff_, fs)):
         for r in range(4):
@@ -1507,7 +1509,7 @@
         + [(low_array(2, 5 * hidden // 2, width // 2), ANY), (low_array(2, 3, hidden // 2, wide), ANY), (low_array(2, 3, head, wide), ANY),
            (low_array(4, 5 * head, width // 2), ANY)]
         + [(low_array(2, 4, hidden // 2, depth), ANY)] * 2,
-        [dma(200), dma(26), dma(4, 2)] + [dma(2, 2, 3), dma(2, 7)] * 4
+        [dma(176), dma(26), dma(4, 2)] + [dma(2, 2, 3), dma(2, 7)] * 2
         + [dma(4, 4), dma(2), dma(3, 4), dma(4, 3, 4), dma(3), dma(3, 3, 4), dma(2, 4), dma(2, 4)]
         + [pltpu.VMEM((2, rows, width), bf16)] * 4
         + [pltpu.VMEM((2 * rows, width), f32),
@@ -1517,8 +1519,8 @@
            pltpu.VMEM((2, length, width), bf16)]
         + scatter_scratch(rows, width) + scatter_scratch(rows, width)
         + [pltpu.VMEM((2, length, length), f32), pltpu.VMEM((2, 8, 8, 128), f32), pltpu.VMEM((2, 8, 8, 128), f32),
-           pltpu.VMEM((2, 8, 128), f32), pltpu.VMEM((2, 8, 8, 128), f32), dma(2, 8), dma(2, 8), pltpu.VMEM((2, 128, 128), f32),
-           pltpu.VMEM((2, 8, 128), f32), pltpu.VMEM((2, 8, 8, 128), f32), dma(2, 8),
+           pltpu.VMEM((2, 8, 128), f32), pltpu.VMEM((2, 8, 8, 128), f32), dma(2), dma(2), pltpu.VMEM((2, 128, 128), f32),
+           pltpu.VMEM((2, 8, 128), f32), pltpu.VMEM((2, 8, 8, 128), f32), dma(2),
            pltpu.VMEM((2 * length, 128), f32), pltpu.VMEM((length, 128), f32),
            pltpu.VMEM((2, 5, length, head), f32), dma(2),
            pltpu.VMEM((2 * head, width), bf16), pltpu.VMEM((4, 2 * head, width), bf16),

time: 386 us -> 373 us (0.966); the launches traced: 379 us -> 371 us
  Pallas kernels: 378 us -> 370 us
    pallas_call x1, Pallas kernels: 373 us -> 365 us  [call(): pl.pallas_call(kernel, out_shape=[shape for shape, _ in outs], in_specs=[...]
where the time goes in v8:
time: 373 us; the launch traced here: 371 us
  Pallas kernels  370 us (99%)
    pallas_call x1, Pallas kernels, call(): pl.pallas_call(kernel, out_shape=[shape for shape, _ in outs], in_specs=[...  365 us

profile of v8, /device:TPU:0, one launch (start us, length us, event | category | flops | bytes accessed | tf_op | source)
XLA Modules:
  0.0 370.8 jit_solution(17836597039119304325)
XLA Ops:
  0.6 365.1 %layer_part.1 = (bf16[128,2048]{1,0:T(8,128)(2,1)}, f32[128,2048]{1,0:T(8,128)}, bf16[512,256]{1,0:T(8,128)(2,1)}, bf16[512,256]{1,0:T(8,128)(2,1)}, bf16[512,25...) custom-call(s32[1,2]{1,0:T(1,128)} %bitcast.11, ...), custom_call_target="tpu_custom_call" | custom-call | tf_op jit(solution)/shard_map/layer_part/pallas_call | solution.py:1407
  365.7 4.9 %finish_arrays.1 = (bf16[128,2048]{1,0:T(8,128)(2,1)}, f32[128,2048]{1,0:T(8,128)}, f32[256,512]{1,0:T(8,128)}, f32[256,512]{1,0:T(8,128)}, f32[256,512]{1,0:T(8...) custom-call(bf16[128,2048]{1,0:T(8,128)(2,1)} %get-tuple-element.30., ...), custom_call_target="tpu_custom_call" | custom-call | tf_op jit(solution)/shard_map/finish_arrays/pallas_call | solution.py:1450

commit v9 on v8

--- a/solution.py
+++ b/solution.py
@@ -385,17 +385,24 @@
         self.copies.remote(src, self.block(b, z, c), self.side_sem.at[b, 0], g, s + 1 - 2 * c)
         local(src, self.block(b, z, c), own_sem)
 
-    def step(self, b, k):
+    def step(self, b, k, inner=None):
         g, s, z, c = self.g, self.s, self.z, self.c
         side = s + 1 - 2 * c
-        has = z >= k
+        ends = jnp.logical_or(z == 0, z == 3)
+
+        def these(has):
+            if inner is None:
+                return has
+            return jnp.logical_and(has, jnp.logical_not(ends) if inner else ends)
+
+        has = these(z >= k)
         at = jnp.maximum(z - k, 0)
         ref = self.block(b, at, c)
         arrived(ref, self.hop_sem.at[b, 0, k - 1], has)
         if k < 3:
             self.spread(ref, b, at, k, jnp.logical_and(has, z < 3), None)
         self.copies.remote(ref, ref, self.side_sem.at[b, k], g, side, has)
-        has = z + k <= 3
+        has = these(z + k <= 3)
         at = jnp.minimum(z + k, 3)
         ref = self.block(b, at, c)
         arrived(ref, self.hop_sem.at[b, 1, k - 1], has)
@@ -689,10 +696,10 @@
 
 def layer_part(
     lengths, decay, x, cot, wq, wk, wv, wu, wo, w1, w2, w3,
-    out, grad_x, fq, fk, fv, fu, fo, ff_, fs, ft,
+    out_all, grad_all, fq, fk, fv, fu, fo, ff_, fs, ft,
     n1_all, dm_all, n2_all, da_all, q_all, k_all, v_all, u_all, o_all, f_all, s_all, t_all, pre_all, in_f, in_t, in_o, in_h, x_f, y_f,
     send, load, own, hop_n, side_n, hop_d, side_d, z_head, z_out, z_ff, xy_head, xy_out, xy_ff, spread_f, join_f,
-    n1, dm, n2, da, h, a_v, b_v, w_v, wa_v, wo_v, p_v, turned, part, side, inbox, side_sem, line_sem,
+    out, grad_x, out_sem, n1, dm, n2, da, h, a_v, b_v, w_v, wa_v, wo_v, p_v, turned, part, side, inbox, side_sem, line_sem,
     side_m, inbox_m, side_sem_m, line_sem_m, table, squares, inbox_sq, scale, scale_in, sq_sem, sc_sem, column,
     mix, mix_in, mix_sem, inverse, mixed, pre, pre_sem, go_v, grads_h,
     xy_f, xy_t, xy_o, xy_h, z_f, z_t, z_o, z_h,
@@ -1012,8 +1019,8 @@
     local(dm_all.at[0], b_v.at[at_b(0)], load.at[2])
     gather_m.finish(own.at[2, 0], 0)
     local(n2_all.at[0], a_v.at[at_b(0)], load.at[0])
-    gather_d.step(1, 1)
-    gather_m.step(1, 1)
+    gather_d.step(1, 1, True)
+    gather_m.step(1, 1, True)
     turned_out.finish()
     for n, (dst, room) in enumerate(((f_all, w1_f), (s_all, w2_f), (t_all, w3_f))):
         if n < 2:
@@ -1110,11 +1117,14 @@
         ref = {0: a_v.at[at_b(0)], 2: b_v.at[at_b(0)], 4: w1_f, 5: w2_f, 6: w3_f}[n]
         arrived(ref, load.at[n])
     feed_forward(0)
-    gather_m.step(1, 2)
-    gather_d.step(1, 2)
+    gather_m.step(1, 2, True)
+    gather_d.step(1, 2, True)
     norm_part(0)
     second[0].begin()
     second[0].start(0)
+    for k in (1, 2):
+        gather_d.step(1, k, False)
+        gather_m.step(1, k, False)
     gather_m.step(1, 3)
     gather_d.step(1, 3)
     gather_d.finish(own.at[1, 1], 1)
@@ -1325,6 +1335,7 @@
             return carry
 
         lax.fori_loop(0, rows // 16, result, 0)
+    local(out, out_all, out_sem.at[2])
     for b in range(2):
         sums[b].finish()
     fourth = scatters_of(early, True, {})
@@ -1385,8 +1396,13 @@
             return carry
 
         lax.fori_loop(0, rows // 16, finish_x, 0)
-
-
+        block = pl.ds(b * rows, rows)
+        local(grad_x.at[block], grad_all.at[block], out_sem.at[b])
+
+
+    arrived(out, out_sem.at[2])
+    for b in range(2):
+        arrived(grad_x.at[pl.ds(b * rows, rows)], out_sem.at[b])
     for n, result in enumerate((ff_, fs)):
         for r in range(4):
             arrived(result.at[pl.ds(0, quarter)], join_f.at[n, r])
@@ -1498,7 +1514,7 @@
         0,
         [(lengths.T, in_smem), (decay_rate, in_smem), (x_low, VMEM), (cotangent[:, 0], VMEM)]
         + [(v, ANY) for v in (w_query, w_key, w_value, w_gate, w_out, w_first, w_second, w_third)],
-        [(low_array(2 * rows, width), VMEM), (wide_array(2 * rows, width), VMEM)]
+        [(low_array(2 * rows, width), ANY), (wide_array(2 * rows, width), ANY)]
         + [(low_array(wide, depth), ANY)] * 4 + [(low_array(depth, wide), ANY)]
         + [(low_array(2 * hidden, depth), ANY)] * 2 + [(low_array(hidden, wide), ANY)]
         + [(gathered, ANY)] * 4
@@ -1509,8 +1525,9 @@
         + [(low_array(2, 5 * hidden // 2, width // 2), ANY), (low_array(2, 3, hidden // 2, wide), ANY), (low_array(2, 3, head, wide), ANY),
            (low_array(4, 5 * head, width // 2), ANY)]
         + [(low_array(2, 4, hidden // 2, depth), ANY)] * 2,
-        [dma(176), dma(26), dma(4, 2)] + [dma(2, 2, 3), dma(2, 7)] * 2
+        [dma(128), dma(26), dma(4, 2)] + [dma(2, 2, 3), dma(2, 7)] * 2
         + [dma(4, 4), dma(2), dma(3, 4), dma(4, 3, 4), dma(3), dma(3, 3, 4), dma(2, 4), dma(2, 4)]
+        + [pltpu.VMEM((2 * rows, width), bf16), pltpu.VMEM((2 * rows, width), f32), dma(3)]
         + [pltpu.VMEM((2, rows, width), bf16)] * 4
         + [pltpu.VMEM((2 * rows, width), f32),
            pltpu.VMEM((2 * length, width), bf16), pltpu.VMEM((2 * length, width), bf16), pltpu.VMEM((3 * hidden, width), bf16),

time: 373 us -> 370 us (level); the launches traced: 371 us -> 364 us
  Pallas kernels: 370 us -> 363 us
    pallas_call x1, Pallas kernels: 365 us -> 358 us  [call(): pl.pallas_call(kernel, out_shape=[shape for shape, _ in outs], in_specs=[...]
where the time goes in v9:
time: 370 us; the launch traced here: 364 us
  Pallas kernels  363 us (98%)
    pallas_call x1, Pallas kernels, call(): pl.pallas_call(kernel, out_shape=[shape for shape, _ in outs], in_specs=[...  358 us

profile of v9, /device:TPU:0, one launch (start us, length us, event | category | flops | bytes accessed | tf_op | source)
XLA Modules:
  0.0 363.7 jit_solution(4553494781414672628)
XLA Ops:
  0.6 357.9 %layer_part.1 = (bf16[128,2048]{1,0:T(8,128)(2,1)}, f32[128,2048]{1,0:T(8,128)}, bf16[512,256]{1,0:T(8,128)(2,1)}, bf16[512,256]{1,0:T(8,128)(2,1)}, bf16[512,25...) custom-call(s32[1,2]{1,0:T(1,128)} %bitcast.11, ...), custom_call_target="tpu_custom_call" | custom-call | tf_op jit(solution)/shard_map/layer_part/pallas_call | solution.py:1423
  358.6 4.9 %finish_arrays.1 = (bf16[128,2048]{1,0:T(8,128)(2,1)}, f32[128,2048]{1,0:T(8,128)}, f32[256,512]{1,0:T(8,128)}, f32[256,512]{1,0:T(8,128)}, f32[256,512]{1,0:T(8...) custom-call(bf16[128,2048]{1,0:T(8,128)(2,1)} %get-tuple-element.30., ...), custom_call_target="tpu_custom_call" | custom-call | tf_op jit(solution)/shard_map/finish_arrays/pallas_call | solution.py:1466

commit v10 on v9

--- a/solution.py
+++ b/solution.py
@@ -799,16 +799,14 @@
     def spread_ff():
         for n, src in enumerate((w1_t, w2_t)):
             for r, o in enumerate(others):
-                turned_out.remote(src.at[aligned(o, quarter, 16)], x_f.at[n, g], spread_f.at[n, r], o, s)
-            local(src.at[aligned(g, quarter, 16)], x_f.at[n, g], spread_f.at[n, 3])
+                turned_out.remote(src.at[aligned(o, quarter, 16)], x_f.at[n, g], spread_f.at[n], o, s)
+            local(src.at[aligned(g, quarter, 16)], x_f.at[n, g], spread_f.at[n])
 
     def ff_block(n, group, zs):
         return (f_all, s_all)[n].at[aligned(group % 2, quarter, 16), aligned(zs, 2 * depth, 128)]
 
     def send_ff(n):
-        for r, o in enumerate(others):
-            arrived(x_f.at[n, o], spread_f.at[n, r])
-        arrived(x_f.at[n, g], spread_f.at[n, 3])
+        arrived(x_f.at[n], spread_f.at[n])
         b = (f_all, s_all)[n].at[aligned(g % 2, quarter, 16), aligned(s, depth, 128)]
         for d in (2, 1, 3, 0):
             to = (z + d) % 4
@@ -1260,9 +1258,9 @@
             arrived(y_f.at[n, o], z_f.at[n, o])
             dst = result.at[aligned(g, quarter, 16)]
             if r < 3:
-                last.remote(y_f.at[n, o], dst, join_f.at[n, r], o, s)
+                last.remote(y_f.at[n, o], dst, join_f.at[n], o, s)
             else:
-                local(y_f.at[n, o], dst, join_f.at[n, r])
+                local(y_f.at[n, o], dst, join_f.at[n])
 
     def rooms_column(rows):
         return [b_v.at[pl.ds(0, rows), pl.ds(i * wide, wide)] for i in range(4)]
@@ -1304,9 +1302,9 @@
             src = total.at[:, aligned(chip, depth, 128)]
             dst = result.at[aligned(z, head, head)]
             if d:
-                last.remote(src, dst, z_h.at[n, d], g, 2 * chip + c)
+                last.remote(src, dst, z_h.at[n], g, 2 * chip + c)
             else:
-                local(src, dst, z_h.at[n, d])
+                local(src, dst, z_h.at[n])
 
     def sum_out():
         groups_o.final(rooms_column(head), load.at[pl.ds(13, 4)])
@@ -1404,14 +1402,12 @@
     for b in range(2):
         arrived(grad_x.at[pl.ds(b * rows, rows)], out_sem.at[b])
     for n, result in enumerate((ff_, fs)):
-        for r in range(4):
-            arrived(result.at[pl.ds(0, quarter)], join_f.at[n, r])
+        arrived(result, join_f.at[n])
     arrived(ft, z_t)
     for j in range(2):
         arrived(fo.at[pl.ds(0, head)], z_o.at[j])
     for n, result in enumerate((fq, fk, fv, fu)):
-        for d in range(4):
-            arrived(result.at[pl.ds(0, head)], z_h.at[n, d])
+        arrived(result, z_h.at[n])
     for b in range(2):
         early[b].finish()
     bulk.finish()
@@ -1525,8 +1521,8 @@
         + [(low_array(2, 5 * hidden // 2, width // 2), ANY), (low_array(2, 3, hidden // 2, wide), ANY), (low_array(2, 3, head, wide), ANY),
            (low_array(4, 5 * head, width // 2), ANY)]
         + [(low_array(2, 4, hidden // 2, depth), ANY)] * 2,
-        [dma(128), dma(26), dma(4, 2)] + [dma(2, 2, 3), dma(2, 7)] * 2
-        + [dma(4, 4), dma(2), dma(3, 4), dma(4, 3, 4), dma(3), dma(3, 3, 4), dma(2, 4), dma(2, 4)]
+        [dma(100), dma(26), dma(4, 2)] + [dma(2, 2, 3), dma(2, 7)] * 2
+        + [dma(4, 4), dma(2), dma(3, 4), dma(4, 3, 4), dma(3), dma(3, 3, 4), dma(2), dma(2)]
         + [pltpu.VMEM((2 * rows, width), bf16), pltpu.VMEM((2 * rows, width), f32), dma(3)]
         + [pltpu.VMEM((2, rows, width), bf16)] * 4
         + [pltpu.VMEM((2 * rows, width), f32),
@@ -1541,11 +1537,11 @@
            pltpu.VMEM((2 * length, 128), f32), pltpu.VMEM((length, 128), f32),
            pltpu.VMEM((2, 5, length, head), f32), dma(2),
            pltpu.VMEM((2 * head, width), bf16), pltpu.VMEM((4, 2 * head, width), bf16),
-           dma(2, 4), dma(2, 3), dma(2, 3), dma(4, 4), dma(2, 4), dma(), dma(2), dma(4, 4)],
+           dma(2, 4), dma(2, 3), dma(2, 3), dma(4, 4), dma(2, 4), dma(), dma(2), dma(4)],
         "layer_part",
     )[:10]
-    results = finished(out, grad_x, [fq, fk, fv, fu, ff, fs], [fo, ft])
-    out, grad_x, fq, fk, fv, fu, ff, fs, fo, ft = results
+    results = finished(out, grad_x, [ff, fs, fq, fk, fv, fu], [ft, fo])
+    out, grad_x, ff, fs, fq, fk, fv, fu, ft, fo = results
     return (out.reshape(2, 1, rows, width), grad_x.reshape(2, 1, rows, width), fq, fk, fv, fu, fo, ff, fs, ft)
 
 

time: 370 us -> 369 us (level)
  no operation moved by 1% of the time
where the time goes in v10:
time: 369 us; the launch traced here: 366 us
  Pallas kernels  365 us (99%)
    pallas_call x1, Pallas kernels, call(): pl.pallas_call(kernel, out_shape=[shape for shape, _ in outs], in_specs=[...  360 us

profile of v10, /device:TPU:0, one launch (start us, length us, event | category | flops | bytes accessed | tf_op | source)
XLA Modules:
  0.0 366.1 jit_solution(7793645475694068650)
XLA Ops:
  0.6 360.4 %layer_part.1 = (bf16[128,2048]{1,0:T(8,128)(2,1)}, f32[128,2048]{1,0:T(8,128)}, bf16[512,256]{1,0:T(8,128)(2,1)}, bf16[512,256]{1,0:T(8,128)(2,1)}, bf16[512,25...) custom-call(s32[1,2]{1,0:T(1,128)} %bitcast.11, ...), custom_call_target="tpu_custom_call" | custom-call | tf_op jit(solution)/shard_map/layer_part/pallas_call | solution.py:1419
  361.1 4.8 %finish_arrays.1 = (bf16[128,2048]{1,0:T(8,128)(2,1)}, f32[128,2048]{1,0:T(8,128)}, f32[256,1408]{1,0:T(8,128)}, f32[256,1408]{1,0:T(8,128)}, f32[256,512]{1,0:T...) custom-call(bf16[128,2048]{1,0:T(8,128)(2,1)} %get-tuple-element.30., ...), custom_call_target="tpu_custom_call" | custom-call | tf_op jit(solution)/shard_map/finish_arrays/pallas_call | solution.py:1462
